TPU v7x, 256 devices: a whole 4x4x8 slice. The times are simulated.
256 devices in a mesh: ctx: 32 (over x, z), head: 2 (over core), dp: 4 (over y).
Axes of the slice: x: 4, y: 4, z: 8, core: 2. Of those that a mesh axis runs over, the one named last changes fastest.
Arguments:
- enc_query: bfloat16 [32768, 2048], P(('dp', 'ctx'), 'head'), parts along dimension 0, may hold values from -24 to 24
- enc_key: bfloat16 [32768, 2048], P(('dp', 'ctx'), 'head'), parts along dimension 0, may hold values from -24 to 24
- enc_value: bfloat16 [32768, 2048], P(('dp', 'ctx'), 'head'), parts along dimension 0, may hold values from -6 to 6
- input_segments: int32 [32768], P(('dp', 'ctx')), parts along dimension 0, may hold values from 0 to 7, as said below
- doc_bounds: int32 [128, 2], P(('dp', 'ctx')), parts along dimension 0, may hold values from 0 to 8192, as said below
- target_query: bfloat16 [4096, 2048], P(('dp', 'ctx'), 'head'), parts along dimension 0, may hold values from -24 to 24
- cross_key: bfloat16 [32768, 2048], P(('dp', 'ctx'), 'head'), parts along dimension 0, may hold values from -24 to 24
- cross_value: bfloat16 [32768, 2048], P(('dp', 'ctx'), 'head'), parts along dimension 0, may hold values from -6 to 6
- target_segments: int32 [4096], P('dp'), parts along dimension 0, may hold values from 0 to 7, as said below
Outputs:
- enc_out: bfloat16 [32768, 2048], P(('dp', 'ctx'), 'head'), parts along dimension 0
- cross_out: bfloat16 [4096, 2048], P(('dp', 'ctx'), 'head'), parts along dimension 0
There are 4 independent parts, one for each index of `dp`. A program takes and returns all parts, laid end to end along the dimension named above; each array names one. Nothing has to cross between parts.
Inputs may be any that keep to these rules, and one draw needn't show every extreme that they name: `input_segments`: ids never fall along the slots; each of the 8 documents holds at least one slot, and one holds exactly 6144 slots. `target_segments`: ids never fall along the slots; each of the 8 documents has at least one target slot. `doc_bounds`: row b holds the first slot of the document of input slot b * 256 and one past the last slot of the document of input slot (b + 1) * 256 - 1, as input_segments gives them.
All inputs are finite; a program needn't handle non-finite values.
Results may differ from a plain program's by a relative error of at most 0.005.
Values may be sent and summed in bfloat16 or wider, within the bound.
No kernel may reach another device: no remote copies, remote signals or barrier semaphores. Data moves between devices by JAX's collectives and lax.ppermute only.
A program may use at most 192 MiB of HBM per device.

v0:
```python
import jax
import jax.numpy as jnp
from jax import lax
from jax.sharding import PartitionSpec as P

HEAD_DIM = 256


neg_big = -1e30


def split_heads(block):
    return block.reshape(block.shape[0], block.shape[1] // HEAD_DIM, HEAD_DIM)


def fold_keys(carry, piece, query3, query_ids, lower, upper):
    keys, values, key_ids = piece
    maximum, total, accum = carry
    key_pos = jnp.arange(keys.shape[0], dtype=jnp.int32)
    scores = jnp.einsum(
        "qhe,khe->hqk", query3, split_heads(keys), preferred_element_type=jnp.float32
    ) * HEAD_DIM ** (-0.5)
    match = (
        (query_ids[:, None] == key_ids[None, :])
        & (key_pos[None, :] >= lower)
        & (key_pos[None, :] < upper)
    )
    match = match[None]
    scores = jnp.where(match, scores, neg_big)
    new_max = jnp.maximum(maximum, jnp.max(scores, axis=2))
    weights = jnp.where(match, jnp.exp(scores - new_max[:, :, None]), 0.0)
    total = jnp.sum(weights, axis=2)
    accum = jnp.einsum(
        "hqk,khe->hqe",
        weights.astype(jnp.bfloat16),
        split_heads(values),
        preferred_element_type=jnp.float32,
    )
    return (new_max, total, accum)


def per_device(
    enc_query,
    enc_key,
    enc_value,
    input_segments,
    doc_bounds,
    target_query,
    cross_key,
    cross_value,
    target_segments,
):
    rows = enc_query.shape[0]
    query3 = split_heads(enc_query)
    heads_here = query3.shape[1]
    query_ids = input_segments + 1
    lower = doc_bounds[0, 0]
    upper = doc_bounds[0, 1]
    me = lax.axis_index("ctx")
    init = (
        jnp.full((heads_here, rows), neg_big, jnp.float32),
        jnp.zeros((heads_here, rows), jnp.float32),
        jnp.zeros((heads_here, rows, HEAD_DIM), jnp.float32),
    )
    own = (enc_key, enc_value, query_ids)
    carry = fold_keys(
        init,
        (
            lax.all_gather(own[0], "ctx", axis=0, tiled=True),
            lax.all_gather(own[1], "ctx", axis=0, tiled=True),
            lax.all_gather(own[2], "ctx", axis=0, tiled=True),
        ),
        query3,
        query_ids,
        lower,
        upper,
    )
    maximum, total, accum = carry
    enc_out = (
        (accum / total[:, :, None])
        .transpose(1, 0, 2)
        .reshape(rows, heads_here * HEAD_DIM)
        .astype(jnp.bfloat16)
    )
    tgt_rows = target_query.shape[0]
    gathered = lax.all_gather(target_query, "ctx", axis=0, tiled=True)
    scores = jnp.einsum(
        "the,khe->htk",
        split_heads(gathered),
        split_heads(cross_key),
        preferred_element_type=jnp.float32,
    ) * HEAD_DIM ** (-0.5)
    match = (target_segments[:, None] == input_segments[None, :])[None]
    local_max = jnp.max(jnp.where(match, scores, neg_big), axis=2)
    global_max = lax.pmax(local_max, "ctx")
    weights = jnp.where(match, jnp.exp(scores - global_max[:, :, None]), 0.0)
    totals = lax.psum(jnp.sum(weights, axis=2), "ctx")
    rounded = weights.astype(jnp.bfloat16)
    values3 = split_heads(cross_value)
    summed = lax.psum_scatter(
        jnp.einsum("htk,khe->the", rounded, values3, preferred_element_type=jnp.float32).reshape(
            tgt_rows * lax.axis_size("ctx"), heads_here * HEAD_DIM
        ),
        "ctx",
        scatter_dimension=0,
        tiled=True,
    )
    mine = lax.dynamic_slice_in_dim(totals, me * tgt_rows, tgt_rows, 1)
    cross_out = (
        (summed.reshape(tgt_rows, heads_here, HEAD_DIM) / mine.T[:, :, None])
        .reshape(tgt_rows, heads_here * HEAD_DIM)
        .astype(jnp.bfloat16)
    )
    return (enc_out, cross_out)


def solution(mesh):
    placed = (
        P(("dp", "ctx"), "head"),
        P(("dp", "ctx"), "head"),
        P(("dp", "ctx"), "head"),
        P(("dp", "ctx")),
        P(("dp", "ctx"), None),
        P(("dp", "ctx"), "head"),
        P(("dp", "ctx"), "head"),
        P(("dp", "ctx"), "head"),
        P("dp"),
    )
    return jax.shard_map(
        per_device,
        mesh=mesh,
        in_specs=placed,
        out_specs=(P(("dp", "ctx"), "head"), P(("dp", "ctx"), "head")),
        check_vma=False,
    )
```

profile of v0, /device:TPU:1, one launch (start us, length us, event | category | flops | bytes accessed | tf_op | source)
XLA Modules:
  0.0 806.1 jit_solution(16458766086460496054)
XLA Ops:
  7.2 0.7 all-gather.9.cloned.1.call-update
  7.9 1.2 copy.44
  9.2 0.9 broadcast_compare_fusion
  10.1 78.3 %all-gather.9.cloned.1.call-done = bf16[1024,1024]{1,0:T(8,128)(2,1)} async-done(((bf16[32,1024]{1,0:T(8,128)(2,1)}), bf16[1024,1024]{1,0:T(8,128)(2,1)}) %all-gather.9.cloned.1.call-update) | async-done | bytes 2097168 | tf_op jit(solution)/shard_map/all_gather | solution.py:86
  88.4 3.9 copy.33
  92.4 4.7 select_reduce_fusion
  97.1 112.6 %pmax.7 = f32[4,1024]{1,0:T(4,128)S(1)} all-reduce(f32[4,1024]{1,0:T(4,128)S(1)} %get-tuple-element.12), channel_id=1, replica_groups=mesh['ctx'=32,'head'=2,'dp'=4] {'ctx'}, use_global_device_ids=true, to_apply=%region_3.4 | all-reduce | flops 4096 | bytes 32768 | tf_op jit(solution)/shard_map/pmax | solution.py:95
  209.7 5.2 fusion.8
  214.8 5.4 copy.38
  220.3 1.0 copy.29
  221.9 29.7 %all-gather = s32[32,1,256]{2,1,0:T(1,128)S(1)} all-gather(s32[1,1,256]{2,1,0:T(1,128)S(1)} %bitcast.47), channel_id=1, replica_groups=mesh['ctx'=32,'head'=2,'dp'=4] {'ctx'}, dimensions={0}, use_global_device_ids=true | all-gather | bytes 33792 | tf_op jit(solution)/shard_map/all_gather | solution.py:71
  252.3 1.3 iota_compare_fusion
  253.7 1.7 and_and_fusion
  255.4 3.1 fusion.6
  258.5 113.2 %psum.7 = f32[4,1024]{1,0:T(4,128)S(1)} all-reduce(f32[4,1024]{1,0:T(4,128)S(1)} %fusion.6), channel_id=1, replica_groups=mesh['ctx'=32,'head'=2,'dp'=4] {'ctx'}, use_global_device_ids=true, to_apply=%region_6.7 | all-reduce | flops 4096 | bytes 32768 | tf_op jit(solution)/shard_map/psum | solution.py:97
  372.0 89.8 %reduce-scatter.2.cloned.1.call-done = f32[32,1024]{1,0:T(8,128)} async-done(((f32[1024,1024]{1,0:T(8,128)}), f32[32,1024]{1,0:T(8,128)}) %reduce-scatter.2.cloned.1.call-update) | async-done | bytes 131088 | tf_op jit(solution)/shard_map/reduce_scatter | solution.py:100
  461.8 1.6 divide_convert_fusion
  463.4 153.3 %all-gather.5.cloned.1.call-done = bf16[8192,1024]{0,1:T(8,128)(2,1)} async-done(((bf16[256,1024]{0,1:T(8,128)(2,1)}), bf16[8192,1024]{0,1:T(8,128)(2,1)}) %all-gather.5.cloned.1.call-update) | async-done | bytes 16777232 | tf_op jit(solution)/shard_map/all_gather | solution.py:69
  616.8 21.9 %fusion = (f32[4,256]{1,0:T(4,128)S(1)}, f32[4,256,8192]{2,1,0:T(8,128)}) fusion(pred[256,8192]{1,0:T(8,128)(4,1)S(1)} %and_and_fusion, bf16[8192,4,256]{0,2,1:T(8,128)(2,1)} %bitcast.49, bf16[32,4,8,256]{3,2,1,0:T(8,128)(2,1)S(1)} %bitcast.51), kind=kOutput, calls=%fused_computation.2 | convolution fusion | flops 4320132096 | bytes 52957184 | tf_op jit(solution)/shard_map/qhe,khe->hqk/dot_general | solution.py:20
  638.7 15.8 %fusion.1 = f32[4,256]{1,0:T(4,128)S(1)} fusion(f32[4,256,8192]{2,1,0:T(8,128)} %get-tuple-element.11, f32[4,256]{1,0:T(4,128)S(1)} %broadcast_maximum_fusion, pred[256,8192]{1,0:T(8,128)(4,1)S(1)} %and_and_fusion), kind=kLoop, calls=%fused_computation.3 | loop fusion | flops 41942016 | bytes 35659776 | tf_op jit(solution)/shard_map/reduce_sum | solution.py:32
  654.5 104.5 %all-gather.7.cloned.1.call-done = bf16[8192,1024]{1,0:T(8,128)(2,1)} async-done(((bf16[256,1024]{1,0:T(8,128)(2,1)}), bf16[8192,1024]{1,0:T(8,128)(2,1)}) %all-gather.7.cloned.1.call-update) | async-done | bytes 16777232 | tf_op jit(solution)/shard_map/all_gather | solution.py:70
  759.0 20.8 %copy.32 = bf16[8192,1024]{0,1:T(8,128)(2,1)} copy(bf16[8192,1024]{1,0:T(8,128)(2,1)} %all-gather.7.cloned.1.call-done) | data formatting | bytes 33554432 | tf_op jit(solution)/shard_map/all_gather | solution.py:70
  779.8 18.8 %fusion.20 = bf16[256,4,256]{0,2,1:T(8,128)(2,1)S(1)} fusion(bf16[8192,4,256]{0,2,1:T(8,128)(2,1)} %bitcast.39, f32[4,256,8192]{2,1,0:T(8,128)} %get-tuple-element.11, f32[4,256]{1,0:T(4,128)S(1)} %broadcast_maximum_fusion, pred[256,8192]{1,0:T(8,128)(4,1)S(1)} %and_and_fusion, f32[256,4]{0,1:T(4,128)S(1)} %bitcast.48), kind=kOutput, calls=%fused_computation.19 | convolution fusion | flops 4337434624 | bytes 52961280 | tf_op jit(solution)/shard_map/hqk,khe->hqe/dot_general | solution.py:33
  798.6 1.0 copy.40
  (22 shorter events, 1.7 us)
Async XLA Ops:
  7.2 81.3 %all-gather.9.cloned.1.call-start = ((), (), s32[]{:S(2)}) async-start(), calls=%async_computation.3 | async-start | bytes 2162688 | tf_op jit(solution)/shard_map/all_gather | solution.py:86
  7.9 453.9 %reduce-scatter.2.cloned.1.call-start = ((), (), s32[]{:S(2)}) async-start(), calls=%async_computation.4 | async-start | bytes 4325376 | tf_op jit(solution)/shard_map/reduce_scatter | solution.py:100
  214.8 5.5 copy-start
  214.8 7.1 copy-start.1
  214.8 36.9 %copy-start.2 = (s32[1,2]{1,0:T(1,128)S(1)}, s32[1,2]{1,0:T(1,128)}, u32[]{:S(2)}) copy-start(s32[1,2]{1,0:T(1,128)} %param.13) | copy-start | bytes 28
  220.2 396.5 %copy-start.3 = (bf16[256,1024]{1,0:T(8,128)(2,1)S(1)}, bf16[256,1024]{1,0:T(8,128)(2,1)}, u32[]{:S(2)}) copy-start(bf16[256,1024]{1,0:T(8,128)(2,1)} %param.9) | copy-start | bytes 1572868
  220.2 396.5 %all-gather.5.cloned.1.call-start = ((), (), s32[]{:S(2)}) async-start(), calls=%async_computation.1 | async-start | bytes 17301504 | tf_op jit(solution)/shard_map/all_gather | solution.py:69
  221.3 537.7 %all-gather.7.cloned.1.call-start = ((), (), s32[]{:S(2)}) async-start(), calls=%async_computation.2 | async-start | bytes 17301504 | tf_op jit(solution)/shard_map/all_gather | solution.py:70
Sparse Core Ops, SparseCore 0:
  10.6 77.7 all-gather.8
  220.4 241.4 reduce-scatter.1
  465.2 151.5 all-gather.4
  619.5 139.4 all-gather.6
where the time goes:
time: 807 us; the launch traced here: 806 us
  waiting for transfers between devices  427 us (53%)
  blocking collectives  256 us (32%)
  matrix products  50.6 us (6%)
  local copies, waits for them, and re-layouts  34.3 us (4%)
  other arithmetic  24.4 us (3%)
  between operations  13.9 us (2%)
    all_gather x1, waiting for transfers between devices, per_device(): lax.all_gather(own[0], 'ctx', axis=0, tiled=True)  153 us
    psum x1, blocking collectives, per_device(): totals = lax.psum(jnp.sum(weights, axis=2), 'ctx')  113 us
    pmax x1, blocking collectives, per_device(): global_max = lax.pmax(local_max, 'ctx')  113 us
    all_gather x1, waiting for transfers between devices, per_device(): lax.all_gather(own[1], 'ctx', axis=0, tiled=True)  105 us
    reduce_scatter x1, waiting for transfers between devices, per_device(): lax.psum_scatter(jnp.einsum('htk,khe->the', rounded, values3, preferred_e...  89.8 us
    all_gather x1, waiting for transfers between devices, per_device(): gathered = lax.all_gather(target_query, 'ctx', axis=0, tiled=True)  78.3 us
    all_gather x1, blocking collectives, per_device(): lax.all_gather(own[2], 'ctx', axis=0, tiled=True)  29.7 us
    dot_general x1, matrix products, fold_keys(): jnp.einsum('qhe,khe->hqk', query3, split_heads(keys), preferred_element_t...  21.9 us
  transfers between devices with their start and end apart: 4, of which 4 were waited for; matrix products, arithmetic and copies ran while one was open for 6% of the time, Pallas kernels for 0%

commit v1 on v0

v1 whole, which is shorter than its diff:
```python
import functools

import jax
import jax.numpy as jnp
from jax import lax
from jax.experimental import pallas as pl
from jax.experimental.pallas import tpu as pltpu
from jax.sharding import Mesh
from jax.sharding import PartitionSpec as P

HEAD_DIM = 256
HALF = 128
TGT = 32
NEG = -1.0e30
LOW = -1.0e29

ROW_V = HALF
ROW_ID = 2 * HALF
ROW_Q = ROW_ID + 16
ROWS = ROW_Q + HALF
KEYS = ROW_Q
ASK = ROWS - ROW_ID
X_V = 2 * HALF
X_ID = 4 * HALF
X_T = X_ID + 16
X_ROWS = X_T + TGT
ORDER = (0, 3, 5, 1, 7, 2, 6, 4)
X_ORDER = (0, 1, 3, 2)
WIDE = HEAD_DIM + 128
MIB = 1024 * 1024
HALF_TYPE = jnp.bfloat16


def z_send(array, shift):
    return lax.ppermute(array, "z", [(i, (i + shift) % 8) for i in range(8)])


def x_send(array, shift):
    return lax.ppermute(array, "x", [(i, (i + shift) % 4) for i in range(4)])


def core_swap(array):
    return lax.ppermute(array, "core", [(0, 1), (1, 0)])


def params(flops, moved, limit=8):
    return dict(
        compiler_params=pltpu.CompilerParams(vmem_limit_bytes=limit * MIB),
        cost_estimate=pl.CostEstimate(flops=flops, bytes_accessed=moved, transcendentals=0),
    )


def rows_at(start, size, unit):
    return pl.ds(pl.multiple_of(start * unit, unit), size)


def half_rows(c):
    return rows_at(c, HALF, HALF)


def columns(j):
    return pl.ds(j * HEAD_DIM, HEAD_DIM)


def whole():
    return pl.BlockSpec(memory_space=pltpu.VMEM)


def scalars():
    return pl.BlockSpec(memory_space=pltpu.SMEM)


def shaped(*shape):
    return jax.ShapeDtypeStruct(shape, HALF_TYPE)


def copy(a, b):
    b[...] = a[...]


def copies(place, plan, ins, outs, after=()):
    def kernel(place_ref, *refs):
        at = (place_ref[0], place_ref[1], place_ref[2])
        for a, b, *when in plan(at, refs[: len(ins)], refs[len(ins) + len(after) :]):
            if when:
                pl.when(when[0])(functools.partial(copy, a, b))
            else:
                copy(a, b)

    return pl.pallas_call(
        kernel,
        out_shape=[shaped(*shape) for shape in outs],
        in_specs=[scalars()] + [whole()] * len(ins) + [pl.BlockSpec(memory_space=pl.ANY)] * len(after),
        out_specs=[whole()] * len(outs),
        **params(0, 2 * MIB),
    )(place, *ins, *after)


def named(number_ref, half):
    row = number_ref[pl.ds(half, 1), :].astype(jnp.float32)
    return jnp.broadcast_to(row, (16, HALF)).astype(HALF_TYPE)


def load(place, keys, values, query, target, cross_keys, cross_values, numbers):
    def kernel(place_ref, k_ref, v_ref, q_ref, t_ref, xk_ref, xv_ref, id_ref, near, away, heads, sems):
        c = place_ref[1]
        made = []
        for side, out in ((1 - c, away), (c, near)):
            for i, ref in enumerate((k_ref, v_ref, q_ref)):
                made.append((ref.at[half_rows(side)], out.at[pl.ds(i * HALF, HALF)]))
        for j in range(4):
            for ref, row, size in ((xk_ref, 0, 2 * HALF), (xv_ref, X_V, 2 * HALF), (t_ref, X_T, TGT)):
                made.append((ref.at[:, columns(j)], heads.at[j, pl.ds(row, size)]))
        made = [pltpu.make_async_copy(a, b, sems.at[i]) for i, (a, b) in enumerate(made)]
        for one in made:
            one.start()
        for j in range(4):
            for half in (0, 1):
                heads[j, X_ID:X_T, half * HALF : half * HALF + HALF] = named(id_ref, half)
        for one in made:
            one.wait()

    return pl.pallas_call(
        kernel,
        out_shape=[shaped(3 * HALF, 4 * HEAD_DIM)] * 2 + [shaped(4, X_ROWS, HEAD_DIM)],
        in_specs=[scalars()] + [pl.BlockSpec(memory_space=pl.ANY)] * 6 + [whole()],
        out_specs=[whole()] * 3,
        scratch_shapes=[pltpu.SemaphoreType.DMA((18,))],
        **params(0, 6 * MIB, 56),
    )(place, keys, values, query, target, cross_keys, cross_values, numbers)


class Either:
    def __init__(self, first, a, b):
        self.first, self.a, self.b = first, a, b

    def __getitem__(self, key):
        return jnp.where(self.first, self.a[key], self.b[key])


class Row:
    def __init__(self, ref, half):
        self.ref, self.half = ref, half

    def __getitem__(self, key):
        row = named(self.ref, self.half)
        return jnp.concatenate([row, row], axis=1)


def plan_pack(shifts, at, ins, outs):
    z, c, _ = at
    near, swapped, ids = ins
    pairs = []
    for k, d in enumerate(shifts):
        head = lax.rem(z + d, 8)
        column = rows_at(lax.rem(head, 4), HEAD_DIM, HEAD_DIM)
        first = (head // 4) == c
        for i, row in enumerate((0, ROW_V, ROW_Q)):
            part = (pl.ds(i * HALF, HALF), column)
            pairs.append((Either(first, near.at[part], swapped.at[part]), outs[k].at[pl.ds(row, HALF)]))
        pairs.append((Row(ids, c), outs[k].at[pl.ds(ROW_ID, 16)]))
    return pairs


def plan_first(at, ins, outs):
    group, ask = outs
    pairs = []
    for i, ref in enumerate(ins):
        pairs.append((ref.at[pl.ds(0, KEYS)], group.at[i]))
        pairs.append((ref.at[pl.ds(ROW_ID, ASK)], ask.at[i]))
    return pairs


def plan_second(at, ins, outs):
    chunks, (left, right, ask_first) = ins[:3], ins[3:]
    to_right, to_left, ask = outs
    pairs = [
        (left.at[pl.ds(0, 3)], to_right.at[pl.ds(0, 3)]),
        (right.at[pl.ds(3, 2)], to_left.at[pl.ds(0, 2)]),
        (ask_first, ask.at[pl.ds(0, 5)]),
    ]
    for i, ref in enumerate(chunks):
        pairs.append((ref.at[pl.ds(0, KEYS)], to_right.at[3 + i]))
        pairs.append((ref.at[pl.ds(0, KEYS)], to_left.at[2 + i]))
        pairs.append((ref.at[pl.ds(ROW_ID, ASK)], ask.at[5 + i]))
    return pairs


def plan_third(at, ins, outs):
    return [(ins[0].at[pl.ds(3, 1)], outs[0]), (ins[1].at[pl.ds(3, 2)], outs[1])]


def plan_targets(at, ins, outs):
    return [
        (ins[0].at[x, pl.ds(X_T, TGT)], outs[0].at[z, pl.ds(x * TGT, TGT)]) for x in range(4) for z in range(8)
    ]


def plan_back(at, ins, outs):
    z = at[0]
    return [
        (ins[0].at[pl.ds(k * HALF, HALF)], outs[0].at[lax.rem(z + 8 - d, 8)]) for k, d in enumerate(ORDER)
    ]


def plan_cross_back(at, ins, outs):
    x = at[2]
    return [
        (ins[0].at[rows_at(lax.rem(x + 4 - d, 4), TGT, TGT)], out) for d, out in zip(X_ORDER, outs, strict=True)
    ]


def plan_back_swap(at, ins, outs):
    return [(ins[0].at[pl.ds(4 * (1 - at[1]), 4)], outs[0])]


def plan_unpack(at, ins, outs):
    c = at[1]
    pairs = []
    back, swapped = ins[:2]
    for j in range(4):
        pairs.append((back.at[4 * c + j], outs[0].at[half_rows(c), columns(j)]))
        pairs.append((swapped.at[j], outs[0].at[half_rows(1 - c), columns(j)]))
    return pairs


def plan_cross_unpack(at, ins, outs):
    pairs = []
    for piece, shift in zip(ins, X_ORDER, strict=True):
        column = rows_at(lax.rem(at[2] + shift, 4), HEAD_DIM, HEAD_DIM)
        pairs.append((piece, outs[0].at[:, column]))
    return pairs


def id_row(ref, start, lanes):
    return ref[start : start + 16, lanes].astype(jnp.float32)[0:1, :]


def attend_kernel(cross, parts, asks, has_carry, final, partner, *refs):
    refs = list(refs)
    q_refs = [refs.pop(0) for _ in range(asks)]
    id_ref = refs.pop(0) if cross else None
    key_refs = [refs.pop(0) for _ in parts]
    carry_refs = [refs.pop(0) if has_carry else None for _ in range(asks)]
    other_ref = refs.pop(0) if partner else None
    out_refs = refs
    keys, values, key_ids = [], [], []
    for ref, (start, count) in zip(key_refs, parts, strict=True):
        if cross:
            for i in range(count):
                keys.append(ref[i, 0:X_V, :])
                values.append(ref[i, X_V:X_ID, :])
                key_ids += [id_row(ref.at[i], X_ID, slice(j, j + 128)) for j in (0, 128)]
            continue
        for i in range(start, start + count):
            keys.append(ref[i, 0:HALF, :])
            values.append(ref[i, ROW_V : ROW_V + HALF, :])
            key_ids.append(id_row(ref.at[i], ROW_ID, slice(0, 128)))
    keys = jnp.concatenate(keys, axis=0)
    values = jnp.concatenate(values, axis=0)
    q_row = 0 if cross else ROW_Q - ROW_ID
    def step(ask, block):
        q_ref, carry_ref, out_ref = q_refs[ask], carry_refs[ask], out_refs[ask]
        rows = rows_at(block, 256, 256)
        chunk = 2 * block
        query = q_ref[pl.ds(chunk, 2), q_row : q_row + HALF, :].reshape(256, HEAD_DIM)
        query = query * jnp.bfloat16(HEAD_DIM**-0.5)
        query_ids = []
        for i in (chunk, chunk + 1):
            row = id_ref.at[i][0:1, :] if cross else id_row(q_ref.at[i], 0, slice(0, 128))
            query_ids.append(jnp.transpose(jnp.broadcast_to(row, (128, 128))))
        query_ids = jnp.concatenate(query_ids, axis=0)
        match = jnp.concatenate([query_ids == ids for ids in key_ids], axis=1)
        scores = lax.dot_general(
            query, keys, (((1,), (1,)), ((), ())), preferred_element_type=jnp.float32
        )
        scores = jnp.where(match, scores, NEG)
        top = jnp.max(scores, axis=1, keepdims=True)
        if has_carry:
            old = carry_ref[rows, HEAD_DIM : HEAD_DIM + 1]
            top = jnp.maximum(top, old)
        else:
            top = jnp.maximum(top, LOW)
        weights = jnp.exp(scores - top)
        total = jnp.sum(weights, axis=1, keepdims=True)
        summed = jnp.dot(
            weights.astype(jnp.bfloat16), values, preferred_element_type=jnp.float32
        )
        if has_carry:
            scale = jnp.exp(old - top)
            total = total + scale * carry_ref[rows, HEAD_DIM + 64 : HEAD_DIM + 65]
            summed = summed + scale * carry_ref[rows, 0:HEAD_DIM]
        lane = lax.broadcasted_iota(jnp.int32, (256, 128), 1)
        if not final:
            out_ref[rows, 0:HEAD_DIM] = summed
            out_ref[rows, HEAD_DIM:WIDE] = jnp.where(lane < 64, top, total)
            return
        some = total > 0.0
        safe = jnp.where(some, total, 1.0)
        level = jnp.where(some, top + jnp.log(safe), NEG)
        summed = summed * (1.0 / safe)
        if partner:
            theirs_out = other_ref[pl.ds(chunk, 2)].reshape(256, WIDE)
            other = level_of(theirs_out[:, HEAD_DIM:WIDE])
            both = jnp.maximum(level, other)
            mine, theirs = jnp.exp(level - both), jnp.exp(other - both)
            share = 1.0 / (mine + theirs)
            summed = (mine * share) * summed + (theirs * share) * theirs_out[:, 0:HEAD_DIM].astype(jnp.float32)
            out_ref[rows, :] = summed.astype(jnp.bfloat16)
        else:
            high = level.astype(jnp.bfloat16).astype(jnp.float32)
            middle = (level - high).astype(jnp.bfloat16).astype(jnp.float32)
            low = level - high - middle
            three = jnp.where(lane < 32, high, jnp.where(lane < 64, middle, low))
            for half in (0, 1):
                pick = slice(half * HALF, half * HALF + HALF)
                out_ref[chunk + half, :, 0:HEAD_DIM] = summed[pick].astype(jnp.bfloat16)
                out_ref[chunk + half, :, HEAD_DIM:WIDE] = three[pick].astype(jnp.bfloat16)

    each = 2

    def body(i, _):
        for ask in range(asks):
            for sub in range(each):
                step(ask, each * i + sub)
        return 0

    lax.fori_loop(0, 4 // each, body, 0)


def level_of(lanes):
    lanes = lanes.astype(jnp.float32)
    return (lanes[:, 0:1] + lanes[:, 32:33]) + lanes[:, 64:65]


def attend(queries, keys, ids=None, carry=(), final=False, other=None):
    arrays = [array for array, _, _ in keys]
    operands = [*queries] + ([] if ids is None else [ids]) + arrays + [*carry]
    operands += [] if other is None else [other]
    aliases = {}
    if carry and not final:
        aliases = {len(queries) + len(keys) + i: i for i in range(len(queries))}
    if not final:
        out = jax.ShapeDtypeStruct((1024, WIDE), jnp.float32)
    elif other is None:
        out = shaped(8, HALF, WIDE)
    else:
        out = shaped(1024, HEAD_DIM)
    parts = tuple((start, count) for _, start, count in keys)
    width = sum(count for _, count in parts) * HALF * (1 if ids is None else 2)
    return pl.pallas_call(
        functools.partial(
            attend_kernel, ids is not None, parts, len(queries), len(carry) > 0, final, other is not None
        ),
        out_shape=[out] * len(queries),
        in_specs=[whole()] * len(operands),
        out_specs=[whole()] * len(queries),
        input_output_aliases=aliases,
        **params(4 * 1024 * len(queries) * width * HEAD_DIM, 4 * MIB, 10),
    )(*operands)


def merge_kernel(part_ref, out_ref):
    levels = [level_of(part_ref[i, :, HEAD_DIM:WIDE]) for i in range(8)]
    top = functools.reduce(jnp.maximum, levels)
    shares = [jnp.exp(level - top) for level in levels]
    summed = sum(
        share * part_ref[i, :, 0:HEAD_DIM].astype(jnp.float32) for i, share in enumerate(shares)
    )
    out_ref[...] = (summed * (1.0 / sum(shares))).astype(jnp.bfloat16)


def merge(part):
    return pl.pallas_call(
        merge_kernel,
        out_shape=shaped(HALF, HEAD_DIM),
        in_specs=[whole()],
        out_specs=whole(),
        **params(0, 2 * MIB),
    )(part)


def per_device(
    enc_query,
    enc_key,
    enc_value,
    input_segments,
    doc_bounds,
    target_query,
    cross_key,
    cross_value,
    target_segments,
):
    del doc_bounds
    ix, iz, ic = lax.axis_index("x"), lax.axis_index("z"), lax.axis_index("core")
    place = jnp.stack([iz, ic, ix]).astype(jnp.int32)
    local = functools.partial(copies, place)
    numbers = input_segments.reshape(2, HALF)
    target_ids = target_segments.reshape(4, 8, TGT).transpose(1, 0, 2).astype(jnp.float32)
    target_ids = jnp.broadcast_to(target_ids.reshape(8, 1, 128), (8, 8, 128))

    near, away, heads = load(
        place, enc_key, enc_value, enc_query, target_query, cross_key, cross_value, numbers
    )
    swapped = core_swap(away)
    def packed(shifts, after=()):
        plan = functools.partial(plan_pack, shifts)
        return local(plan, [near, swapped, numbers], [(ROWS, HEAD_DIM)] * len(shifts), after)

    sent = packed(ORDER[:5])
    got = [sent[0]] + [z_send(sent[k], ORDER[k]) for k in range(1, 5)]
    cross = lax.all_to_all(heads, "x", 0, 0, tiled=True)
    group, ask = local(plan_first, got, [(5, KEYS, HEAD_DIM), (5, ASK, HEAD_DIM)], [cross])


    sent = packed(ORDER[5:], [group])
    rest = [z_send(chunk, d) for chunk, d in zip(sent, ORDER[5:], strict=True)]
    left, right = x_send(group, 1), x_send(group, 3)
    to_right, to_left, mine = local(
        plan_second,
        [*rest, left, right, ask],
        [(6, KEYS, HEAD_DIM), (5, KEYS, HEAD_DIM), (8, ASK, HEAD_DIM)],
    )

    from_left, from_right = x_send(to_right, 1), x_send(to_left, 3)
    theirs = core_swap(mine)
    (targets,) = local(plan_targets, [cross], [(8, HALF, HEAD_DIM)], [to_right])
    targets = lax.all_to_all(targets, "z", 0, 0, tiled=True)
    queries = (mine, theirs)
    carry = attend(queries, [(group, 0, 5), (to_right, 3, 3)])
    carry = attend(queries, [(left, 0, 5), (right, 0, 5)], carry=carry)
    lasts = local(
        plan_third, [from_left, from_right], [(1, KEYS, HEAD_DIM), (2, KEYS, HEAD_DIM)], [carry[0], targets]
    )

    far = [x_send(lasts[0], 1), x_send(lasts[1], 3)]
    (part,) = attend([targets], [(cross, 0, 4)], ids=target_ids, final=True)
    part = lax.all_to_all(part, "z", 0, 0, tiled=True)
    carry = attend(queries, [(from_left, 0, 6), (from_right, 0, 5)], carry=carry)
    far_keys = [(far[0], 0, 1), (far[1], 0, 2)]
    (partial,) = attend([theirs], far_keys, carry=carry[1:], final=True)
    (done,) = attend([mine], far_keys, carry=carry[:1], final=True, other=core_swap(partial))

    (back,) = local(plan_back, [done], [(8, HALF, HEAD_DIM)])
    merged = merge(part)
    blocks = local(plan_cross_back, [merged], [(TGT, HEAD_DIM)] * 4, [back])
    blocks = [x_send(b, -d) if d else b for b, d in zip(blocks, X_ORDER, strict=True)]
    back = lax.all_to_all(back, "z", 0, 0, tiled=True)
    (away,) = local(plan_back_swap, [back], [(4, HALF, HEAD_DIM)], blocks)
    (enc_out,) = local(plan_unpack, [back, core_swap(away)], [(2 * HALF, 4 * HEAD_DIM)])
    (cross_out,) = local(plan_cross_unpack, blocks, [(TGT, 4 * HEAD_DIM)])
    return enc_out, cross_out


def solution(mesh):
    shape = mesh.shape
    split = Mesh(
        mesh.devices.reshape(4, shape["ctx"] // 4, shape["head"], shape["dp"]), ("x", "z", "core", "dp")
    )
    tokens = P(("dp", "x", "z"), "core")
    placed = (
        tokens,
        tokens,
        tokens,
        P(("dp", "x", "z")),
        P(("dp", "x", "z"), None),
        tokens,
        tokens,
        tokens,
        P("dp"),
    )
    return jax.shard_map(
        per_device, mesh=split, in_specs=placed, out_specs=(tokens, tokens), check_vma=False
    )
```

time: 807 us -> 169 us (0.21)
  waiting for transfers between devices: 427 us -> 43.6 us
  blocking collectives: 256 us -> 0 us
  starting transfers between devices: 0.16 us -> 59.7 us
  matrix products: 50.6 us -> 0 us
  Pallas kernels: 0 us -> 45.9 us
  other arithmetic: 24.4 us -> 0.56 us
  local copies, waits for them, and re-layouts: 34.3 us -> 17.8 us
  between operations: 13.9 us -> 0.94 us
    all_gather x3 -> x0, waiting for transfers between devices: 336 us -> none  [the longest x1 153 us: per_device(): lax.all_gather(own[0], 'ctx', axis=0, tiled=True)]
    psum x1 -> x0, blocking collectives: 113 us -> none  [per_device(): totals = lax.psum(jnp.sum(weights, axis=2), 'ctx')]
    pmax x1 -> x0, blocking collectives: 113 us -> none  [per_device(): global_max = lax.pmax(local_max, 'ctx')]
    reduce_scatter x1 -> x0, waiting for transfers between devices: 89.8 us -> none  [per_device(): lax.psum_scatter(jnp.einsum('htk,khe->the', rounded, values3, preferred_e...]
    dot_general x4 -> x0, matrix products: 50.6 us -> none  [the longest x1 21.9 us: fold_keys(): jnp.einsum('qhe,khe->hqk', query3, split_heads(keys), preferred_element_t...]
    pallas_call x0 -> x19, Pallas kernels: none -> 45.9 us  [the longest x6 28 us: attend(): pl.pallas_call(functools.partial(attend_kernel, ids is not None, parts, l...]
    ppermute x0 -> x20, starting transfers between devices: none -> 34.6 us  [the longest x7 16.2 us: z_send(): return lax.ppermute(array, 'z', [(i, (i + shift) % 8) for i in range(8)])]
    all_gather x1 -> x0, blocking collectives: 29.7 us -> none  [per_device(): lax.all_gather(own[2], 'ctx', axis=0, tiled=True)]
  transfers between devices with their start and end apart: 4 -> 24, of which waited for: 4 -> 11; matrix products, arithmetic and copies ran while one was open for 6% -> 0% of each run, Pallas kernels for 0% -> 21%
where the time goes in v1:
time: 169 us; the launch traced here: 168 us
  starting transfers between devices  59.7 us (35%)
  Pallas kernels  45.9 us (27%)
  waiting for transfers between devices  43.6 us (26%)
  local copies, waits for them, and re-layouts  17.8 us (11%)
    pallas_call x6, Pallas kernels, attend(): pl.pallas_call(functools.partial(attend_kernel, ids is not None, parts, l...  28 us
    ppermute x7, waiting for transfers between devices, z_send(): return lax.ppermute(array, 'z', [(i, (i + shift) % 8) for i in range(8)])  20 us
    unnamed x52, local copies, waits for them, and re-layouts  17.6 us
    ppermute x7, starting transfers between devices, z_send(): return lax.ppermute(array, 'z', [(i, (i + shift) % 8) for i in range(8)])  16.2 us
    pallas_call x11, Pallas kernels, copies(): pl.pallas_call(kernel, out_shape=[shaped(*shape) for shape in outs], in_s...  13.3 us
    ppermute x9, starting transfers between devices, x_send(): return lax.ppermute(array, 'x', [(i, (i + shift) % 4) for i in range(4)])  11.7 us
    all_to_all x1, starting transfers between devices, per_device(): targets = lax.all_to_all(targets, 'z', 0, 0, tiled=True)  10.4 us
    all_to_all x1, waiting for transfers between devices, per_device(): back = lax.all_to_all(back, 'z', 0, 0, tiled=True)  9.47 us
  transfers between devices with their start and end apart: 24, of which 11 were waited for; matrix products, arithmetic and copies ran while one was open for 0% of the time, Pallas kernels for 21%

profile of v1, /device:TPU:1, one launch (start us, length us, event | category | flops | bytes accessed | tf_op | source)
XLA Modules:
  0.0 168.4 jit_solution(6279598829918805699)
XLA Ops:
  1.2 4.1 %shard_map.95 = (bf16[384,1024]{1,0:T(8,128)(2,1)}, bf16[384,1024]{1,0:T(8,128)(2,1)}, bf16[4,560,256]{2,1,0:T(8,128)(2,1)}) custom-call(s32[3]{0:T(128)} %pad_add_fusion.place_ref, bf16[256,1024]{1,0:T(8,128)(2,1)} %k_ref.1, bf16[256,1024]{1,0:T(8,128)(2,1)} %v_ref.1, bf16[256,1024]{1,0:T(8,128)(2,1)} %q_ref.1, bf16[32,1024]{1,0:T(8,128)(2,1)} %t_ref.1, ...), custom_call_target="tpu_custom_call" | custom-call | bytes 6291456 | tf_op jit(solution)/shard_map/pallas_call | solution.py:123
  5.3 3.3 %collective-permute-start = (bf16[384,1024]{1,0:T(8,128)(2,1)}, bf16[384,1024]{1,0:T(8,128)(2,1)S(1)}, u32[]{:S(2)}, u32[]{:S(2)}) collective-permute-start(bf16[384,1024]{1,0:T(8,128)(2,1)} %get-tuple-element.31), channel_id=1, source_target_pairs={{0,4},{4,0},{1,5},{5,1},{2,6},{6,2},{3,7},{7,3},{8,12},{12,8},{9,1... | collective-permute-start | bytes 2359304 | tf_op jit(solution)/shard_map/ppermute | solution.py:43
  8.6 3.5 %all-to-all-start = ((bf16[4,560,256]{2,1,0:T(8,128)(2,1)}), bf16[4,560,256]{2,1,0:T(8,128)(2,1)S(1)}, u32[]{:S(2)}, u32[]{:S(2)}) async-start(bf16[4,560,256]{2,1,0:T(8,128)(2,1)} %get-tuple-element.37), calls=%async_computation | async-start | bytes 2293760 | tf_op jit(solution)/shard_map/all_to_all | solution.py:412
  13.8 3.1 %collective-permute-start.1 = (bf16[400,256]{1,0:T(8,128)(2,1)}, bf16[400,256]{1,0:T(8,128)(2,1)S(1)}, u32[]{:S(2)}, u32[]{:S(2)}) collective-permute-start(bf16[400,256]{1,0:T(8,128)(2,1)} %get-tuple-element.33), channel_id=1, source_target_pairs={{0,24},{8,32},{16,40},{24,48},{32,56},{40,0},{48,8},{56,16},{1,25}... | collective-permute-start | bytes 614408 | tf_op jit(solution)/shard_map/ppermute | solution.py:35
  21.7 6.5 %all-to-all-done.refs_5_.refs_0_.refs_2_ = bf16[4,560,256]{2,1,0:T(8,128)(2,1)S(1)} async-done(((bf16[4,560,256]{2,1,0:T(8,128)(2,1)}), bf16[4,560,256]{2,1,0:T(8,128)(2,1)S(1)}, u32[]{:S(2)}, u32[]{:S(2)}) %all-to-all-start) | async-done | bytes 1146912 | tf_op jit(solution)/shard_map/all_to_all | solution.py:412
  29.4 7.3 %collective-permute-done.3.refs_3_ = bf16[400,256]{1,0:T(8,128)(2,1)S(1)} collective-permute-done((bf16[400,256]{1,0:T(8,128)(2,1)}, bf16[400,256]{1,0:T(8,128)(2,1)S(1)}, u32[]{:S(2)}, u32[]{:S(2)}) %collective-permute-start.3) | collective-permute-done | bytes 204832 | tf_op jit(solution)/shard_map/ppermute | solution.py:35
  39.5 2.7 %collective-permute-start.9 = (bf16[5,272,256]{2,1,0:T(8,128)(2,1)S(1)}, bf16[5,272,256]{2,1,0:T(8,128)(2,1)S(1)}, u32[]{:S(2)}, u32[]{:S(2)}) collective-permute-start(bf16[5,272,256]{2,1,0:T(8,128)(2,1)S(1)} %get-tuple-element.38.refs_3_.refs_2_), channel_id=1, source_target_pairs={{0,192},{64,0},{128,64},{192,128},{1,193},{65,1},{129,65},{193,129... | collective-permute-start | bytes 2088968 | tf_op jit(solution)/shard_map/ppermute | solution.py:39
  43.3 3.3 %collective-permute-start.6 = (bf16[400,256]{1,0:T(8,128)(2,1)S(1)}, bf16[400,256]{1,0:T(8,128)(2,1)S(1)}, u32[]{:S(2)}, u32[]{:S(2)}) collective-permute-start(bf16[400,256]{1,0:T(8,128)(2,1)S(1)} %get-tuple-element.40), channel_id=1, source_target_pairs={{0,48},{8,56},{16,0},{24,8},{32,16},{40,24},{48,32},{56,40},{1,49}... | collective-permute-start | bytes 614408 | tf_op jit(solution)/shard_map/ppermute | solution.py:35
  46.6 4.7 %collective-permute-start.7 = (bf16[400,256]{1,0:T(8,128)(2,1)S(1)}, bf16[400,256]{1,0:T(8,128)(2,1)S(1)}, u32[]{:S(2)}, u32[]{:S(2)}) collective-permute-start(bf16[400,256]{1,0:T(8,128)(2,1)S(1)} %get-tuple-element.41), channel_id=1, source_target_pairs={{0,32},{8,40},{16,48},{24,56},{32,0},{40,8},{48,16},{56,24},{1,33}... | collective-permute-start | bytes 614408 | tf_op jit(solution)/shard_map/ppermute | solution.py:35
  51.2 3.8 %collective-permute-done.5.refs_0_ = bf16[400,256]{1,0:T(8,128)(2,1)S(1)} collective-permute-done((bf16[400,256]{1,0:T(8,128)(2,1)S(1)}, bf16[400,256]{1,0:T(8,128)(2,1)S(1)}, u32[]{:S(2)}, u32[]{:S(2)}) %collective-permute-start.5) | collective-permute-done | bytes 204832 | tf_op jit(solution)/shard_map/ppermute | solution.py:35
  55.0 6.0 %collective-permute-done.7.refs_2_ = bf16[400,256]{1,0:T(8,128)(2,1)S(1)} collective-permute-done((bf16[400,256]{1,0:T(8,128)(2,1)S(1)}, bf16[400,256]{1,0:T(8,128)(2,1)S(1)}, u32[]{:S(2)}, u32[]{:S(2)}) %collective-permute-start.7) | collective-permute-done | bytes 204832 | tf_op jit(solution)/shard_map/ppermute | solution.py:35
  65.7 10.4 %all-to-all-start.1 = ((bf16[8,128,256]{2,1,0:T(8,128)(2,1)}), bf16[8,128,256]{2,1,0:T(8,128)(2,1)S(1)}, u32[]{:S(2)}, u32[]{:S(2)}) async-start(bf16[8,128,256]{2,1,0:T(8,128)(2,1)} %shard_map.102), calls=%async_computation.1 | async-start | bytes 1048576 | tf_op jit(solution)/shard_map/all_to_all | solution.py:428
  77.6 2.4 %collective-permute-start.11 = (bf16[5,272,256]{2,1,0:T(8,128)(2,1)}, bf16[5,272,256]{2,1,0:T(8,128)(2,1)}, u32[]{:S(2)}, u32[]{:S(2)}) collective-permute-start(bf16[5,272,256]{2,1,0:T(8,128)(2,1)} %copy-done.24), channel_id=1, source_target_pairs={{0,192},{64,0},{128,64},{192,128},{1,193},{65,1},{129,65},{193,129... | collective-permute-start | bytes 2088968 | tf_op jit(solution)/shard_map/ppermute | solution.py:39
  84.3 5.3 %shard_map.100 = (f32[1024,384]{1,0:T(8,128)S(1)}, f32[1024,384]{1,0:T(8,128)S(1)}) custom-call(bf16[8,144,256]{2,1,0:T(8,128)(2,1)S(1)} %copy-done.20, bf16[8,144,256]{2,1,0:T(8,128)(2,1)S(1)} %copy-done.17, bf16[5,272,256]{2,1,0:T(8,128)(2,1)S(1)} %copy-done.11, bf16[6,272,256]{2,1,0:T(8,128)(2,1)} %get-tuple-element.44.refs_3_.refs_1_), custom_call_target="tpu_custom_call" | custom-call | flops 2147483648 | bytes 4194304 | tf_op jit(solution)/shard_map/pallas_call | solution.py:351
  90.8 2.5 %all-to-all-done.1.refs_3_.refs_0_ = bf16[8,128,256]{2,1,0:T(8,128)(2,1)S(1)} async-done(((bf16[8,128,256]{2,1,0:T(8,128)(2,1)}), bf16[8,128,256]{2,1,0:T(8,128)(2,1)S(1)}, u32[]{:S(2)}, u32[]{:S(2)}) %all-to-all-start.1) | async-done | bytes 524320 | tf_op jit(solution)/shard_map/all_to_all | solution.py:428
  93.3 2.9 %shard_map.108 = bf16[8,128,384]{2,1,0:T(8,128)(2,1)S(1)} custom-call(bf16[8,128,256]{2,1,0:T(8,128)(2,1)S(1)} %all-to-all-done.1.refs_3_.refs_0_, f32[8,8,128]{2,1,0:T(8,128)S(1)} %broadcast_in_dim.8.refs_1_, bf16[4,560,256]{2,1,0:T(8,128)(2,1)S(1)} %all-to-all-done.refs_5_.refs_0_.refs_2_), custom_call_target="tpu_custom_call" | custom-call | flops 1073741824 | bytes 4194304 | tf_op jit(solution)/shard_map/pallas_call | solution.py:351
  97.1 4.3 %all-to-all-start.3 = ((bf16[8,128,384]{2,1,0:T(8,128)(2,1)}), bf16[8,128,384]{2,1,0:T(8,128)(2,1)S(1)}, u32[]{:S(2)}, u32[]{:S(2)}) async-start(bf16[8,128,384]{2,1,0:T(8,128)(2,1)} %copy-done.9), calls=%async_computation.3 | async-start | bytes 1572864 | tf_op jit(solution)/shard_map/all_to_all | solution.py:438
  107.2 6.4 %shard_map.101 = (f32[1024,384]{1,0:T(8,128)S(1)}, f32[1024,384]{1,0:T(8,128)S(1)}) custom-call(bf16[8,144,256]{2,1,0:T(8,128)(2,1)S(1)} %copy-done.21, bf16[8,144,256]{2,1,0:T(8,128)(2,1)S(1)} %copy-done.18, bf16[5,272,256]{2,1,0:T(8,128)(2,1)S(1)} %copy-done.15, bf16[5,272,256]{2,1,0:T(8,128)(2,1)S(1)} %copy-done.13, ...), custom_call_target="tpu_custom_call", output_to_operand_aliasing={{0}: (4, {}), {1}: (5, {})} | custom-call | flops 2684354560 | bytes 4194304 | tf_op jit(solution)/shard_map/pallas_call | solution.py:351
  119.0 8.8 %shard_map.104 = (f32[1024,384]{1,0:T(8,128)S(1)}, f32[1024,384]{1,0:T(8,128)S(1)}) custom-call(bf16[8,144,256]{2,1,0:T(8,128)(2,1)S(1)} %copy-done.21, bf16[8,144,256]{2,1,0:T(8,128)(2,1)S(1)} %copy-done.18, bf16[6,272,256]{2,1,0:T(8,128)(2,1)} %collective-permute-done.10.refs_0_.refs_2_, ...), custom_call_target="tpu_custom_call", output_to_operand_aliasing={{0}: (4, {}), {1}: (5, {})} | custom-call | flops 2952790016 | bytes 4194304 | tf_op jit(solution)/shard_map/pallas_call | solution.py:351
  136.1 2.4 %shard_map.106.refs_0_ = bf16[1024,256]{1,0:T(8,128)(2,1)S(1)} custom-call(bf16[8,144,256]{2,1,0:T(8,128)(2,1)S(1)} %copy-done.21, bf16[1,272,256]{2,1,0:T(8,128)(2,1)S(1)} %collective-permute-done.13.refs_1_, bf16[2,272,256]{2,1,0:T(8,128)(2,1)S(1)} %collective-permute-done.14.refs_2_, f32[1024,384]{1,0:T(8,128)S(1)} %get-tuple-element.52.refs_3_, ...), custom_call_target="tpu_custom_call" | custom-call | flops 402653184 | bytes 4194304 | tf_op jit(solution)/shard_map/pallas_call | solution.py:351
  139.9 6.8 %all-to-all-start.2 = ((bf16[8,128,256]{2,1,0:T(8,128)(2,1)}), bf16[8,128,256]{2,1,0:T(8,128)(2,1)S(1)}, u32[]{:S(2)}, u32[]{:S(2)}) async-start(bf16[8,128,256]{2,1,0:T(8,128)(2,1)} %shard_map.107.refs_1_), calls=%async_computation.2 | async-start | bytes 1048576 | tf_op jit(solution)/shard_map/all_to_all | solution.py:448
  147.8 3.0 %collective-permute-start.16 = (bf16[32,256]{1,0:T(8,128)(2,1)S(1)}, bf16[32,256]{1,0:T(8,128)(2,1)S(1)}, u32[]{:S(2)}, u32[]{:S(2)}) collective-permute-start(bf16[32,256]{1,0:T(8,128)(2,1)S(1)} %get-tuple-element.55), channel_id=1, source_target_pairs={{0,192},{64,0},{128,64},{192,128},{1,193},{65,1},{129,65},{193,129... | collective-permute-start | bytes 49160 | tf_op jit(solution)/shard_map/ppermute | solution.py:39
  152.1 2.8 %collective-permute-done.17.refs_3_.refs_2_ = bf16[32,256]{1,0:T(8,128)(2,1)S(1)} collective-permute-done((bf16[32,256]{1,0:T(8,128)(2,1)S(1)}, bf16[32,256]{1,0:T(8,128)(2,1)S(1)}, u32[]{:S(2)}, u32[]{:S(2)}) %collective-permute-start.17) | collective-permute-done | bytes 16416 | tf_op jit(solution)/shard_map/ppermute | solution.py:39
  155.2 9.5 %all-to-all-done.2.refs_0_ = bf16[8,128,256]{2,1,0:T(8,128)(2,1)S(1)} async-done(((bf16[8,128,256]{2,1,0:T(8,128)(2,1)}), bf16[8,128,256]{2,1,0:T(8,128)(2,1)S(1)}, u32[]{:S(2)}, u32[]{:S(2)}) %all-to-all-start.2) | async-done | bytes 524320 | tf_op jit(solution)/shard_map/all_to_all | solution.py:448
  (101 shorter events, 51.6 us)
Async XLA Ops:
  5.3 6.9 %collective-permute-start = (bf16[384,1024]{1,0:T(8,128)(2,1)}, bf16[384,1024]{1,0:T(8,128)(2,1)S(1)}, u32[]{:S(2)}, u32[]{:S(2)}) collective-permute-start(bf16[384,1024]{1,0:T(8,128)(2,1)} %get-tuple-element.31), channel_id=1, source_target_pairs={{0,4},{4,0},{1,5},{5,1},{2,6},{6,2},{3,7},{7,3},{8,12},{12,8},{9,1... | collective-permute-start | bytes 2359304 | tf_op jit(solution)/shard_map/ppermute | solution.py:43
  8.6 19.6 %all-to-all-start = ((bf16[4,560,256]{2,1,0:T(8,128)(2,1)}), bf16[4,560,256]{2,1,0:T(8,128)(2,1)S(1)}, u32[]{:S(2)}, u32[]{:S(2)}) async-start(bf16[4,560,256]{2,1,0:T(8,128)(2,1)} %get-tuple-element.37), calls=%async_computation | async-start | bytes 2293760 | tf_op jit(solution)/shard_map/all_to_all | solution.py:412
  13.8 15.6 %collective-permute-start.1 = (bf16[400,256]{1,0:T(8,128)(2,1)}, bf16[400,256]{1,0:T(8,128)(2,1)S(1)}, u32[]{:S(2)}, u32[]{:S(2)}) collective-permute-start(bf16[400,256]{1,0:T(8,128)(2,1)} %get-tuple-element.33), channel_id=1, source_target_pairs={{0,24},{8,32},{16,40},{24,48},{32,56},{40,0},{48,8},{56,16},{1,25}... | collective-permute-start | bytes 614408 | tf_op jit(solution)/shard_map/ppermute | solution.py:35
  16.9 12.5 %collective-permute-start.2 = (bf16[400,256]{1,0:T(8,128)(2,1)}, bf16[400,256]{1,0:T(8,128)(2,1)S(1)}, u32[]{:S(2)}, u32[]{:S(2)}) collective-permute-start(bf16[400,256]{1,0:T(8,128)(2,1)} %get-tuple-element.34), channel_id=1, source_target_pairs={{0,40},{8,48},{16,56},{24,0},{32,8},{40,16},{48,24},{56,32},{1,41}... | collective-permute-start | bytes 614408 | tf_op jit(solution)/shard_map/ppermute | solution.py:35
  19.0 17.7 %collective-permute-start.3 = (bf16[400,256]{1,0:T(8,128)(2,1)}, bf16[400,256]{1,0:T(8,128)(2,1)S(1)}, u32[]{:S(2)}, u32[]{:S(2)}) collective-permute-start(bf16[400,256]{1,0:T(8,128)(2,1)} %get-tuple-element.35), channel_id=1, source_target_pairs={{0,8},{8,16},{16,24},{24,32},{32,40},{40,48},{48,56},{56,0},{1,9},... | collective-permute-start | bytes 614408 | tf_op jit(solution)/shard_map/ppermute | solution.py:35
  19.8 18.7 %collective-permute-start.4 = (bf16[400,256]{1,0:T(8,128)(2,1)}, bf16[400,256]{1,0:T(8,128)(2,1)}, u32[]{:S(2)}, u32[]{:S(2)}) collective-permute-start(bf16[400,256]{1,0:T(8,128)(2,1)} %get-tuple-element.36), channel_id=1, source_target_pairs={{0,56},{8,0},{16,8},{24,16},{32,24},{40,32},{48,40},{56,48},{1,57}... | collective-permute-start | bytes 614408 | tf_op jit(solution)/shard_map/ppermute | solution.py:35
  39.5 21.6 %collective-permute-start.9 = (bf16[5,272,256]{2,1,0:T(8,128)(2,1)S(1)}, bf16[5,272,256]{2,1,0:T(8,128)(2,1)S(1)}, u32[]{:S(2)}, u32[]{:S(2)}) collective-permute-start(bf16[5,272,256]{2,1,0:T(8,128)(2,1)S(1)} %get-tuple-element.38.refs_3_.refs_2_), channel_id=1, source_target_pairs={{0,192},{64,0},{128,64},{192,128},{1,193},{65,1},{129,65},{193,129... | collective-permute-start | bytes 2088968 | tf_op jit(solution)/shard_map/ppermute | solution.py:39
  42.2 18.9 %collective-permute-start.8 = (bf16[5,272,256]{2,1,0:T(8,128)(2,1)S(1)}, bf16[5,272,256]{2,1,0:T(8,128)(2,1)S(1)}, u32[]{:S(2)}, u32[]{:S(2)}) collective-permute-start(bf16[5,272,256]{2,1,0:T(8,128)(2,1)S(1)} %get-tuple-element.38.refs_3_.refs_2_), channel_id=1, source_target_pairs={{0,64},{64,128},{128,192},{192,0},{1,65},{65,129},{129,193},{193,1... | collective-permute-start | bytes 2088968 | tf_op jit(solution)/shard_map/ppermute | solution.py:39
  42.9 12.1 %collective-permute-start.5 = (bf16[400,256]{1,0:T(8,128)(2,1)S(1)}, bf16[400,256]{1,0:T(8,128)(2,1)S(1)}, u32[]{:S(2)}, u32[]{:S(2)}) collective-permute-start(bf16[400,256]{1,0:T(8,128)(2,1)S(1)} %get-tuple-element.39), channel_id=1, source_target_pairs={{0,16},{8,24},{16,32},{24,40},{32,48},{40,56},{48,0},{56,8},{1,17}... | collective-permute-start | bytes 614408 | tf_op jit(solution)/shard_map/ppermute | solution.py:35
  43.3 11.7 %collective-permute-start.6 = (bf16[400,256]{1,0:T(8,128)(2,1)S(1)}, bf16[400,256]{1,0:T(8,128)(2,1)S(1)}, u32[]{:S(2)}, u32[]{:S(2)}) collective-permute-start(bf16[400,256]{1,0:T(8,128)(2,1)S(1)} %get-tuple-element.40), channel_id=1, source_target_pairs={{0,48},{8,56},{16,0},{24,8},{32,16},{40,24},{48,32},{56,40},{1,49}... | collective-permute-start | bytes 614408 | tf_op jit(solution)/shard_map/ppermute | solution.py:35
  46.6 14.5 %collective-permute-start.7 = (bf16[400,256]{1,0:T(8,128)(2,1)S(1)}, bf16[400,256]{1,0:T(8,128)(2,1)S(1)}, u32[]{:S(2)}, u32[]{:S(2)}) collective-permute-start(bf16[400,256]{1,0:T(8,128)(2,1)S(1)} %get-tuple-element.41), channel_id=1, source_target_pairs={{0,32},{8,40},{16,48},{24,56},{32,0},{40,8},{48,16},{56,24},{1,33}... | collective-permute-start | bytes 614408 | tf_op jit(solution)/shard_map/ppermute | solution.py:35
  65.7 27.6 %all-to-all-start.1 = ((bf16[8,128,256]{2,1,0:T(8,128)(2,1)}), bf16[8,128,256]{2,1,0:T(8,128)(2,1)S(1)}, u32[]{:S(2)}, u32[]{:S(2)}) async-start(bf16[8,128,256]{2,1,0:T(8,128)(2,1)} %shard_map.102), calls=%async_computation.1 | async-start | bytes 1048576 | tf_op jit(solution)/shard_map/all_to_all | solution.py:428
  76.1 4.1 %collective-permute-start.12 = (bf16[8,144,256]{2,1,0:T(8,128)(2,1)S(1)}, bf16[8,144,256]{2,1,0:T(8,128)(2,1)S(1)}, u32[]{:S(2)}, u32[]{:S(2)}) collective-permute-start(bf16[8,144,256]{2,1,0:T(8,128)(2,1)S(1)} %get-tuple-element.43.refs_0_), channel_id=1, source_target_pairs={{0,4},{4,0},{1,5},{5,1},{2,6},{6,2},{3,7},{7,3},{8,12},{12,8},{9,1... | collective-permute-start | bytes 1769480 | tf_op jit(solution)/shard_map/ppermute | solution.py:43
  77.3 36.3 %collective-permute-start.10 = (bf16[6,272,256]{2,1,0:T(8,128)(2,1)}, bf16[6,272,256]{2,1,0:T(8,128)(2,1)}, u32[]{:S(2)}, u32[]{:S(2)}) collective-permute-start(bf16[6,272,256]{2,1,0:T(8,128)(2,1)} %get-tuple-element.44.refs_3_.refs_1_), channel_id=1, source_target_pairs={{0,64},{64,128},{128,192},{192,0},{1,65},{65,129},{129,193},{193,1... | collective-permute-start | bytes 2506760 | tf_op jit(solution)/shard_map/ppermute | solution.py:39
  77.6 36.0 %collective-permute-start.11 = (bf16[5,272,256]{2,1,0:T(8,128)(2,1)}, bf16[5,272,256]{2,1,0:T(8,128)(2,1)}, u32[]{:S(2)}, u32[]{:S(2)}) collective-permute-start(bf16[5,272,256]{2,1,0:T(8,128)(2,1)} %copy-done.24), channel_id=1, source_target_pairs={{0,192},{64,0},{128,64},{192,128},{1,193},{65,1},{129,65},{193,129... | collective-permute-start | bytes 2088968 | tf_op jit(solution)/shard_map/ppermute | solution.py:39
  97.1 42.8 %all-to-all-start.3 = ((bf16[8,128,384]{2,1,0:T(8,128)(2,1)}), bf16[8,128,384]{2,1,0:T(8,128)(2,1)S(1)}, u32[]{:S(2)}, u32[]{:S(2)}) async-start(bf16[8,128,384]{2,1,0:T(8,128)(2,1)} %copy-done.9), calls=%async_computation.3 | async-start | bytes 1572864 | tf_op jit(solution)/shard_map/all_to_all | solution.py:438
  115.6 13.4 %collective-permute-start.14 = (bf16[2,272,256]{2,1,0:T(8,128)(2,1)S(1)}, bf16[2,272,256]{2,1,0:T(8,128)(2,1)S(1)}, u32[]{:S(2)}, u32[]{:S(2)}) collective-permute-start(bf16[2,272,256]{2,1,0:T(8,128)(2,1)S(1)} %get-tuple-element.50), channel_id=1, source_target_pairs={{0,192},{64,0},{128,64},{192,128},{1,193},{65,1},{129,65},{193,129... | collective-permute-start | bytes 835592 | tf_op jit(solution)/shard_map/ppermute | solution.py:39
  117.6 11.4 %collective-permute-start.13 = (bf16[1,272,256]{2,1,0:T(8,128)(2,1)S(1)}, bf16[1,272,256]{2,1,0:T(8,128)(2,1)S(1)}, u32[]{:S(2)}, u32[]{:S(2)}) collective-permute-start(bf16[1,272,256]{2,1,0:T(8,128)(2,1)S(1)} %get-tuple-element.49), channel_id=1, source_target_pairs={{0,64},{64,128},{128,192},{192,0},{1,65},{65,129},{129,193},{193,1... | collective-permute-start | bytes 417800 | tf_op jit(solution)/shard_map/ppermute | solution.py:39
  132.6 3.5 %collective-permute-start.15 = (bf16[8,128,384]{2,1,0:T(8,128)(2,1)S(1)}, bf16[8,128,384]{2,1,0:T(8,128)(2,1)S(1)}, u32[]{:S(2)}, u32[]{:S(2)}) collective-permute-start(bf16[8,128,384]{2,1,0:T(8,128)(2,1)S(1)} %shard_map.105), channel_id=1, source_target_pairs={{0,4},{4,0},{1,5},{5,1},{2,6},{6,2},{3,7},{7,3},{8,12},{12,8},{9,1... | collective-permute-start | bytes 2359304 | tf_op jit(solution)/shard_map/ppermute | solution.py:43
  139.9 24.8 %all-to-all-start.2 = ((bf16[8,128,256]{2,1,0:T(8,128)(2,1)}), bf16[8,128,256]{2,1,0:T(8,128)(2,1)S(1)}, u32[]{:S(2)}, u32[]{:S(2)}) async-start(bf16[8,128,256]{2,1,0:T(8,128)(2,1)} %shard_map.107.refs_1_), calls=%async_computation.2 | async-start | bytes 1048576 | tf_op jit(solution)/shard_map/all_to_all | solution.py:448
  147.8 4.3 %collective-permute-start.16 = (bf16[32,256]{1,0:T(8,128)(2,1)S(1)}, bf16[32,256]{1,0:T(8,128)(2,1)S(1)}, u32[]{:S(2)}, u32[]{:S(2)}) collective-permute-start(bf16[32,256]{1,0:T(8,128)(2,1)S(1)} %get-tuple-element.55), channel_id=1, source_target_pairs={{0,192},{64,0},{128,64},{192,128},{1,193},{65,1},{129,65},{193,129... | collective-permute-start | bytes 49160 | tf_op jit(solution)/shard_map/ppermute | solution.py:39
  150.8 4.1 %collective-permute-start.17 = (bf16[32,256]{1,0:T(8,128)(2,1)S(1)}, bf16[32,256]{1,0:T(8,128)(2,1)S(1)}, u32[]{:S(2)}, u32[]{:S(2)}) collective-permute-start(bf16[32,256]{1,0:T(8,128)(2,1)S(1)} %get-tuple-element.56), channel_id=1, source_target_pairs={{0,64},{64,128},{128,192},{192,0},{1,65},{65,129},{129,193},{193,1... | collective-permute-start | bytes 49160 | tf_op jit(solution)/shard_map/ppermute | solution.py:39
  150.8 4.4 %collective-permute-start.18 = (bf16[32,256]{1,0:T(8,128)(2,1)S(1)}, bf16[32,256]{1,0:T(8,128)(2,1)S(1)}, u32[]{:S(2)}, u32[]{:S(2)}) collective-permute-start(bf16[32,256]{1,0:T(8,128)(2,1)S(1)} %get-tuple-element.57), channel_id=1, source_target_pairs={{0,128},{64,192},{128,0},{192,64},{1,129},{65,193},{129,1},{193,65... | collective-permute-start | bytes 49160 | tf_op jit(solution)/shard_map/ppermute | solution.py:39
  165.2 1.8 %collective-permute-start.19 = (bf16[4,128,256]{2,1,0:T(8,128)(2,1)S(1)}, bf16[4,128,256]{2,1,0:T(8,128)(2,1)S(1)}, u32[]{:S(2)}, u32[]{:S(2)}) collective-permute-start(bf16[4,128,256]{2,1,0:T(8,128)(2,1)S(1)} %shard_map.111), channel_id=1, source_target_pairs={{0,4},{4,0},{1,5},{5,1},{2,6},{6,2},{3,7},{7,3},{8,12},{12,8},{9,1... | collective-permute-start | bytes 786440 | tf_op jit(solution)/shard_map/ppermute | solution.py:43
  (26 other events, 82.2 us)

commit v2 on v1

--- a/solution.py
+++ b/solution.py
@@ -23,7 +23,7 @@
 X_V = 2 * HALF
 X_ID = 4 * HALF
 X_T = X_ID + 16
-X_ROWS = X_T + TGT
+X_ROWS = X_T + 8 * TGT
 ORDER = (0, 3, 5, 1, 7, 2, 6, 4)
 X_ORDER = (0, 1, 3, 2)
 WIDE = HEAD_DIM + 128
@@ -101,33 +101,57 @@
     return jnp.broadcast_to(row, (16, HALF)).astype(HALF_TYPE)
 
 
-def load(place, keys, values, query, target, cross_keys, cross_values, numbers):
-    def kernel(place_ref, k_ref, v_ref, q_ref, t_ref, xk_ref, xv_ref, id_ref, near, away, heads, sems):
+def run(made, sems):
+    made = [pltpu.make_async_copy(a, b, sems.at[i]) for i, (a, b) in enumerate(made)]
+    for one in made:
+        one.start()
+    return made
+
+
+def load(place, keys, values, query):
+    def kernel(place_ref, k_ref, v_ref, q_ref, near, away, sems):
         c = place_ref[1]
         made = []
         for side, out in ((1 - c, away), (c, near)):
             for i, ref in enumerate((k_ref, v_ref, q_ref)):
                 made.append((ref.at[half_rows(side)], out.at[pl.ds(i * HALF, HALF)]))
+        for one in run(made, sems):
+            one.wait()
+
+    return pl.pallas_call(
+        kernel,
+        out_shape=[shaped(3 * HALF, 4 * HEAD_DIM)] * 2,
+        in_specs=[scalars()] + [pl.BlockSpec(memory_space=pl.ANY)] * 3,
+        out_specs=[whole()] * 2,
+        scratch_shapes=[pltpu.SemaphoreType.DMA((6,))],
+        **params(0, 6 * MIB, 56),
+    )(place, keys, values, query)
+
+
+def load_cross(cross_keys, cross_values, numbers, targets, after):
+    def kernel(xk_ref, xv_ref, id_ref, t_ref, _, heads, sems):
+        made = []
         for j in range(4):
-            for ref, row, size in ((xk_ref, 0, 2 * HALF), (xv_ref, X_V, 2 * HALF), (t_ref, X_T, TGT)):
-                made.append((ref.at[:, columns(j)], heads.at[j, pl.ds(row, size)]))
-        made = [pltpu.make_async_copy(a, b, sems.at[i]) for i, (a, b) in enumerate(made)]
-        for one in made:
-            one.start()
+            for ref, row in ((xk_ref, 0), (xv_ref, X_V)):
+                made.append((ref.at[:, columns(j)], heads.at[j, pl.ds(row, 2 * HALF)]))
+            for z in range(8):
+                made.append((t_ref.at[z, :, columns(j)], heads.at[j, pl.ds(X_T + z * TGT, TGT)]))
+        made = run(made, sems)
         for j in range(4):
             for half in (0, 1):
                 heads[j, X_ID:X_T, half * HALF : half * HALF + HALF] = named(id_ref, half)
         for one in made:
             one.wait()
 
+    anywhere = pl.BlockSpec(memory_space=pl.ANY)
     return pl.pallas_call(
         kernel,
-        out_shape=[shaped(3 * HALF, 4 * HEAD_DIM)] * 2 + [shaped(4, X_ROWS, HEAD_DIM)],
-        in_specs=[scalars()] + [pl.BlockSpec(memory_space=pl.ANY)] * 6 + [whole()],
-        out_specs=[whole()] * 3,
-        scratch_shapes=[pltpu.SemaphoreType.DMA((18,))],
-        **params(0, 6 * MIB, 56),
-    )(place, keys, values, query, target, cross_keys, cross_values, numbers)
+        out_shape=shaped(4, X_ROWS, HEAD_DIM),
+        in_specs=[anywhere, anywhere, whole(), anywhere, anywhere],
+        out_specs=whole(),
+        scratch_shapes=[pltpu.SemaphoreType.DMA((40,))],
+        **params(0, 4 * MIB, 56),
+    )(cross_keys, cross_values, numbers, targets, after)
 
 
 class Either:
@@ -192,7 +216,9 @@
 
 def plan_targets(at, ins, outs):
     return [
-        (ins[0].at[x, pl.ds(X_T, TGT)], outs[0].at[z, pl.ds(x * TGT, TGT)]) for x in range(4) for z in range(8)
+        (ins[0].at[x, pl.ds(X_T + z * TGT, TGT)], outs[0].at[z, pl.ds(x * TGT, TGT)])
+        for x in range(4)
+        for z in range(8)
     ]
 
 
@@ -356,7 +382,7 @@
         in_specs=[whole()] * len(operands),
         out_specs=[whole()] * len(queries),
         input_output_aliases=aliases,
-        **params(4 * 1024 * len(queries) * width * HEAD_DIM, 4 * MIB, 10),
+        **params(4 * 1024 * len(queries) * width * HEAD_DIM, 4 * MIB, 24),
     )(*operands)
 
 
@@ -399,9 +425,9 @@
     target_ids = target_segments.reshape(4, 8, TGT).transpose(1, 0, 2).astype(jnp.float32)
     target_ids = jnp.broadcast_to(target_ids.reshape(8, 1, 128), (8, 8, 128))
 
-    near, away, heads = load(
-        place, enc_key, enc_value, enc_query, target_query, cross_key, cross_value, numbers
-    )
+    spread = jnp.broadcast_to(target_query[None], (8, TGT, 4 * HEAD_DIM))
+    spread = lax.all_to_all(spread, "z", 0, 0, tiled=True)
+    near, away = load(place, enc_key, enc_value, enc_query)
     swapped = core_swap(away)
     def packed(shifts, after=()):
         plan = functools.partial(plan_pack, shifts)
@@ -409,8 +435,9 @@
 
     sent = packed(ORDER[:5])
     got = [sent[0]] + [z_send(sent[k], ORDER[k]) for k in range(1, 5)]
+    heads = load_cross(cross_key, cross_value, numbers, spread, got[3])
     cross = lax.all_to_all(heads, "x", 0, 0, tiled=True)
-    group, ask = local(plan_first, got, [(5, KEYS, HEAD_DIM), (5, ASK, HEAD_DIM)], [cross])
+    group, ask = local(plan_first, got, [(5, KEYS, HEAD_DIM), (5, ASK, HEAD_DIM)], [heads])
 
 
     sent = packed(ORDER[5:], [group])
@@ -425,17 +452,15 @@
     from_left, from_right = x_send(to_right, 1), x_send(to_left, 3)
     theirs = core_swap(mine)
     (targets,) = local(plan_targets, [cross], [(8, HALF, HEAD_DIM)], [to_right])
-    targets = lax.all_to_all(targets, "z", 0, 0, tiled=True)
-    queries = (mine, theirs)
-    carry = attend(queries, [(group, 0, 5), (to_right, 3, 3)])
-    carry = attend(queries, [(left, 0, 5), (right, 0, 5)], carry=carry)
-    lasts = local(
-        plan_third, [from_left, from_right], [(1, KEYS, HEAD_DIM), (2, KEYS, HEAD_DIM)], [carry[0], targets]
-    )
-
-    far = [x_send(lasts[0], 1), x_send(lasts[1], 3)]
     (part,) = attend([targets], [(cross, 0, 4)], ids=target_ids, final=True)
     part = lax.all_to_all(part, "z", 0, 0, tiled=True)
+    queries = (mine, theirs)
+    carry = attend(queries, [(group, 0, 5), (to_right, 3, 3), (left, 0, 5), (right, 0, 5)])
+    lasts = local(
+        plan_third, [from_left, from_right], [(1, KEYS, HEAD_DIM), (2, KEYS, HEAD_DIM)], [carry[0]]
+    )
+
+    far = [x_send(lasts[0], 1), x_send(lasts[1], 3)]
     carry = attend(queries, [(from_left, 0, 6), (from_right, 0, 5)], carry=carry)
     far_keys = [(far[0], 0, 1), (far[1], 0, 2)]
     (partial,) = attend([theirs], far_keys, carry=carry[1:], final=True)

time: 169 us -> 158 us (0.935)
  local copies, waits for them, and re-layouts: 17.8 us -> 4.45 us
  starting transfers between devices: 59.7 us -> 50.4 us
  waiting for transfers between devices: 43.6 us -> 51.9 us
  Pallas kernels: 45.9 us -> 49.3 us
    unnamed x52 -> x38, local copies, waits for them, and re-layouts: 17.6 us -> 3.43 us
    all_to_all x1, waiting for transfers between devices: 2.52 us -> 9.79 us  [per_device(): spread = lax.all_to_all(spread, 'z', 0, 0, tiled=True)]
    ppermute x9, waiting for transfers between devices: 3.13 us -> 10 us  [x_send(): return lax.ppermute(array, 'x', [(i, (i + shift) % 4) for i in range(4)])]
    all_to_all x1, waiting for transfers between devices: 6.55 us -> 0.01 us  [per_device(): cross = lax.all_to_all(heads, 'x', 0, 0, tiled=True)]
    ppermute x7, starting transfers between devices: 16.2 us -> 11.6 us  [z_send(): return lax.ppermute(array, 'z', [(i, (i + shift) % 8) for i in range(8)])]
    all_to_all x1, starting transfers between devices: 10.4 us -> 6.45 us  [per_device(): spread = lax.all_to_all(spread, 'z', 0, 0, tiled=True)]
    pallas_call x1 -> x2, Pallas kernels: 4.07 us -> 7.03 us  [the longest x1 3.7 us: load_cross(): pl.pallas_call(kernel, out_shape=shaped(4, X_ROWS, HEAD_DIM), in_specs=[a...]
    ppermute x9, starting transfers between devices: 11.7 us -> 9.15 us  [x_send(): return lax.ppermute(array, 'x', [(i, (i + shift) % 4) for i in range(4)])]
  transfers between devices with their start and end apart: 24 -> 24, of which waited for: 11 -> 12; matrix products, arithmetic and copies ran while one was open for 0% -> 1% of each run, Pallas kernels for 21% -> 28%
where the time goes in v2:
time: 158 us
  waiting for transfers between devices  51.9 us (33%)
  starting transfers between devices  50.4 us (32%)
  Pallas kernels  49.3 us (31%)
  local copies, waits for them, and re-layouts  4.45 us (3%)
    pallas_call x5, Pallas kernels, attend(): pl.pallas_call(functools.partial(attend_kernel, ids is not None, parts, l...  29.4 us
    ppermute x7, waiting for transfers between devices, z_send(): return lax.ppermute(array, 'z', [(i, (i + shift) % 8) for i in range(8)])  18.9 us
    pallas_call x11, Pallas kernels, copies(): pl.pallas_call(kernel, out_shape=[shaped(*shape) for shape in outs], in_s...  12.4 us
    ppermute x7, starting transfers between devices, z_send(): return lax.ppermute(array, 'z', [(i, (i + shift) % 8) for i in range(8)])  11.6 us
    all_to_all x1, waiting for transfers between devices, per_device(): back = lax.all_to_all(back, 'z', 0, 0, tiled=True)  11.3 us
    ppermute x9, waiting for transfers between devices, x_send(): return lax.ppermute(array, 'x', [(i, (i + shift) % 4) for i in range(4)])  10 us
    all_to_all x1, waiting for transfers between devices, per_device(): spread = lax.all_to_all(spread, 'z', 0, 0, tiled=True)  9.79 us
    ppermute x9, starting transfers between devices, x_send(): return lax.ppermute(array, 'x', [(i, (i + shift) % 4) for i in range(4)])  9.15 us
  transfers between devices with their start and end apart: 24, of which 12 were waited for; matrix products, arithmetic and copies ran while one was open for 1% of the time, Pallas kernels for 28%

profile of v2, /device:TPU:1, one launch (start us, length us, event | category | flops | bytes accessed | tf_op | source)
XLA Modules:
  0.0 157.6 jit_solution(15878915397909014731)
XLA Ops:
  1.3 3.3 %shard_map.95 = (bf16[384,1024]{1,0:T(8,128)(2,1)}, bf16[384,1024]{1,0:T(8,128)(2,1)}) custom-call(s32[3]{0:T(128)} %pad_add_fusion.place_ref, bf16[256,1024]{1,0:T(8,128)(2,1)} %k_ref.1, bf16[256,1024]{1,0:T(8,128)(2,1)} %v_ref.1, bf16[256,1024]{1,0:T(8,128)(2,1)} %q_ref.1), custom_call_target="tpu_custom_call" | custom-call | bytes 6291456 | tf_op jit(solution)/shard_map/pallas_call | solution.py:121
  4.6 3.3 %collective-permute-start = (bf16[384,1024]{1,0:T(8,128)(2,1)}, bf16[384,1024]{1,0:T(8,128)(2,1)S(1)}, u32[]{:S(2)}, u32[]{:S(2)}) collective-permute-start(bf16[384,1024]{1,0:T(8,128)(2,1)} %get-tuple-element.28), channel_id=1, source_target_pairs={{0,4},{4,0},{1,5},{5,1},{2,6},{6,2},{3,7},{7,3},{8,12},{12,8},{9,1... | collective-permute-start | bytes 2359304 | tf_op jit(solution)/shard_map/ppermute | solution.py:43
  8.8 6.5 %all-to-all-start = ((bf16[8,32,1024]{2,1,0:T(8,128)(2,1)}), bf16[8,32,1024]{2,1,0:T(8,128)(2,1)S(1)}, u32[]{:S(2)}, u32[]{:S(2)}) async-start(bf16[8,32,1024]{2,1,0:T(8,128)(2,1)} %broadcast_in_dim.6), calls=%async_computation | async-start | bytes 1048576 | tf_op jit(solution)/shard_map/all_to_all | solution.py:429
  19.0 4.2 %collective-permute-start.1 = (bf16[400,256]{1,0:T(8,128)(2,1)}, bf16[400,256]{1,0:T(8,128)(2,1)}, u32[]{:S(2)}, u32[]{:S(2)}) collective-permute-start(bf16[400,256]{1,0:T(8,128)(2,1)} %get-tuple-element.30), channel_id=1, source_target_pairs={{0,24},{8,32},{16,40},{24,48},{32,56},{40,0},{48,8},{56,16},{1,25}... | collective-permute-start | bytes 614408 | tf_op jit(solution)/shard_map/ppermute | solution.py:35
  23.5 9.8 %all-to-all-done.t_ref = bf16[8,32,1024]{2,1,0:T(8,128)(2,1)S(1)} async-done(((bf16[8,32,1024]{2,1,0:T(8,128)(2,1)}), bf16[8,32,1024]{2,1,0:T(8,128)(2,1)S(1)}, u32[]{:S(2)}, u32[]{:S(2)}) %all-to-all-start) | async-done | bytes 524320 | tf_op jit(solution)/shard_map/all_to_all | solution.py:429
  35.1 3.7 %shard_map.97.refs_5_ = bf16[4,784,256]{2,1,0:T(8,128)(2,1)} custom-call(bf16[256,1024]{1,0:T(8,128)(2,1)} %xk_ref.1, bf16[256,1024]{1,0:T(8,128)(2,1)} %xv_ref.1, s32[2,128]{1,0:T(2,128)} %bitcast.5, bf16[8,32,1024]{2,1,0:T(8,128)(2,1)} %copy-done.16, bf16[400,256]{1,0:T(8,128)(2,1)} %copy-done.5), custom_call_target="tpu_custom_call" | custom-call | bytes 4194304 | tf_op jit(solution)/shard_map/pallas_call | solution.py:147
  38.8 4.2 %all-to-all-start.2 = ((bf16[4,784,256]{2,1,0:T(8,128)(2,1)}), bf16[4,784,256]{2,1,0:T(8,128)(2,1)S(1)}, u32[]{:S(2)}, u32[]{:S(2)}) async-start(bf16[4,784,256]{2,1,0:T(8,128)(2,1)} %shard_map.97.refs_5_), calls=%async_computation.2 | async-start | bytes 3211264 | tf_op jit(solution)/shard_map/all_to_all | solution.py:439
  43.0 5.5 %collective-permute-done.1.refs_1_ = bf16[400,256]{1,0:T(8,128)(2,1)} collective-permute-done((bf16[400,256]{1,0:T(8,128)(2,1)}, bf16[400,256]{1,0:T(8,128)(2,1)}, u32[]{:S(2)}, u32[]{:S(2)}) %collective-permute-start.1) | collective-permute-done | bytes 204832 | tf_op jit(solution)/shard_map/ppermute | solution.py:35
  50.7 2.6 %collective-permute-start.9 = (bf16[5,272,256]{2,1,0:T(8,128)(2,1)S(1)}, bf16[5,272,256]{2,1,0:T(8,128)(2,1)S(1)}, u32[]{:S(2)}, u32[]{:S(2)}) collective-permute-start(bf16[5,272,256]{2,1,0:T(8,128)(2,1)S(1)} %get-tuple-element.34.refs_3_.refs_2_), channel_id=1, source_target_pairs={{0,192},{64,0},{128,64},{192,128},{1,193},{65,1},{129,65},{193,129... | collective-permute-start | bytes 2088968 | tf_op jit(solution)/shard_map/ppermute | solution.py:39
  54.5 3.2 %collective-permute-start.6 = (bf16[400,256]{1,0:T(8,128)(2,1)S(1)}, bf16[400,256]{1,0:T(8,128)(2,1)S(1)}, u32[]{:S(2)}, u32[]{:S(2)}) collective-permute-start(bf16[400,256]{1,0:T(8,128)(2,1)S(1)} %get-tuple-element.36), channel_id=1, source_target_pairs={{0,48},{8,56},{16,0},{24,8},{32,16},{40,24},{48,32},{56,40},{1,49}... | collective-permute-start | bytes 614408 | tf_op jit(solution)/shard_map/ppermute | solution.py:35
  59.7 7.6 %collective-permute-done.5.refs_0_ = bf16[400,256]{1,0:T(8,128)(2,1)S(1)} collective-permute-done((bf16[400,256]{1,0:T(8,128)(2,1)S(1)}, bf16[400,256]{1,0:T(8,128)(2,1)S(1)}, u32[]{:S(2)}, u32[]{:S(2)}) %collective-permute-start.5) | collective-permute-done | bytes 204832 | tf_op jit(solution)/shard_map/ppermute | solution.py:35
  67.3 4.6 %collective-permute-done.7.refs_2_ = bf16[400,256]{1,0:T(8,128)(2,1)S(1)} collective-permute-done((bf16[400,256]{1,0:T(8,128)(2,1)S(1)}, bf16[400,256]{1,0:T(8,128)(2,1)S(1)}, u32[]{:S(2)}, u32[]{:S(2)}) %collective-permute-start.7) | collective-permute-done | bytes 204832 | tf_op jit(solution)/shard_map/ppermute | solution.py:35
  71.9 3.2 %collective-permute-done.9.refs_4_.refs_5_ = bf16[5,272,256]{2,1,0:T(8,128)(2,1)S(1)} collective-permute-done((bf16[5,272,256]{2,1,0:T(8,128)(2,1)S(1)}, bf16[5,272,256]{2,1,0:T(8,128)(2,1)S(1)}, u32[]{:S(2)}, u32[]{:S(2)}) %collective-permute-start.9) | collective-permute-done | bytes 696352 | tf_op jit(solution)/shard_map/ppermute | solution.py:39
  75.1 3.6 %collective-permute-done.8.refs_3_.refs_4_ = bf16[5,272,256]{2,1,0:T(8,128)(2,1)S(1)} collective-permute-done((bf16[5,272,256]{2,1,0:T(8,128)(2,1)S(1)}, bf16[5,272,256]{2,1,0:T(8,128)(2,1)S(1)}, u32[]{:S(2)}, u32[]{:S(2)}) %collective-permute-start.8) | collective-permute-done | bytes 696352 | tf_op jit(solution)/shard_map/ppermute | solution.py:39
  81.6 2.7 %collective-permute-start.11 = (bf16[5,272,256]{2,1,0:T(8,128)(2,1)}, bf16[5,272,256]{2,1,0:T(8,128)(2,1)S(1)}, u32[]{:S(2)}, u32[]{:S(2)}) collective-permute-start(bf16[5,272,256]{2,1,0:T(8,128)(2,1)} %get-tuple-element.41), channel_id=1, source_target_pairs={{0,192},{64,0},{128,64},{192,128},{1,193},{65,1},{129,65},{193,129... | collective-permute-start | bytes 2088968 | tf_op jit(solution)/shard_map/ppermute | solution.py:39
  85.1 3.8 %shard_map.108 = bf16[8,128,384]{2,1,0:T(8,128)(2,1)} custom-call(bf16[8,128,256]{2,1,0:T(8,128)(2,1)S(1)} %shard_map.107.refs_0_, f32[8,8,128]{2,1,0:T(8,128)S(1)} %broadcast_in_dim.15.refs_1_, bf16[4,784,256]{2,1,0:T(8,128)(2,1)S(1)} %all-to-all-done.2.refs_0_.refs_2_), custom_call_target="tpu_custom_call" | custom-call | flops 1073741824 | bytes 4194304 | tf_op jit(solution)/shard_map/pallas_call | solution.py:377
  88.9 5.5 %all-to-all-start.3 = ((bf16[8,128,384]{2,1,0:T(8,128)(2,1)}), bf16[8,128,384]{2,1,0:T(8,128)(2,1)S(1)}, u32[]{:S(2)}, u32[]{:S(2)}) async-start(bf16[8,128,384]{2,1,0:T(8,128)(2,1)} %shard_map.108), calls=%async_computation.3 | async-start | bytes 1572864 | tf_op jit(solution)/shard_map/all_to_all | solution.py:456
  95.5 10.2 %shard_map.101 = (f32[1024,384]{1,0:T(8,128)S(1)}, f32[1024,384]{1,0:T(8,128)S(1)}) custom-call(bf16[8,144,256]{2,1,0:T(8,128)(2,1)} %get-tuple-element.39.refs_0_, bf16[8,144,256]{2,1,0:T(8,128)(2,1)} %collective-permute-done.12.refs_1_.refs_0_, bf16[5,272,256]{2,1,0:T(8,128)(2,1)S(1)} %copy-done.8, bf16[6,272,256]{2,1,0:T(8,128)(2,1)} %get-tuple-element.40.refs_3_.refs_1_, ...), custom_call_target="tpu_custom_call" | custom-call | flops 4831838208 | bytes 4194304 | tf_op jit(solution)/shard_map/pallas_call | solution.py:377
  108.5 8.8 %shard_map.103 = (f32[1024,384]{1,0:T(8,128)S(1)}, f32[1024,384]{1,0:T(8,128)S(1)}) custom-call(bf16[8,144,256]{2,1,0:T(8,128)(2,1)} %get-tuple-element.39.refs_0_, bf16[8,144,256]{2,1,0:T(8,128)(2,1)} %collective-permute-done.12.refs_1_.refs_0_, ...), custom_call_target="tpu_custom_call", output_to_operand_aliasing={{0}: (4, {}), {1}: (5, {})} | custom-call | flops 2952790016 | bytes 4194304 | tf_op jit(solution)/shard_map/pallas_call | solution.py:377
  117.3 3.2 %shard_map.104 = bf16[8,128,384]{2,1,0:T(8,128)(2,1)S(1)} custom-call(bf16[8,144,256]{2,1,0:T(8,128)(2,1)} %collective-permute-done.12.refs_1_.refs_0_, bf16[1,272,256]{2,1,0:T(8,128)(2,1)S(1)} %collective-permute-done.13.refs_1_, bf16[2,272,256]{2,1,0:T(8,128)(2,1)S(1)} %collective-permute-done.14.refs_2_, f32[1024,384]{1,0:T(8,128)S(1)} %get-tuple-element.47.refs_3_), custom_call_target="tpu_custom_call" | custom-call | flops 402653184 | bytes 4194304 | tf_op jit(solution)/shard_map/pallas_call | solution.py:377
  124.2 3.4 %shard_map.105.refs_0_ = bf16[1024,256]{1,0:T(8,128)(2,1)S(1)} custom-call(bf16[8,144,256]{2,1,0:T(8,128)(2,1)} %get-tuple-element.39.refs_0_, bf16[1,272,256]{2,1,0:T(8,128)(2,1)S(1)} %collective-permute-done.13.refs_1_, bf16[2,272,256]{2,1,0:T(8,128)(2,1)S(1)} %collective-permute-done.14.refs_2_, f32[1024,384]{1,0:T(8,128)S(1)} %get-tuple-element.46.refs_3_, ...), custom_call_target="tpu_custom_call" | custom-call | flops 402653184 | bytes 4194304 | tf_op jit(solution)/shard_map/pallas_call | solution.py:377
  129.0 6.9 %all-to-all-start.1 = ((bf16[8,128,256]{2,1,0:T(8,128)(2,1)}), bf16[8,128,256]{2,1,0:T(8,128)(2,1)S(1)}, u32[]{:S(2)}, u32[]{:S(2)}) async-start(bf16[8,128,256]{2,1,0:T(8,128)(2,1)} %shard_map.106.refs_1_), calls=%async_computation.1 | async-start | bytes 1048576 | tf_op jit(solution)/shard_map/all_to_all | solution.py:473
  139.7 2.2 %collective-permute-done.17.refs_3_.refs_2_ = bf16[32,256]{1,0:T(8,128)(2,1)S(1)} collective-permute-done((bf16[32,256]{1,0:T(8,128)(2,1)S(1)}, bf16[32,256]{1,0:T(8,128)(2,1)S(1)}, u32[]{:S(2)}, u32[]{:S(2)}) %collective-permute-start.17) | collective-permute-done | bytes 16416 | tf_op jit(solution)/shard_map/ppermute | solution.py:39
  142.6 11.3 %all-to-all-done.1.refs_0_ = bf16[8,128,256]{2,1,0:T(8,128)(2,1)S(1)} async-done(((bf16[8,128,256]{2,1,0:T(8,128)(2,1)}), bf16[8,128,256]{2,1,0:T(8,128)(2,1)S(1)}, u32[]{:S(2)}, u32[]{:S(2)}) %all-to-all-start.1) | async-done | bytes 524320 | tf_op jit(solution)/shard_map/all_to_all | solution.py:473
  (88 shorter events, 33.4 us)
Async XLA Ops:
  4.6 10.6 %collective-permute-start = (bf16[384,1024]{1,0:T(8,128)(2,1)}, bf16[384,1024]{1,0:T(8,128)(2,1)S(1)}, u32[]{:S(2)}, u32[]{:S(2)}) collective-permute-start(bf16[384,1024]{1,0:T(8,128)(2,1)} %get-tuple-element.28), channel_id=1, source_target_pairs={{0,4},{4,0},{1,5},{5,1},{2,6},{6,2},{3,7},{7,3},{8,12},{12,8},{9,1... | collective-permute-start | bytes 2359304 | tf_op jit(solution)/shard_map/ppermute | solution.py:43
  8.8 24.5 %all-to-all-start = ((bf16[8,32,1024]{2,1,0:T(8,128)(2,1)}), bf16[8,32,1024]{2,1,0:T(8,128)(2,1)S(1)}, u32[]{:S(2)}, u32[]{:S(2)}) async-start(bf16[8,32,1024]{2,1,0:T(8,128)(2,1)} %broadcast_in_dim.6), calls=%async_computation | async-start | bytes 1048576 | tf_op jit(solution)/shard_map/all_to_all | solution.py:429
  17.5 16.8 %collective-permute-start.3 = (bf16[400,256]{1,0:T(8,128)(2,1)S(1)}, bf16[400,256]{1,0:T(8,128)(2,1)S(1)}, u32[]{:S(2)}, u32[]{:S(2)}) collective-permute-start(bf16[400,256]{1,0:T(8,128)(2,1)S(1)} %get-tuple-element.32), channel_id=1, source_target_pairs={{0,8},{8,16},{16,24},{24,32},{32,40},{40,48},{48,56},{56,0},{1,9},... | collective-permute-start | bytes 614408 | tf_op jit(solution)/shard_map/ppermute | solution.py:35
  19.0 29.5 %collective-permute-start.1 = (bf16[400,256]{1,0:T(8,128)(2,1)}, bf16[400,256]{1,0:T(8,128)(2,1)}, u32[]{:S(2)}, u32[]{:S(2)}) collective-permute-start(bf16[400,256]{1,0:T(8,128)(2,1)} %get-tuple-element.30), channel_id=1, source_target_pairs={{0,24},{8,32},{16,40},{24,48},{32,56},{40,0},{48,8},{56,16},{1,25}... | collective-permute-start | bytes 614408 | tf_op jit(solution)/shard_map/ppermute | solution.py:35
  23.2 25.3 %collective-permute-start.2 = (bf16[400,256]{1,0:T(8,128)(2,1)}, bf16[400,256]{1,0:T(8,128)(2,1)}, u32[]{:S(2)}, u32[]{:S(2)}) collective-permute-start(bf16[400,256]{1,0:T(8,128)(2,1)} %get-tuple-element.31), channel_id=1, source_target_pairs={{0,40},{8,48},{16,56},{24,0},{32,8},{40,16},{48,24},{56,32},{1,41}... | collective-permute-start | bytes 614408 | tf_op jit(solution)/shard_map/ppermute | solution.py:35
  23.5 25.0 %collective-permute-start.4 = (bf16[400,256]{1,0:T(8,128)(2,1)}, bf16[400,256]{1,0:T(8,128)(2,1)}, u32[]{:S(2)}, u32[]{:S(2)}) collective-permute-start(bf16[400,256]{1,0:T(8,128)(2,1)} %get-tuple-element.33), channel_id=1, source_target_pairs={{0,56},{8,0},{16,8},{24,16},{32,24},{40,32},{48,40},{56,48},{1,57}... | collective-permute-start | bytes 614408 | tf_op jit(solution)/shard_map/ppermute | solution.py:35
  38.8 45.7 %all-to-all-start.2 = ((bf16[4,784,256]{2,1,0:T(8,128)(2,1)}), bf16[4,784,256]{2,1,0:T(8,128)(2,1)S(1)}, u32[]{:S(2)}, u32[]{:S(2)}) async-start(bf16[4,784,256]{2,1,0:T(8,128)(2,1)} %shard_map.97.refs_5_), calls=%async_computation.2 | async-start | bytes 3211264 | tf_op jit(solution)/shard_map/all_to_all | solution.py:439
  50.7 24.4 %collective-permute-start.9 = (bf16[5,272,256]{2,1,0:T(8,128)(2,1)S(1)}, bf16[5,272,256]{2,1,0:T(8,128)(2,1)S(1)}, u32[]{:S(2)}, u32[]{:S(2)}) collective-permute-start(bf16[5,272,256]{2,1,0:T(8,128)(2,1)S(1)} %get-tuple-element.34.refs_3_.refs_2_), channel_id=1, source_target_pairs={{0,192},{64,0},{128,64},{192,128},{1,193},{65,1},{129,65},{193,129... | collective-permute-start | bytes 2088968 | tf_op jit(solution)/shard_map/ppermute | solution.py:39
  53.2 25.4 %collective-permute-start.8 = (bf16[5,272,256]{2,1,0:T(8,128)(2,1)S(1)}, bf16[5,272,256]{2,1,0:T(8,128)(2,1)S(1)}, u32[]{:S(2)}, u32[]{:S(2)}) collective-permute-start(bf16[5,272,256]{2,1,0:T(8,128)(2,1)S(1)} %get-tuple-element.34.refs_3_.refs_2_), channel_id=1, source_target_pairs={{0,64},{64,128},{128,192},{192,0},{1,65},{65,129},{129,193},{193,1... | collective-permute-start | bytes 2088968 | tf_op jit(solution)/shard_map/ppermute | solution.py:39
  54.0 13.3 %collective-permute-start.5 = (bf16[400,256]{1,0:T(8,128)(2,1)S(1)}, bf16[400,256]{1,0:T(8,128)(2,1)S(1)}, u32[]{:S(2)}, u32[]{:S(2)}) collective-permute-start(bf16[400,256]{1,0:T(8,128)(2,1)S(1)} %get-tuple-element.35), channel_id=1, source_target_pairs={{0,16},{8,24},{16,32},{24,40},{32,48},{40,56},{48,0},{56,8},{1,17}... | collective-permute-start | bytes 614408 | tf_op jit(solution)/shard_map/ppermute | solution.py:35
  54.5 12.8 %collective-permute-start.6 = (bf16[400,256]{1,0:T(8,128)(2,1)S(1)}, bf16[400,256]{1,0:T(8,128)(2,1)S(1)}, u32[]{:S(2)}, u32[]{:S(2)}) collective-permute-start(bf16[400,256]{1,0:T(8,128)(2,1)S(1)} %get-tuple-element.36), channel_id=1, source_target_pairs={{0,48},{8,56},{16,0},{24,8},{32,16},{40,24},{48,32},{56,40},{1,49}... | collective-permute-start | bytes 614408 | tf_op jit(solution)/shard_map/ppermute | solution.py:35
  57.6 14.2 %collective-permute-start.7 = (bf16[400,256]{1,0:T(8,128)(2,1)S(1)}, bf16[400,256]{1,0:T(8,128)(2,1)S(1)}, u32[]{:S(2)}, u32[]{:S(2)}) collective-permute-start(bf16[400,256]{1,0:T(8,128)(2,1)S(1)} %get-tuple-element.37), channel_id=1, source_target_pairs={{0,32},{8,40},{16,48},{24,56},{32,0},{40,8},{48,16},{56,24},{1,33}... | collective-permute-start | bytes 614408 | tf_op jit(solution)/shard_map/ppermute | solution.py:35
  80.7 13.7 %collective-permute-start.12 = (bf16[8,144,256]{2,1,0:T(8,128)(2,1)}, bf16[8,144,256]{2,1,0:T(8,128)(2,1)}, u32[]{:S(2)}, u32[]{:S(2)}) collective-permute-start(bf16[8,144,256]{2,1,0:T(8,128)(2,1)} %get-tuple-element.39.refs_0_), channel_id=1, source_target_pairs={{0,4},{4,0},{1,5},{5,1},{2,6},{6,2},{3,7},{7,3},{8,12},{12,8},{9,1... | collective-permute-start | bytes 1769480 | tf_op jit(solution)/shard_map/ppermute | solution.py:43
  81.6 24.1 %collective-permute-start.10 = (bf16[6,272,256]{2,1,0:T(8,128)(2,1)}, bf16[6,272,256]{2,1,0:T(8,128)(2,1)}, u32[]{:S(2)}, u32[]{:S(2)}) collective-permute-start(bf16[6,272,256]{2,1,0:T(8,128)(2,1)} %get-tuple-element.40.refs_3_.refs_1_), channel_id=1, source_target_pairs={{0,64},{64,128},{128,192},{192,0},{1,65},{65,129},{129,193},{193,1... | collective-permute-start | bytes 2506760 | tf_op jit(solution)/shard_map/ppermute | solution.py:39
  81.6 24.1 %collective-permute-start.11 = (bf16[5,272,256]{2,1,0:T(8,128)(2,1)}, bf16[5,272,256]{2,1,0:T(8,128)(2,1)S(1)}, u32[]{:S(2)}, u32[]{:S(2)}) collective-permute-start(bf16[5,272,256]{2,1,0:T(8,128)(2,1)} %get-tuple-element.41), channel_id=1, source_target_pairs={{0,192},{64,0},{128,64},{192,128},{1,193},{65,1},{129,65},{193,129... | collective-permute-start | bytes 2088968 | tf_op jit(solution)/shard_map/ppermute | solution.py:39
  88.9 40.2 %all-to-all-start.3 = ((bf16[8,128,384]{2,1,0:T(8,128)(2,1)}), bf16[8,128,384]{2,1,0:T(8,128)(2,1)S(1)}, u32[]{:S(2)}, u32[]{:S(2)}) async-start(bf16[8,128,384]{2,1,0:T(8,128)(2,1)} %shard_map.108), calls=%async_computation.3 | async-start | bytes 1572864 | tf_op jit(solution)/shard_map/all_to_all | solution.py:456
  106.9 10.4 %collective-permute-start.14 = (bf16[2,272,256]{2,1,0:T(8,128)(2,1)S(1)}, bf16[2,272,256]{2,1,0:T(8,128)(2,1)S(1)}, u32[]{:S(2)}, u32[]{:S(2)}) collective-permute-start(bf16[2,272,256]{2,1,0:T(8,128)(2,1)S(1)} %get-tuple-element.44), channel_id=1, source_target_pairs={{0,192},{64,0},{128,64},{192,128},{1,193},{65,1},{129,65},{193,129... | collective-permute-start | bytes 835592 | tf_op jit(solution)/shard_map/ppermute | solution.py:39
  107.0 10.3 %collective-permute-start.13 = (bf16[1,272,256]{2,1,0:T(8,128)(2,1)S(1)}, bf16[1,272,256]{2,1,0:T(8,128)(2,1)S(1)}, u32[]{:S(2)}, u32[]{:S(2)}) collective-permute-start(bf16[1,272,256]{2,1,0:T(8,128)(2,1)S(1)} %get-tuple-element.43), channel_id=1, source_target_pairs={{0,64},{64,128},{128,192},{192,0},{1,65},{65,129},{129,193},{193,1... | collective-permute-start | bytes 417800 | tf_op jit(solution)/shard_map/ppermute | solution.py:39
  120.5 3.6 %collective-permute-start.15 = (bf16[8,128,384]{2,1,0:T(8,128)(2,1)S(1)}, bf16[8,128,384]{2,1,0:T(8,128)(2,1)S(1)}, u32[]{:S(2)}, u32[]{:S(2)}) collective-permute-start(bf16[8,128,384]{2,1,0:T(8,128)(2,1)S(1)} %shard_map.104), channel_id=1, source_target_pairs={{0,4},{4,0},{1,5},{5,1},{2,6},{6,2},{3,7},{7,3},{8,12},{12,8},{9,1... | collective-permute-start | bytes 2359304 | tf_op jit(solution)/shard_map/ppermute | solution.py:43
  129.0 24.9 %all-to-all-start.1 = ((bf16[8,128,256]{2,1,0:T(8,128)(2,1)}), bf16[8,128,256]{2,1,0:T(8,128)(2,1)S(1)}, u32[]{:S(2)}, u32[]{:S(2)}) async-start(bf16[8,128,256]{2,1,0:T(8,128)(2,1)} %shard_map.106.refs_1_), calls=%async_computation.1 | async-start | bytes 1048576 | tf_op jit(solution)/shard_map/all_to_all | solution.py:473
  137.0 2.7 %collective-permute-start.16 = (bf16[32,256]{1,0:T(8,128)(2,1)S(1)}, bf16[32,256]{1,0:T(8,128)(2,1)S(1)}, u32[]{:S(2)}, u32[]{:S(2)}) collective-permute-start(bf16[32,256]{1,0:T(8,128)(2,1)S(1)} %get-tuple-element.49), channel_id=1, source_target_pairs={{0,192},{64,0},{128,64},{192,128},{1,193},{65,1},{129,65},{193,129... | collective-permute-start | bytes 49160 | tf_op jit(solution)/shard_map/ppermute | solution.py:39
  138.1 3.8 %collective-permute-start.17 = (bf16[32,256]{1,0:T(8,128)(2,1)S(1)}, bf16[32,256]{1,0:T(8,128)(2,1)S(1)}, u32[]{:S(2)}, u32[]{:S(2)}) collective-permute-start(bf16[32,256]{1,0:T(8,128)(2,1)S(1)} %get-tuple-element.50), channel_id=1, source_target_pairs={{0,64},{64,128},{128,192},{192,0},{1,65},{65,129},{129,193},{193,1... | collective-permute-start | bytes 49160 | tf_op jit(solution)/shard_map/ppermute | solution.py:39
  138.5 4.1 %collective-permute-start.18 = (bf16[32,256]{1,0:T(8,128)(2,1)S(1)}, bf16[32,256]{1,0:T(8,128)(2,1)S(1)}, u32[]{:S(2)}, u32[]{:S(2)}) collective-permute-start(bf16[32,256]{1,0:T(8,128)(2,1)S(1)} %get-tuple-element.51), channel_id=1, source_target_pairs={{0,128},{64,192},{128,0},{192,64},{1,129},{65,193},{129,1},{193,65... | collective-permute-start | bytes 49160 | tf_op jit(solution)/shard_map/ppermute | solution.py:39
  154.5 1.8 %collective-permute-start.19 = (bf16[4,128,256]{2,1,0:T(8,128)(2,1)S(1)}, bf16[4,128,256]{2,1,0:T(8,128)(2,1)S(1)}, u32[]{:S(2)}, u32[]{:S(2)}) collective-permute-start(bf16[4,128,256]{2,1,0:T(8,128)(2,1)S(1)} %shard_map.111), channel_id=1, source_target_pairs={{0,4},{4,0},{1,5},{5,1},{2,6},{6,2},{3,7},{7,3},{8,12},{12,8},{9,1... | collective-permute-start | bytes 786440 | tf_op jit(solution)/shard_map/ppermute | solution.py:43
  (19 other events, 166.3 us)

commit v3 on v2

--- a/solution.py
+++ b/solution.py
@@ -51,6 +51,8 @@
 
 
 def rows_at(start, size, unit):
+    if isinstance(start, int):
+        return pl.ds(start * unit, size)
     return pl.ds(pl.multiple_of(start * unit, unit), size)
 
 
@@ -222,13 +224,6 @@
     ]
 
 
-def plan_back(at, ins, outs):
-    z = at[0]
-    return [
-        (ins[0].at[pl.ds(k * HALF, HALF)], outs[0].at[lax.rem(z + 8 - d, 8)]) for k, d in enumerate(ORDER)
-    ]
-
-
 def plan_cross_back(at, ins, outs):
     x = at[2]
     return [
@@ -264,6 +259,7 @@
 
 def attend_kernel(cross, parts, asks, has_carry, final, partner, *refs):
     refs = list(refs)
+    place_ref = refs.pop(0) if partner else None
     q_refs = [refs.pop(0) for _ in range(asks)]
     id_ref = refs.pop(0) if cross else None
     key_refs = [refs.pop(0) for _ in parts]
@@ -332,7 +328,9 @@
             mine, theirs = jnp.exp(level - both), jnp.exp(other - both)
             share = 1.0 / (mine + theirs)
             summed = (mine * share) * summed + (theirs * share) * theirs_out[:, 0:HEAD_DIM].astype(jnp.float32)
-            out_ref[rows, :] = summed.astype(jnp.bfloat16)
+            for half in (0, 1):
+                to = lax.rem(place_ref[0] + 8 - ORDER[chunk + half], 8)
+                out_ref[to] = summed[half * HALF : half * HALF + HALF].astype(jnp.bfloat16)
         else:
             high = level.astype(jnp.bfloat16).astype(jnp.float32)
             middle = (level - high).astype(jnp.bfloat16).astype(jnp.float32)
@@ -351,7 +349,11 @@
                 step(ask, each * i + sub)
         return 0
 
-    lax.fori_loop(0, 4 // each, body, 0)
+    if partner:
+        for block in range(4):
+            step(0, block)
+    else:
+        lax.fori_loop(0, 4 // each, body, 0)
 
 
 def level_of(lanes):
@@ -359,7 +361,7 @@
     return (lanes[:, 0:1] + lanes[:, 32:33]) + lanes[:, 64:65]
 
 
-def attend(queries, keys, ids=None, carry=(), final=False, other=None):
+def attend(queries, keys, ids=None, carry=(), final=False, other=None, place=None):
     arrays = [array for array, _, _ in keys]
     operands = [*queries] + ([] if ids is None else [ids]) + arrays + [*carry]
     operands += [] if other is None else [other]
@@ -371,15 +373,18 @@
     elif other is None:
         out = shaped(8, HALF, WIDE)
     else:
-        out = shaped(1024, HEAD_DIM)
+        out = shaped(8, HALF, HEAD_DIM)
     parts = tuple((start, count) for _, start, count in keys)
     width = sum(count for _, count in parts) * HALF * (1 if ids is None else 2)
+    specs = [whole()] * len(operands)
+    if other is not None:
+        operands, specs = [place] + operands, [scalars()] + specs
     return pl.pallas_call(
         functools.partial(
             attend_kernel, ids is not None, parts, len(queries), len(carry) > 0, final, other is not None
         ),
         out_shape=[out] * len(queries),
-        in_specs=[whole()] * len(operands),
+        in_specs=specs,
         out_specs=[whole()] * len(queries),
         input_output_aliases=aliases,
         **params(4 * 1024 * len(queries) * width * HEAD_DIM, 4 * MIB, 24),
@@ -440,7 +445,7 @@
     group, ask = local(plan_first, got, [(5, KEYS, HEAD_DIM), (5, ASK, HEAD_DIM)], [heads])
 
 
-    sent = packed(ORDER[5:], [group])
+    sent = packed(ORDER[5:], [got[3]])
     rest = [z_send(chunk, d) for chunk, d in zip(sent, ORDER[5:], strict=True)]
     left, right = x_send(group, 1), x_send(group, 3)
     to_right, to_left, mine = local(
@@ -464,9 +469,8 @@
     carry = attend(queries, [(from_left, 0, 6), (from_right, 0, 5)], carry=carry)
     far_keys = [(far[0], 0, 1), (far[1], 0, 2)]
     (partial,) = attend([theirs], far_keys, carry=carry[1:], final=True)
-    (done,) = attend([mine], far_keys, carry=carry[:1], final=True, other=core_swap(partial))
-
-    (back,) = local(plan_back, [done], [(8, HALF, HEAD_DIM)])
+    (back,) = attend([mine], far_keys, carry=carry[:1], final=True, other=core_swap(partial), place=place)
+
     merged = merge(part)
     blocks = local(plan_cross_back, [merged], [(TGT, HEAD_DIM)] * 4, [back])
     blocks = [x_send(b, -d) if d else b for b, d in zip(blocks, X_ORDER, strict=True)]

time: 158 us -> 158 us (level)
    pallas_call x11 -> x10, Pallas kernels: 12.4 us -> 11 us  [copies(): pl.pallas_call(kernel, out_shape=[shaped(*shape) for shape in outs], in_s...]
where the time goes in v3:
time: 158 us; the launch traced here: 157 us
  waiting for transfers between devices  51.9 us (33%)
  starting transfers between devices  50.4 us (32%)
  Pallas kernels  48.5 us (31%)
  local copies, waits for them, and re-layouts  4.45 us (3%)
    pallas_call x5, Pallas kernels, attend(): pl.pallas_call(functools.partial(attend_kernel, ids is not None, parts, l...  30 us
    ppermute x7, waiting for transfers between devices, z_send(): return lax.ppermute(array, 'z', [(i, (i + shift) % 8) for i in range(8)])  18.9 us
    ppermute x7, starting transfers between devices, z_send(): return lax.ppermute(array, 'z', [(i, (i + shift) % 8) for i in range(8)])  11.6 us
    all_to_all x1, waiting for transfers between devices, per_device(): back = lax.all_to_all(back, 'z', 0, 0, tiled=True)  11.3 us
    pallas_call x10, Pallas kernels, copies(): pl.pallas_call(kernel, out_shape=[shaped(*shape) for shape in outs], in_s...  11 us
    ppermute x9, waiting for transfers between devices, x_send(): return lax.ppermute(array, 'x', [(i, (i + shift) % 4) for i in range(4)])  10.1 us
    all_to_all x1, waiting for transfers between devices, per_device(): spread = lax.all_to_all(spread, 'z', 0, 0, tiled=True)  9.79 us
    ppermute x9, starting transfers between devices, x_send(): return lax.ppermute(array, 'x', [(i, (i + shift) % 4) for i in range(4)])  9.15 us
  transfers between devices with their start and end apart: 24, of which 12 were waited for; matrix products, arithmetic and copies ran while one was open for 1% of the time, Pallas kernels for 28%

profile of v3, /device:TPU:1, one launch (start us, length us, event | category | flops | bytes accessed | tf_op | source)
XLA Modules:
  0.0 156.8 jit_solution(13876909409538625134)
XLA Ops:
  1.3 3.3 %shard_map.95 = (bf16[384,1024]{1,0:T(8,128)(2,1)}, bf16[384,1024]{1,0:T(8,128)(2,1)}) custom-call(s32[3]{0:T(128)} %pad_add_fusion.place_ref.refs_0_, bf16[256,1024]{1,0:T(8,128)(2,1)} %k_ref.1, bf16[256,1024]{1,0:T(8,128)(2,1)} %v_ref.1, bf16[256,1024]{1,0:T(8,128)(2,1)} %q_ref.1), custom_call_target="tpu_custom_call" | custom-call | bytes 6291456 | tf_op jit(solution)/shard_map/pallas_call | solution.py:123
  4.6 3.3 %collective-permute-start = (bf16[384,1024]{1,0:T(8,128)(2,1)}, bf16[384,1024]{1,0:T(8,128)(2,1)S(1)}, u32[]{:S(2)}, u32[]{:S(2)}) collective-permute-start(bf16[384,1024]{1,0:T(8,128)(2,1)} %get-tuple-element.28), channel_id=1, source_target_pairs={{0,4},{4,0},{1,5},{5,1},{2,6},{6,2},{3,7},{7,3},{8,12},{12,8},{9,1... | collective-permute-start | bytes 2359304 | tf_op jit(solution)/shard_map/ppermute | solution.py:43
  8.8 6.5 %all-to-all-start = ((bf16[8,32,1024]{2,1,0:T(8,128)(2,1)}), bf16[8,32,1024]{2,1,0:T(8,128)(2,1)S(1)}, u32[]{:S(2)}, u32[]{:S(2)}) async-start(bf16[8,32,1024]{2,1,0:T(8,128)(2,1)} %broadcast_in_dim.6), calls=%async_computation | async-start | bytes 1048576 | tf_op jit(solution)/shard_map/all_to_all | solution.py:434
  19.0 4.2 %collective-permute-start.5 = (bf16[400,256]{1,0:T(8,128)(2,1)}, bf16[400,256]{1,0:T(8,128)(2,1)}, u32[]{:S(2)}, u32[]{:S(2)}) collective-permute-start(bf16[400,256]{1,0:T(8,128)(2,1)} %get-tuple-element.34), channel_id=1, source_target_pairs={{0,24},{8,32},{16,40},{24,48},{32,56},{40,0},{48,8},{56,16},{1,25}... | collective-permute-start | bytes 614408 | tf_op jit(solution)/shard_map/ppermute | solution.py:35
  23.5 9.8 %all-to-all-done.t_ref = bf16[8,32,1024]{2,1,0:T(8,128)(2,1)S(1)} async-done(((bf16[8,32,1024]{2,1,0:T(8,128)(2,1)}), bf16[8,32,1024]{2,1,0:T(8,128)(2,1)S(1)}, u32[]{:S(2)}, u32[]{:S(2)}) %all-to-all-start) | async-done | bytes 524320 | tf_op jit(solution)/shard_map/all_to_all | solution.py:434
  35.1 3.7 %shard_map.98.refs_5_ = bf16[4,784,256]{2,1,0:T(8,128)(2,1)} custom-call(bf16[256,1024]{1,0:T(8,128)(2,1)} %xk_ref.1, bf16[256,1024]{1,0:T(8,128)(2,1)} %xv_ref.1, s32[2,128]{1,0:T(2,128)} %bitcast.5, bf16[8,32,1024]{2,1,0:T(8,128)(2,1)} %copy-done.16, bf16[400,256]{1,0:T(8,128)(2,1)} %copy-done.5), custom_call_target="tpu_custom_call" | custom-call | bytes 4194304 | tf_op jit(solution)/shard_map/pallas_call | solution.py:149
  38.8 4.2 %all-to-all-start.2 = ((bf16[4,784,256]{2,1,0:T(8,128)(2,1)}), bf16[4,784,256]{2,1,0:T(8,128)(2,1)S(1)}, u32[]{:S(2)}, u32[]{:S(2)}) async-start(bf16[4,784,256]{2,1,0:T(8,128)(2,1)} %shard_map.98.refs_5_), calls=%async_computation.2 | async-start | bytes 3211264 | tf_op jit(solution)/shard_map/all_to_all | solution.py:444
  43.0 5.5 %collective-permute-done.5.refs_1_ = bf16[400,256]{1,0:T(8,128)(2,1)} collective-permute-done((bf16[400,256]{1,0:T(8,128)(2,1)}, bf16[400,256]{1,0:T(8,128)(2,1)}, u32[]{:S(2)}, u32[]{:S(2)}) %collective-permute-start.5) | collective-permute-done | bytes 204832 | tf_op jit(solution)/shard_map/ppermute | solution.py:35
  50.7 2.6 %collective-permute-start.9 = (bf16[5,272,256]{2,1,0:T(8,128)(2,1)S(1)}, bf16[5,272,256]{2,1,0:T(8,128)(2,1)S(1)}, u32[]{:S(2)}, u32[]{:S(2)}) collective-permute-start(bf16[5,272,256]{2,1,0:T(8,128)(2,1)S(1)} %get-tuple-element.37.refs_2_), channel_id=1, source_target_pairs={{0,192},{64,0},{128,64},{192,128},{1,193},{65,1},{129,65},{193,129... | collective-permute-start | bytes 2088968 | tf_op jit(solution)/shard_map/ppermute | solution.py:39
  54.5 3.2 %collective-permute-start.3 = (bf16[400,256]{1,0:T(8,128)(2,1)S(1)}, bf16[400,256]{1,0:T(8,128)(2,1)S(1)}, u32[]{:S(2)}, u32[]{:S(2)}) collective-permute-start(bf16[400,256]{1,0:T(8,128)(2,1)S(1)} %get-tuple-element.31), channel_id=1, source_target_pairs={{0,48},{8,56},{16,0},{24,8},{32,16},{40,24},{48,32},{56,40},{1,49}... | collective-permute-start | bytes 614408 | tf_op jit(solution)/shard_map/ppermute | solution.py:35
  59.7 7.6 %collective-permute-done.2.refs_0_ = bf16[400,256]{1,0:T(8,128)(2,1)S(1)} collective-permute-done((bf16[400,256]{1,0:T(8,128)(2,1)S(1)}, bf16[400,256]{1,0:T(8,128)(2,1)S(1)}, u32[]{:S(2)}, u32[]{:S(2)}) %collective-permute-start.2) | collective-permute-done | bytes 204832 | tf_op jit(solution)/shard_map/ppermute | solution.py:35
  67.2 4.6 %collective-permute-done.4.refs_2_ = bf16[400,256]{1,0:T(8,128)(2,1)S(1)} collective-permute-done((bf16[400,256]{1,0:T(8,128)(2,1)S(1)}, bf16[400,256]{1,0:T(8,128)(2,1)S(1)}, u32[]{:S(2)}, u32[]{:S(2)}) %collective-permute-start.4) | collective-permute-done | bytes 204832 | tf_op jit(solution)/shard_map/ppermute | solution.py:35
  71.9 3.2 %collective-permute-done.9.refs_4_.refs_5_ = bf16[5,272,256]{2,1,0:T(8,128)(2,1)S(1)} collective-permute-done((bf16[5,272,256]{2,1,0:T(8,128)(2,1)S(1)}, bf16[5,272,256]{2,1,0:T(8,128)(2,1)S(1)}, u32[]{:S(2)}, u32[]{:S(2)}) %collective-permute-start.9) | collective-permute-done | bytes 696352 | tf_op jit(solution)/shard_map/ppermute | solution.py:39
  75.1 3.6 %collective-permute-done.8.refs_3_.refs_4_ = bf16[5,272,256]{2,1,0:T(8,128)(2,1)S(1)} collective-permute-done((bf16[5,272,256]{2,1,0:T(8,128)(2,1)S(1)}, bf16[5,272,256]{2,1,0:T(8,128)(2,1)S(1)}, u32[]{:S(2)}, u32[]{:S(2)}) %collective-permute-start.8) | collective-permute-done | bytes 696352 | tf_op jit(solution)/shard_map/ppermute | solution.py:39
  81.6 2.7 %collective-permute-start.11 = (bf16[5,272,256]{2,1,0:T(8,128)(2,1)}, bf16[5,272,256]{2,1,0:T(8,128)(2,1)S(1)}, u32[]{:S(2)}, u32[]{:S(2)}) collective-permute-start(bf16[5,272,256]{2,1,0:T(8,128)(2,1)} %get-tuple-element.41), channel_id=1, source_target_pairs={{0,192},{64,0},{128,64},{192,128},{1,193},{65,1},{129,65},{193,129... | collective-permute-start | bytes 2088968 | tf_op jit(solution)/shard_map/ppermute | solution.py:39
  85.1 3.8 %shard_map.107 = bf16[8,128,384]{2,1,0:T(8,128)(2,1)} custom-call(bf16[8,128,256]{2,1,0:T(8,128)(2,1)S(1)} %shard_map.106.refs_0_, f32[8,8,128]{2,1,0:T(8,128)S(1)} %broadcast_in_dim.15.refs_1_, bf16[4,784,256]{2,1,0:T(8,128)(2,1)S(1)} %all-to-all-done.2.refs_0_.refs_2_), custom_call_target="tpu_custom_call" | custom-call | flops 1073741824 | bytes 4194304 | tf_op jit(solution)/shard_map/pallas_call | solution.py:382
  88.9 5.5 %all-to-all-start.3 = ((bf16[8,128,384]{2,1,0:T(8,128)(2,1)}), bf16[8,128,384]{2,1,0:T(8,128)(2,1)S(1)}, u32[]{:S(2)}, u32[]{:S(2)}) async-start(bf16[8,128,384]{2,1,0:T(8,128)(2,1)} %shard_map.107), calls=%async_computation.3 | async-start | bytes 1572864 | tf_op jit(solution)/shard_map/all_to_all | solution.py:461
  95.5 10.2 %shard_map.101 = (f32[1024,384]{1,0:T(8,128)S(1)}, f32[1024,384]{1,0:T(8,128)S(1)}) custom-call(bf16[8,144,256]{2,1,0:T(8,128)(2,1)} %get-tuple-element.39.refs_0_.refs_1_, bf16[8,144,256]{2,1,0:T(8,128)(2,1)} %collective-permute-done.12.refs_1_.refs_0_, bf16[5,272,256]{2,1,0:T(8,128)(2,1)S(1)} %copy-done.15, ...), custom_call_target="tpu_custom_call" | custom-call | flops 4831838208 | bytes 4194304 | tf_op jit(solution)/shard_map/pallas_call | solution.py:382
  108.5 8.8 %shard_map.103 = (f32[1024,384]{1,0:T(8,128)S(1)}, f32[1024,384]{1,0:T(8,128)S(1)}) custom-call(bf16[8,144,256]{2,1,0:T(8,128)(2,1)} %get-tuple-element.39.refs_0_.refs_1_, bf16[8,144,256]{2,1,0:T(8,128)(2,1)} %collective-permute-done.12.refs_1_.refs_0_, ...), custom_call_target="tpu_custom_call", output_to_operand_aliasing={{0}: (4, {}), {1}: (5, {})} | custom-call | flops 2952790016 | bytes 4194304 | tf_op jit(solution)/shard_map/pallas_call | solution.py:382
  117.3 3.2 %shard_map.104 = bf16[8,128,384]{2,1,0:T(8,128)(2,1)S(1)} custom-call(bf16[8,144,256]{2,1,0:T(8,128)(2,1)} %collective-permute-done.12.refs_1_.refs_0_, bf16[1,272,256]{2,1,0:T(8,128)(2,1)S(1)} %collective-permute-done.13.refs_1_.refs_2_, bf16[2,272,256]{2,1,0:T(8,128)(2,1)S(1)} %collective-permute-done.14.refs_2_.refs_3_, ...), custom_call_target="tpu_custom_call" | custom-call | flops 402653184 | bytes 4194304 | tf_op jit(solution)/shard_map/pallas_call | solution.py:382
  124.2 4.0 %shard_map.105.refs_1_ = bf16[8,128,256]{2,1,0:T(8,128)(2,1)} custom-call(s32[3]{0:T(128)S(1)} %copy-done.11, bf16[8,144,256]{2,1,0:T(8,128)(2,1)} %get-tuple-element.39.refs_0_.refs_1_, bf16[1,272,256]{2,1,0:T(8,128)(2,1)S(1)} %collective-permute-done.13.refs_1_.refs_2_, bf16[2,272,256]{2,1,0:T(8,128)(2,1)S(1)} %collective-permute-done.14.refs_2_.refs_3_, ...), custom_call_target="tpu_custom_call" | custom-call | flops 402653184 | bytes 4194304 | tf_op jit(solution)/shard_map/pallas_call | solution.py:382
  128.2 6.9 %all-to-all-start.1 = ((bf16[8,128,256]{2,1,0:T(8,128)(2,1)}), bf16[8,128,256]{2,1,0:T(8,128)(2,1)S(1)}, u32[]{:S(2)}, u32[]{:S(2)}) async-start(bf16[8,128,256]{2,1,0:T(8,128)(2,1)} %shard_map.105.refs_1_), calls=%async_computation.1 | async-start | bytes 1048576 | tf_op jit(solution)/shard_map/all_to_all | solution.py:477
  138.8 2.2 %collective-permute-done.17.refs_3_.refs_2_ = bf16[32,256]{1,0:T(8,128)(2,1)S(1)} collective-permute-done((bf16[32,256]{1,0:T(8,128)(2,1)S(1)}, bf16[32,256]{1,0:T(8,128)(2,1)S(1)}, u32[]{:S(2)}, u32[]{:S(2)}) %collective-permute-start.17) | collective-permute-done | bytes 16416 | tf_op jit(solution)/shard_map/ppermute | solution.py:39
  141.8 11.3 %all-to-all-done.1.refs_0_ = bf16[8,128,256]{2,1,0:T(8,128)(2,1)S(1)} async-done(((bf16[8,128,256]{2,1,0:T(8,128)(2,1)}), bf16[8,128,256]{2,1,0:T(8,128)(2,1)S(1)}, u32[]{:S(2)}, u32[]{:S(2)}) %all-to-all-start.1) | async-done | bytes 524320 | tf_op jit(solution)/shard_map/all_to_all | solution.py:477
  (87 shorter events, 32.0 us)
Async XLA Ops:
  4.6 10.6 %collective-permute-start = (bf16[384,1024]{1,0:T(8,128)(2,1)}, bf16[384,1024]{1,0:T(8,128)(2,1)S(1)}, u32[]{:S(2)}, u32[]{:S(2)}) collective-permute-start(bf16[384,1024]{1,0:T(8,128)(2,1)} %get-tuple-element.28), channel_id=1, source_target_pairs={{0,4},{4,0},{1,5},{5,1},{2,6},{6,2},{3,7},{7,3},{8,12},{12,8},{9,1... | collective-permute-start | bytes 2359304 | tf_op jit(solution)/shard_map/ppermute | solution.py:43
  8.8 24.5 %all-to-all-start = ((bf16[8,32,1024]{2,1,0:T(8,128)(2,1)}), bf16[8,32,1024]{2,1,0:T(8,128)(2,1)S(1)}, u32[]{:S(2)}, u32[]{:S(2)}) async-start(bf16[8,32,1024]{2,1,0:T(8,128)(2,1)} %broadcast_in_dim.6), calls=%async_computation | async-start | bytes 1048576 | tf_op jit(solution)/shard_map/all_to_all | solution.py:434
  17.5 16.8 %collective-permute-start.1 = (bf16[400,256]{1,0:T(8,128)(2,1)S(1)}, bf16[400,256]{1,0:T(8,128)(2,1)S(1)}, u32[]{:S(2)}, u32[]{:S(2)}) collective-permute-start(bf16[400,256]{1,0:T(8,128)(2,1)S(1)} %get-tuple-element.29), channel_id=1, source_target_pairs={{0,8},{8,16},{16,24},{24,32},{32,40},{40,48},{48,56},{56,0},{1,9},... | collective-permute-start | bytes 614408 | tf_op jit(solution)/shard_map/ppermute | solution.py:35
  19.0 29.5 %collective-permute-start.5 = (bf16[400,256]{1,0:T(8,128)(2,1)}, bf16[400,256]{1,0:T(8,128)(2,1)}, u32[]{:S(2)}, u32[]{:S(2)}) collective-permute-start(bf16[400,256]{1,0:T(8,128)(2,1)} %get-tuple-element.34), channel_id=1, source_target_pairs={{0,24},{8,32},{16,40},{24,48},{32,56},{40,0},{48,8},{56,16},{1,25}... | collective-permute-start | bytes 614408 | tf_op jit(solution)/shard_map/ppermute | solution.py:35
  23.2 25.3 %collective-permute-start.6 = (bf16[400,256]{1,0:T(8,128)(2,1)}, bf16[400,256]{1,0:T(8,128)(2,1)}, u32[]{:S(2)}, u32[]{:S(2)}) collective-permute-start(bf16[400,256]{1,0:T(8,128)(2,1)} %get-tuple-element.35), channel_id=1, source_target_pairs={{0,40},{8,48},{16,56},{24,0},{32,8},{40,16},{48,24},{56,32},{1,41}... | collective-permute-start | bytes 614408 | tf_op jit(solution)/shard_map/ppermute | solution.py:35
  23.5 25.0 %collective-permute-start.7 = (bf16[400,256]{1,0:T(8,128)(2,1)}, bf16[400,256]{1,0:T(8,128)(2,1)}, u32[]{:S(2)}, u32[]{:S(2)}) collective-permute-start(bf16[400,256]{1,0:T(8,128)(2,1)} %get-tuple-element.36), channel_id=1, source_target_pairs={{0,56},{8,0},{16,8},{24,16},{32,24},{40,32},{48,40},{56,48},{1,57}... | collective-permute-start | bytes 614408 | tf_op jit(solution)/shard_map/ppermute | solution.py:35
  38.8 45.7 %all-to-all-start.2 = ((bf16[4,784,256]{2,1,0:T(8,128)(2,1)}), bf16[4,784,256]{2,1,0:T(8,128)(2,1)S(1)}, u32[]{:S(2)}, u32[]{:S(2)}) async-start(bf16[4,784,256]{2,1,0:T(8,128)(2,1)} %shard_map.98.refs_5_), calls=%async_computation.2 | async-start | bytes 3211264 | tf_op jit(solution)/shard_map/all_to_all | solution.py:444
  50.7 24.4 %collective-permute-start.9 = (bf16[5,272,256]{2,1,0:T(8,128)(2,1)S(1)}, bf16[5,272,256]{2,1,0:T(8,128)(2,1)S(1)}, u32[]{:S(2)}, u32[]{:S(2)}) collective-permute-start(bf16[5,272,256]{2,1,0:T(8,128)(2,1)S(1)} %get-tuple-element.37.refs_2_), channel_id=1, source_target_pairs={{0,192},{64,0},{128,64},{192,128},{1,193},{65,1},{129,65},{193,129... | collective-permute-start | bytes 2088968 | tf_op jit(solution)/shard_map/ppermute | solution.py:39
  53.2 25.4 %collective-permute-start.8 = (bf16[5,272,256]{2,1,0:T(8,128)(2,1)S(1)}, bf16[5,272,256]{2,1,0:T(8,128)(2,1)S(1)}, u32[]{:S(2)}, u32[]{:S(2)}) collective-permute-start(bf16[5,272,256]{2,1,0:T(8,128)(2,1)S(1)} %get-tuple-element.37.refs_2_), channel_id=1, source_target_pairs={{0,64},{64,128},{128,192},{192,0},{1,65},{65,129},{129,193},{193,1... | collective-permute-start | bytes 2088968 | tf_op jit(solution)/shard_map/ppermute | solution.py:39
  54.0 13.3 %collective-permute-start.2 = (bf16[400,256]{1,0:T(8,128)(2,1)S(1)}, bf16[400,256]{1,0:T(8,128)(2,1)S(1)}, u32[]{:S(2)}, u32[]{:S(2)}) collective-permute-start(bf16[400,256]{1,0:T(8,128)(2,1)S(1)} %get-tuple-element.30), channel_id=1, source_target_pairs={{0,16},{8,24},{16,32},{24,40},{32,48},{40,56},{48,0},{56,8},{1,17}... | collective-permute-start | bytes 614408 | tf_op jit(solution)/shard_map/ppermute | solution.py:35
  54.5 12.8 %collective-permute-start.3 = (bf16[400,256]{1,0:T(8,128)(2,1)S(1)}, bf16[400,256]{1,0:T(8,128)(2,1)S(1)}, u32[]{:S(2)}, u32[]{:S(2)}) collective-permute-start(bf16[400,256]{1,0:T(8,128)(2,1)S(1)} %get-tuple-element.31), channel_id=1, source_target_pairs={{0,48},{8,56},{16,0},{24,8},{32,16},{40,24},{48,32},{56,40},{1,49}... | collective-permute-start | bytes 614408 | tf_op jit(solution)/shard_map/ppermute | solution.py:35
  57.6 14.2 %collective-permute-start.4 = (bf16[400,256]{1,0:T(8,128)(2,1)S(1)}, bf16[400,256]{1,0:T(8,128)(2,1)S(1)}, u32[]{:S(2)}, u32[]{:S(2)}) collective-permute-start(bf16[400,256]{1,0:T(8,128)(2,1)S(1)} %get-tuple-element.32), channel_id=1, source_target_pairs={{0,32},{8,40},{16,48},{24,56},{32,0},{40,8},{48,16},{56,24},{1,33}... | collective-permute-start | bytes 614408 | tf_op jit(solution)/shard_map/ppermute | solution.py:35
  80.7 13.7 %collective-permute-start.12 = (bf16[8,144,256]{2,1,0:T(8,128)(2,1)}, bf16[8,144,256]{2,1,0:T(8,128)(2,1)}, u32[]{:S(2)}, u32[]{:S(2)}) collective-permute-start(bf16[8,144,256]{2,1,0:T(8,128)(2,1)} %get-tuple-element.39.refs_0_.refs_1_), channel_id=1, source_target_pairs={{0,4},{4,0},{1,5},{5,1},{2,6},{6,2},{3,7},{7,3},{8,12},{12,8},{9,1... | collective-permute-start | bytes 1769480 | tf_op jit(solution)/shard_map/ppermute | solution.py:43
  81.6 24.1 %collective-permute-start.10 = (bf16[6,272,256]{2,1,0:T(8,128)(2,1)}, bf16[6,272,256]{2,1,0:T(8,128)(2,1)}, u32[]{:S(2)}, u32[]{:S(2)}) collective-permute-start(bf16[6,272,256]{2,1,0:T(8,128)(2,1)} %get-tuple-element.40.refs_3_.refs_1_), channel_id=1, source_target_pairs={{0,64},{64,128},{128,192},{192,0},{1,65},{65,129},{129,193},{193,1... | collective-permute-start | bytes 2506760 | tf_op jit(solution)/shard_map/ppermute | solution.py:39
  81.6 24.1 %collective-permute-start.11 = (bf16[5,272,256]{2,1,0:T(8,128)(2,1)}, bf16[5,272,256]{2,1,0:T(8,128)(2,1)S(1)}, u32[]{:S(2)}, u32[]{:S(2)}) collective-permute-start(bf16[5,272,256]{2,1,0:T(8,128)(2,1)} %get-tuple-element.41), channel_id=1, source_target_pairs={{0,192},{64,0},{128,64},{192,128},{1,193},{65,1},{129,65},{193,129... | collective-permute-start | bytes 2088968 | tf_op jit(solution)/shard_map/ppermute | solution.py:39
  88.9 39.3 %all-to-all-start.3 = ((bf16[8,128,384]{2,1,0:T(8,128)(2,1)}), bf16[8,128,384]{2,1,0:T(8,128)(2,1)S(1)}, u32[]{:S(2)}, u32[]{:S(2)}) async-start(bf16[8,128,384]{2,1,0:T(8,128)(2,1)} %shard_map.107), calls=%async_computation.3 | async-start | bytes 1572864 | tf_op jit(solution)/shard_map/all_to_all | solution.py:461
  106.9 10.4 %collective-permute-start.14 = (bf16[2,272,256]{2,1,0:T(8,128)(2,1)S(1)}, bf16[2,272,256]{2,1,0:T(8,128)(2,1)S(1)}, u32[]{:S(2)}, u32[]{:S(2)}) collective-permute-start(bf16[2,272,256]{2,1,0:T(8,128)(2,1)S(1)} %get-tuple-element.44), channel_id=1, source_target_pairs={{0,192},{64,0},{128,64},{192,128},{1,193},{65,1},{129,65},{193,129... | collective-permute-start | bytes 835592 | tf_op jit(solution)/shard_map/ppermute | solution.py:39
  107.0 10.3 %collective-permute-start.13 = (bf16[1,272,256]{2,1,0:T(8,128)(2,1)S(1)}, bf16[1,272,256]{2,1,0:T(8,128)(2,1)S(1)}, u32[]{:S(2)}, u32[]{:S(2)}) collective-permute-start(bf16[1,272,256]{2,1,0:T(8,128)(2,1)S(1)} %get-tuple-element.43), channel_id=1, source_target_pairs={{0,64},{64,128},{128,192},{192,0},{1,65},{65,129},{129,193},{193,1... | collective-permute-start | bytes 417800 | tf_op jit(solution)/shard_map/ppermute | solution.py:39
  120.5 3.6 %collective-permute-start.15 = (bf16[8,128,384]{2,1,0:T(8,128)(2,1)S(1)}, bf16[8,128,384]{2,1,0:T(8,128)(2,1)S(1)}, u32[]{:S(2)}, u32[]{:S(2)}) collective-permute-start(bf16[8,128,384]{2,1,0:T(8,128)(2,1)S(1)} %shard_map.104), channel_id=1, source_target_pairs={{0,4},{4,0},{1,5},{5,1},{2,6},{6,2},{3,7},{7,3},{8,12},{12,8},{9,1... | collective-permute-start | bytes 2359304 | tf_op jit(solution)/shard_map/ppermute | solution.py:43
  128.2 24.9 %all-to-all-start.1 = ((bf16[8,128,256]{2,1,0:T(8,128)(2,1)}), bf16[8,128,256]{2,1,0:T(8,128)(2,1)S(1)}, u32[]{:S(2)}, u32[]{:S(2)}) async-start(bf16[8,128,256]{2,1,0:T(8,128)(2,1)} %shard_map.105.refs_1_), calls=%async_computation.1 | async-start | bytes 1048576 | tf_op jit(solution)/shard_map/all_to_all | solution.py:477
  136.1 2.7 %collective-permute-start.16 = (bf16[32,256]{1,0:T(8,128)(2,1)S(1)}, bf16[32,256]{1,0:T(8,128)(2,1)S(1)}, u32[]{:S(2)}, u32[]{:S(2)}) collective-permute-start(bf16[32,256]{1,0:T(8,128)(2,1)S(1)} %get-tuple-element.49), channel_id=1, source_target_pairs={{0,192},{64,0},{128,64},{192,128},{1,193},{65,1},{129,65},{193,129... | collective-permute-start | bytes 49160 | tf_op jit(solution)/shard_map/ppermute | solution.py:39
  137.2 3.8 %collective-permute-start.17 = (bf16[32,256]{1,0:T(8,128)(2,1)S(1)}, bf16[32,256]{1,0:T(8,128)(2,1)S(1)}, u32[]{:S(2)}, u32[]{:S(2)}) collective-permute-start(bf16[32,256]{1,0:T(8,128)(2,1)S(1)} %get-tuple-element.50), channel_id=1, source_target_pairs={{0,64},{64,128},{128,192},{192,0},{1,65},{65,129},{129,193},{193,1... | collective-permute-start | bytes 49160 | tf_op jit(solution)/shard_map/ppermute | solution.py:39
  137.7 4.1 %collective-permute-start.18 = (bf16[32,256]{1,0:T(8,128)(2,1)S(1)}, bf16[32,256]{1,0:T(8,128)(2,1)S(1)}, u32[]{:S(2)}, u32[]{:S(2)}) collective-permute-start(bf16[32,256]{1,0:T(8,128)(2,1)S(1)} %get-tuple-element.51), channel_id=1, source_target_pairs={{0,128},{64,192},{128,0},{192,64},{1,129},{65,193},{129,1},{193,65... | collective-permute-start | bytes 49160 | tf_op jit(solution)/shard_map/ppermute | solution.py:39
  153.6 1.8 %collective-permute-start.19 = (bf16[4,128,256]{2,1,0:T(8,128)(2,1)S(1)}, bf16[4,128,256]{2,1,0:T(8,128)(2,1)S(1)}, u32[]{:S(2)}, u32[]{:S(2)}) collective-permute-start(bf16[4,128,256]{2,1,0:T(8,128)(2,1)S(1)} %shard_map.110), channel_id=1, source_target_pairs={{0,4},{4,0},{1,5},{5,1},{2,6},{6,2},{3,7},{7,3},{8,12},{12,8},{9,1... | collective-permute-start | bytes 786440 | tf_op jit(solution)/shard_map/ppermute | solution.py:43
  (19 other events, 193.0 us)

commit v4 on v3

--- a/solution.py
+++ b/solution.py
@@ -391,6 +391,33 @@
     )(*operands)
 
 
+def finish_kernel(place_ref, carry_ref, other_ref, out_ref):
+    for chunk in range(8):
+        rows = slice(chunk * HALF, chunk * HALF + HALF)
+        top = carry_ref[rows, HEAD_DIM : HEAD_DIM + 1]
+        total = carry_ref[rows, HEAD_DIM + 64 : HEAD_DIM + 65]
+        some = total > 0.0
+        safe = jnp.where(some, total, 1.0)
+        level = jnp.where(some, top + jnp.log(safe), NEG)
+        other = level_of(other_ref[chunk, :, HEAD_DIM:WIDE])
+        both = jnp.maximum(level, other)
+        mine, theirs = jnp.exp(level - both), jnp.exp(other - both)
+        share = 1.0 / (mine + theirs)
+        summed = (mine * share / safe) * carry_ref[rows, 0:HEAD_DIM]
+        summed += (theirs * share) * other_ref[chunk, :, 0:HEAD_DIM].astype(jnp.float32)
+        out_ref[lax.rem(place_ref[0] + 8 - ORDER[chunk], 8)] = summed.astype(jnp.bfloat16)
+
+
+def finish(place, carry, other):
+    return pl.pallas_call(
+        finish_kernel,
+        out_shape=shaped(8, HALF, HEAD_DIM),
+        in_specs=[scalars(), whole(), whole()],
+        out_specs=whole(),
+        **params(0, 3 * MIB),
+    )(place, carry, other)
+
+
 def merge_kernel(part_ref, out_ref):
     levels = [level_of(part_ref[i, :, HEAD_DIM:WIDE]) for i in range(8)]
     top = functools.reduce(jnp.maximum, levels)
@@ -469,7 +496,8 @@
     carry = attend(queries, [(from_left, 0, 6), (from_right, 0, 5)], carry=carry)
     far_keys = [(far[0], 0, 1), (far[1], 0, 2)]
     (partial,) = attend([theirs], far_keys, carry=carry[1:], final=True)
-    (back,) = attend([mine], far_keys, carry=carry[:1], final=True, other=core_swap(partial), place=place)
+    (last,) = attend([mine], far_keys, carry=carry[:1])
+    back = finish(place, last, core_swap(partial))
 
     merged = merge(part)
     blocks = local(plan_cross_back, [merged], [(TGT, HEAD_DIM)] * 4, [back])

time: 158 us -> 160 us (1.013)
  Pallas kernels: 48.5 us -> 52.6 us
  waiting for transfers between devices: 51.9 us -> 50.1 us
    pallas_call x0 -> x1, Pallas kernels: none -> 4.91 us  [finish(): pl.pallas_call(finish_kernel, out_shape=shaped(8, HALF, HEAD_DIM), in_spe...]
    ppermute x4, waiting for transfers between devices: 1.92 us -> 0.01 us  [core_swap(): return lax.ppermute(array, 'core', [(0, 1), (1, 0)])]
  transfers between devices with their start and end apart: 24 -> 24, of which waited for: 12 -> 11; matrix products, arithmetic and copies ran while one was open for 1% -> 1% of each run, Pallas kernels for 28% -> 30%
where the time goes in v4:
time: 160 us; the launch traced here: 159 us
  Pallas kernels  52.6 us (33%)
  starting transfers between devices  50.4 us (32%)
  waiting for transfers between devices  50.1 us (31%)
  local copies, waits for them, and re-layouts  4.45 us (3%)
    pallas_call x5, Pallas kernels, attend(): pl.pallas_call(functools.partial(attend_kernel, ids is not None, parts, l...  29.2 us
    ppermute x7, waiting for transfers between devices, z_send(): return lax.ppermute(array, 'z', [(i, (i + shift) % 8) for i in range(8)])  18.9 us
    ppermute x7, starting transfers between devices, z_send(): return lax.ppermute(array, 'z', [(i, (i + shift) % 8) for i in range(8)])  11.6 us
    all_to_all x1, waiting for transfers between devices, per_device(): back = lax.all_to_all(back, 'z', 0, 0, tiled=True)  11 us
    pallas_call x10, Pallas kernels, copies(): pl.pallas_call(kernel, out_shape=[shaped(*shape) for shape in outs], in_s...  11 us
    ppermute x9, waiting for transfers between devices, x_send(): return lax.ppermute(array, 'x', [(i, (i + shift) % 4) for i in range(4)])  10.4 us
    all_to_all x1, waiting for transfers between devices, per_device(): spread = lax.all_to_all(spread, 'z', 0, 0, tiled=True)  9.79 us
    ppermute x9, starting transfers between devices, x_send(): return lax.ppermute(array, 'x', [(i, (i + shift) % 4) for i in range(4)])  9.15 us
  transfers between devices with their start and end apart: 24, of which 11 were waited for; matrix products, arithmetic and copies ran while one was open for 1% of the time, Pallas kernels for 30%

profile of v4, /device:TPU:1, one launch (start us, length us, event | category | flops | bytes accessed | tf_op | source)
XLA Modules:
  0.0 159.1 jit_solution(9104186092017918418)
XLA Ops:
  1.3 3.3 %shard_map.95 = (bf16[384,1024]{1,0:T(8,128)(2,1)}, bf16[384,1024]{1,0:T(8,128)(2,1)}) custom-call(s32[3]{0:T(128)} %pad_add_fusion.place_ref, bf16[256,1024]{1,0:T(8,128)(2,1)} %k_ref.1, bf16[256,1024]{1,0:T(8,128)(2,1)} %v_ref.1, bf16[256,1024]{1,0:T(8,128)(2,1)} %q_ref.1), custom_call_target="tpu_custom_call" | custom-call | bytes 6291456 | tf_op jit(solution)/shard_map/pallas_call | solution.py:123
  4.6 3.3 %collective-permute-start = (bf16[384,1024]{1,0:T(8,128)(2,1)}, bf16[384,1024]{1,0:T(8,128)(2,1)S(1)}, u32[]{:S(2)}, u32[]{:S(2)}) collective-permute-start(bf16[384,1024]{1,0:T(8,128)(2,1)} %get-tuple-element.28), channel_id=1, source_target_pairs={{0,4},{4,0},{1,5},{5,1},{2,6},{6,2},{3,7},{7,3},{8,12},{12,8},{9,1... | collective-permute-start | bytes 2359304 | tf_op jit(solution)/shard_map/ppermute | solution.py:43
  8.8 6.5 %all-to-all-start = ((bf16[8,32,1024]{2,1,0:T(8,128)(2,1)}), bf16[8,32,1024]{2,1,0:T(8,128)(2,1)S(1)}, u32[]{:S(2)}, u32[]{:S(2)}) async-start(bf16[8,32,1024]{2,1,0:T(8,128)(2,1)} %broadcast_in_dim.6), calls=%async_computation | async-start | bytes 1048576 | tf_op jit(solution)/shard_map/all_to_all | solution.py:461
  19.0 4.2 %collective-permute-start.5 = (bf16[400,256]{1,0:T(8,128)(2,1)}, bf16[400,256]{1,0:T(8,128)(2,1)}, u32[]{:S(2)}, u32[]{:S(2)}) collective-permute-start(bf16[400,256]{1,0:T(8,128)(2,1)} %get-tuple-element.34), channel_id=1, source_target_pairs={{0,24},{8,32},{16,40},{24,48},{32,56},{40,0},{48,8},{56,16},{1,25}... | collective-permute-start | bytes 614408 | tf_op jit(solution)/shard_map/ppermute | solution.py:35
  23.5 9.8 %all-to-all-done.t_ref = bf16[8,32,1024]{2,1,0:T(8,128)(2,1)S(1)} async-done(((bf16[8,32,1024]{2,1,0:T(8,128)(2,1)}), bf16[8,32,1024]{2,1,0:T(8,128)(2,1)S(1)}, u32[]{:S(2)}, u32[]{:S(2)}) %all-to-all-start) | async-done | bytes 524320 | tf_op jit(solution)/shard_map/all_to_all | solution.py:461
  35.1 3.7 %shard_map.98.refs_5_ = bf16[4,784,256]{2,1,0:T(8,128)(2,1)} custom-call(bf16[256,1024]{1,0:T(8,128)(2,1)} %xk_ref.1, bf16[256,1024]{1,0:T(8,128)(2,1)} %xv_ref.1, s32[2,128]{1,0:T(2,128)} %bitcast.5, bf16[8,32,1024]{2,1,0:T(8,128)(2,1)} %copy-done.16, bf16[400,256]{1,0:T(8,128)(2,1)} %copy-done.5), custom_call_target="tpu_custom_call" | custom-call | bytes 4194304 | tf_op jit(solution)/shard_map/pallas_call | solution.py:149
  38.8 4.2 %all-to-all-start.2 = ((bf16[4,784,256]{2,1,0:T(8,128)(2,1)}), bf16[4,784,256]{2,1,0:T(8,128)(2,1)S(1)}, u32[]{:S(2)}, u32[]{:S(2)}) async-start(bf16[4,784,256]{2,1,0:T(8,128)(2,1)} %shard_map.98.refs_5_), calls=%async_computation.2 | async-start | bytes 3211264 | tf_op jit(solution)/shard_map/all_to_all | solution.py:471
  43.0 5.5 %collective-permute-done.5.refs_1_ = bf16[400,256]{1,0:T(8,128)(2,1)} collective-permute-done((bf16[400,256]{1,0:T(8,128)(2,1)}, bf16[400,256]{1,0:T(8,128)(2,1)}, u32[]{:S(2)}, u32[]{:S(2)}) %collective-permute-start.5) | collective-permute-done | bytes 204832 | tf_op jit(solution)/shard_map/ppermute | solution.py:35
  50.7 2.6 %collective-permute-start.9 = (bf16[5,272,256]{2,1,0:T(8,128)(2,1)S(1)}, bf16[5,272,256]{2,1,0:T(8,128)(2,1)S(1)}, u32[]{:S(2)}, u32[]{:S(2)}) collective-permute-start(bf16[5,272,256]{2,1,0:T(8,128)(2,1)S(1)} %get-tuple-element.37.refs_2_), channel_id=1, source_target_pairs={{0,192},{64,0},{128,64},{192,128},{1,193},{65,1},{129,65},{193,129... | collective-permute-start | bytes 2088968 | tf_op jit(solution)/shard_map/ppermute | solution.py:39
  54.5 3.2 %collective-permute-start.3 = (bf16[400,256]{1,0:T(8,128)(2,1)S(1)}, bf16[400,256]{1,0:T(8,128)(2,1)S(1)}, u32[]{:S(2)}, u32[]{:S(2)}) collective-permute-start(bf16[400,256]{1,0:T(8,128)(2,1)S(1)} %get-tuple-element.31), channel_id=1, source_target_pairs={{0,48},{8,56},{16,0},{24,8},{32,16},{40,24},{48,32},{56,40},{1,49}... | collective-permute-start | bytes 614408 | tf_op jit(solution)/shard_map/ppermute | solution.py:35
  59.7 7.6 %collective-permute-done.2.refs_0_ = bf16[400,256]{1,0:T(8,128)(2,1)S(1)} collective-permute-done((bf16[400,256]{1,0:T(8,128)(2,1)S(1)}, bf16[400,256]{1,0:T(8,128)(2,1)S(1)}, u32[]{:S(2)}, u32[]{:S(2)}) %collective-permute-start.2) | collective-permute-done | bytes 204832 | tf_op jit(solution)/shard_map/ppermute | solution.py:35
  67.2 4.6 %collective-permute-done.4.refs_2_ = bf16[400,256]{1,0:T(8,128)(2,1)S(1)} collective-permute-done((bf16[400,256]{1,0:T(8,128)(2,1)S(1)}, bf16[400,256]{1,0:T(8,128)(2,1)S(1)}, u32[]{:S(2)}, u32[]{:S(2)}) %collective-permute-start.4) | collective-permute-done | bytes 204832 | tf_op jit(solution)/shard_map/ppermute | solution.py:35
  71.9 3.2 %collective-permute-done.9.refs_4_.refs_5_ = bf16[5,272,256]{2,1,0:T(8,128)(2,1)S(1)} collective-permute-done((bf16[5,272,256]{2,1,0:T(8,128)(2,1)S(1)}, bf16[5,272,256]{2,1,0:T(8,128)(2,1)S(1)}, u32[]{:S(2)}, u32[]{:S(2)}) %collective-permute-start.9) | collective-permute-done | bytes 696352 | tf_op jit(solution)/shard_map/ppermute | solution.py:39
  75.1 3.6 %collective-permute-done.8.refs_3_.refs_4_ = bf16[5,272,256]{2,1,0:T(8,128)(2,1)S(1)} collective-permute-done((bf16[5,272,256]{2,1,0:T(8,128)(2,1)S(1)}, bf16[5,272,256]{2,1,0:T(8,128)(2,1)S(1)}, u32[]{:S(2)}, u32[]{:S(2)}) %collective-permute-start.8) | collective-permute-done | bytes 696352 | tf_op jit(solution)/shard_map/ppermute | solution.py:39
  81.6 2.7 %collective-permute-start.11 = (bf16[5,272,256]{2,1,0:T(8,128)(2,1)}, bf16[5,272,256]{2,1,0:T(8,128)(2,1)S(1)}, u32[]{:S(2)}, u32[]{:S(2)}) collective-permute-start(bf16[5,272,256]{2,1,0:T(8,128)(2,1)} %get-tuple-element.41), channel_id=1, source_target_pairs={{0,192},{64,0},{128,64},{192,128},{1,193},{65,1},{129,65},{193,129... | collective-permute-start | bytes 2088968 | tf_op jit(solution)/shard_map/ppermute | solution.py:39
  85.1 3.8 %shard_map.108 = bf16[8,128,384]{2,1,0:T(8,128)(2,1)} custom-call(bf16[8,128,256]{2,1,0:T(8,128)(2,1)S(1)} %shard_map.107.refs_0_, f32[8,8,128]{2,1,0:T(8,128)S(1)} %broadcast_in_dim.15.refs_1_, bf16[4,784,256]{2,1,0:T(8,128)(2,1)S(1)} %all-to-all-done.2.refs_0_.refs_2_), custom_call_target="tpu_custom_call" | custom-call | flops 1073741824 | bytes 4194304 | tf_op jit(solution)/shard_map/pallas_call | solution.py:382
  88.9 5.5 %all-to-all-start.3 = ((bf16[8,128,384]{2,1,0:T(8,128)(2,1)}), bf16[8,128,384]{2,1,0:T(8,128)(2,1)S(1)}, u32[]{:S(2)}, u32[]{:S(2)}) async-start(bf16[8,128,384]{2,1,0:T(8,128)(2,1)} %shard_map.108), calls=%async_computation.3 | async-start | bytes 1572864 | tf_op jit(solution)/shard_map/all_to_all | solution.py:488
  95.5 10.2 %shard_map.101 = (f32[1024,384]{1,0:T(8,128)S(1)}, f32[1024,384]{1,0:T(8,128)S(1)}) custom-call(bf16[8,144,256]{2,1,0:T(8,128)(2,1)} %get-tuple-element.39.refs_0_, bf16[8,144,256]{2,1,0:T(8,128)(2,1)} %collective-permute-done.12.refs_1_.refs_0_, bf16[5,272,256]{2,1,0:T(8,128)(2,1)S(1)} %copy-done.15, ...), custom_call_target="tpu_custom_call" | custom-call | flops 4831838208 | bytes 4194304 | tf_op jit(solution)/shard_map/pallas_call | solution.py:382
  108.5 8.8 %shard_map.103 = (f32[1024,384]{1,0:T(8,128)S(1)}, f32[1024,384]{1,0:T(8,128)S(1)}) custom-call(bf16[8,144,256]{2,1,0:T(8,128)(2,1)} %get-tuple-element.39.refs_0_, bf16[8,144,256]{2,1,0:T(8,128)(2,1)} %collective-permute-done.12.refs_1_.refs_0_, ...), custom_call_target="tpu_custom_call", output_to_operand_aliasing={{0}: (4, {}), {1}: (5, {})} | custom-call | flops 2952790016 | bytes 4194304 | tf_op jit(solution)/shard_map/pallas_call | solution.py:382
  117.3 3.2 %shard_map.105 = bf16[8,128,384]{2,1,0:T(8,128)(2,1)S(1)} custom-call(bf16[8,144,256]{2,1,0:T(8,128)(2,1)} %collective-permute-done.12.refs_1_.refs_0_, bf16[1,272,256]{2,1,0:T(8,128)(2,1)S(1)} %collective-permute-done.13.refs_1_, bf16[2,272,256]{2,1,0:T(8,128)(2,1)S(1)} %collective-permute-done.14.refs_2_, f32[1024,384]{1,0:T(8,128)S(1)} %get-tuple-element.47.refs_3_), custom_call_target="tpu_custom_call" | custom-call | flops 402653184 | bytes 4194304 | tf_op jit(solution)/shard_map/pallas_call | solution.py:382
  122.3 3.2 %shard_map.104.carry_ref = f32[1024,384]{1,0:T(8,128)S(1)} custom-call(bf16[8,144,256]{2,1,0:T(8,128)(2,1)} %get-tuple-element.39.refs_0_, bf16[1,272,256]{2,1,0:T(8,128)(2,1)S(1)} %collective-permute-done.13.refs_1_, bf16[2,272,256]{2,1,0:T(8,128)(2,1)S(1)} %collective-permute-done.14.refs_2_, ...), custom_call_target="tpu_custom_call", output_to_operand_aliasing={{}: (3, {})} | custom-call | flops 402653184 | bytes 4194304 | tf_op jit(solution)/shard_map/pallas_call | solution.py:382
  125.5 4.9 %shard_map.106.refs_1_ = bf16[8,128,256]{2,1,0:T(8,128)(2,1)} custom-call(s32[3]{0:T(128)S(1)} %copy-done.11, f32[1024,384]{1,0:T(8,128)S(1)} %shard_map.104.carry_ref, bf16[8,128,384]{2,1,0:T(8,128)(2,1)S(1)} %collective-permute-done.15.other_ref), custom_call_target="tpu_custom_call" | custom-call | bytes 3145728 | tf_op jit(solution)/shard_map/pallas_call | solution.py:412
  130.4 6.9 %all-to-all-start.1 = ((bf16[8,128,256]{2,1,0:T(8,128)(2,1)}), bf16[8,128,256]{2,1,0:T(8,128)(2,1)S(1)}, u32[]{:S(2)}, u32[]{:S(2)}) async-start(bf16[8,128,256]{2,1,0:T(8,128)(2,1)} %shard_map.106.refs_1_), calls=%async_computation.1 | async-start | bytes 1048576 | tf_op jit(solution)/shard_map/all_to_all | solution.py:505
  144.3 11.0 %all-to-all-done.1.refs_0_ = bf16[8,128,256]{2,1,0:T(8,128)(2,1)S(1)} async-done(((bf16[8,128,256]{2,1,0:T(8,128)(2,1)}), bf16[8,128,256]{2,1,0:T(8,128)(2,1)S(1)}, u32[]{:S(2)}, u32[]{:S(2)}) %all-to-all-start.1) | async-done | bytes 524320 | tf_op jit(solution)/shard_map/all_to_all | solution.py:505
  (88 shorter events, 32.6 us)
Async XLA Ops:
  4.6 10.6 %collective-permute-start = (bf16[384,1024]{1,0:T(8,128)(2,1)}, bf16[384,1024]{1,0:T(8,128)(2,1)S(1)}, u32[]{:S(2)}, u32[]{:S(2)}) collective-permute-start(bf16[384,1024]{1,0:T(8,128)(2,1)} %get-tuple-element.28), channel_id=1, source_target_pairs={{0,4},{4,0},{1,5},{5,1},{2,6},{6,2},{3,7},{7,3},{8,12},{12,8},{9,1... | collective-permute-start | bytes 2359304 | tf_op jit(solution)/shard_map/ppermute | solution.py:43
  8.8 24.5 %all-to-all-start = ((bf16[8,32,1024]{2,1,0:T(8,128)(2,1)}), bf16[8,32,1024]{2,1,0:T(8,128)(2,1)S(1)}, u32[]{:S(2)}, u32[]{:S(2)}) async-start(bf16[8,32,1024]{2,1,0:T(8,128)(2,1)} %broadcast_in_dim.6), calls=%async_computation | async-start | bytes 1048576 | tf_op jit(solution)/shard_map/all_to_all | solution.py:461
  17.5 16.8 %collective-permute-start.1 = (bf16[400,256]{1,0:T(8,128)(2,1)S(1)}, bf16[400,256]{1,0:T(8,128)(2,1)S(1)}, u32[]{:S(2)}, u32[]{:S(2)}) collective-permute-start(bf16[400,256]{1,0:T(8,128)(2,1)S(1)} %get-tuple-element.29), channel_id=1, source_target_pairs={{0,8},{8,16},{16,24},{24,32},{32,40},{40,48},{48,56},{56,0},{1,9},... | collective-permute-start | bytes 614408 | tf_op jit(solution)/shard_map/ppermute | solution.py:35
  19.0 29.5 %collective-permute-start.5 = (bf16[400,256]{1,0:T(8,128)(2,1)}, bf16[400,256]{1,0:T(8,128)(2,1)}, u32[]{:S(2)}, u32[]{:S(2)}) collective-permute-start(bf16[400,256]{1,0:T(8,128)(2,1)} %get-tuple-element.34), channel_id=1, source_target_pairs={{0,24},{8,32},{16,40},{24,48},{32,56},{40,0},{48,8},{56,16},{1,25}... | collective-permute-start | bytes 614408 | tf_op jit(solution)/shard_map/ppermute | solution.py:35
  23.2 25.3 %collective-permute-start.6 = (bf16[400,256]{1,0:T(8,128)(2,1)}, bf16[400,256]{1,0:T(8,128)(2,1)}, u32[]{:S(2)}, u32[]{:S(2)}) collective-permute-start(bf16[400,256]{1,0:T(8,128)(2,1)} %get-tuple-element.35), channel_id=1, source_target_pairs={{0,40},{8,48},{16,56},{24,0},{32,8},{40,16},{48,24},{56,32},{1,41}... | collective-permute-start | bytes 614408 | tf_op jit(solution)/shard_map/ppermute | solution.py:35
  23.5 25.0 %collective-permute-start.7 = (bf16[400,256]{1,0:T(8,128)(2,1)}, bf16[400,256]{1,0:T(8,128)(2,1)}, u32[]{:S(2)}, u32[]{:S(2)}) collective-permute-start(bf16[400,256]{1,0:T(8,128)(2,1)} %get-tuple-element.36), channel_id=1, source_target_pairs={{0,56},{8,0},{16,8},{24,16},{32,24},{40,32},{48,40},{56,48},{1,57}... | collective-permute-start | bytes 614408 | tf_op jit(solution)/shard_map/ppermute | solution.py:35
  38.8 45.7 %all-to-all-start.2 = ((bf16[4,784,256]{2,1,0:T(8,128)(2,1)}), bf16[4,784,256]{2,1,0:T(8,128)(2,1)S(1)}, u32[]{:S(2)}, u32[]{:S(2)}) async-start(bf16[4,784,256]{2,1,0:T(8,128)(2,1)} %shard_map.98.refs_5_), calls=%async_computation.2 | async-start | bytes 3211264 | tf_op jit(solution)/shard_map/all_to_all | solution.py:471
  50.7 24.4 %collective-permute-start.9 = (bf16[5,272,256]{2,1,0:T(8,128)(2,1)S(1)}, bf16[5,272,256]{2,1,0:T(8,128)(2,1)S(1)}, u32[]{:S(2)}, u32[]{:S(2)}) collective-permute-start(bf16[5,272,256]{2,1,0:T(8,128)(2,1)S(1)} %get-tuple-element.37.refs_2_), channel_id=1, source_target_pairs={{0,192},{64,0},{128,64},{192,128},{1,193},{65,1},{129,65},{193,129... | collective-permute-start | bytes 2088968 | tf_op jit(solution)/shard_map/ppermute | solution.py:39
  53.2 25.4 %collective-permute-start.8 = (bf16[5,272,256]{2,1,0:T(8,128)(2,1)S(1)}, bf16[5,272,256]{2,1,0:T(8,128)(2,1)S(1)}, u32[]{:S(2)}, u32[]{:S(2)}) collective-permute-start(bf16[5,272,256]{2,1,0:T(8,128)(2,1)S(1)} %get-tuple-element.37.refs_2_), channel_id=1, source_target_pairs={{0,64},{64,128},{128,192},{192,0},{1,65},{65,129},{129,193},{193,1... | collective-permute-start | bytes 2088968 | tf_op jit(solution)/shard_map/ppermute | solution.py:39
  54.0 13.3 %collective-permute-start.2 = (bf16[400,256]{1,0:T(8,128)(2,1)S(1)}, bf16[400,256]{1,0:T(8,128)(2,1)S(1)}, u32[]{:S(2)}, u32[]{:S(2)}) collective-permute-start(bf16[400,256]{1,0:T(8,128)(2,1)S(1)} %get-tuple-element.30), channel_id=1, source_target_pairs={{0,16},{8,24},{16,32},{24,40},{32,48},{40,56},{48,0},{56,8},{1,17}... | collective-permute-start | bytes 614408 | tf_op jit(solution)/shard_map/ppermute | solution.py:35
  54.5 12.8 %collective-permute-start.3 = (bf16[400,256]{1,0:T(8,128)(2,1)S(1)}, bf16[400,256]{1,0:T(8,128)(2,1)S(1)}, u32[]{:S(2)}, u32[]{:S(2)}) collective-permute-start(bf16[400,256]{1,0:T(8,128)(2,1)S(1)} %get-tuple-element.31), channel_id=1, source_target_pairs={{0,48},{8,56},{16,0},{24,8},{32,16},{40,24},{48,32},{56,40},{1,49}... | collective-permute-start | bytes 614408 | tf_op jit(solution)/shard_map/ppermute | solution.py:35
  57.6 14.2 %collective-permute-start.4 = (bf16[400,256]{1,0:T(8,128)(2,1)S(1)}, bf16[400,256]{1,0:T(8,128)(2,1)S(1)}, u32[]{:S(2)}, u32[]{:S(2)}) collective-permute-start(bf16[400,256]{1,0:T(8,128)(2,1)S(1)} %get-tuple-element.32), channel_id=1, source_target_pairs={{0,32},{8,40},{16,48},{24,56},{32,0},{40,8},{48,16},{56,24},{1,33}... | collective-permute-start | bytes 614408 | tf_op jit(solution)/shard_map/ppermute | solution.py:35
  80.7 13.7 %collective-permute-start.12 = (bf16[8,144,256]{2,1,0:T(8,128)(2,1)}, bf16[8,144,256]{2,1,0:T(8,128)(2,1)}, u32[]{:S(2)}, u32[]{:S(2)}) collective-permute-start(bf16[8,144,256]{2,1,0:T(8,128)(2,1)} %get-tuple-element.39.refs_0_), channel_id=1, source_target_pairs={{0,4},{4,0},{1,5},{5,1},{2,6},{6,2},{3,7},{7,3},{8,12},{12,8},{9,1... | collective-permute-start | bytes 1769480 | tf_op jit(solution)/shard_map/ppermute | solution.py:43
  81.6 24.1 %collective-permute-start.10 = (bf16[6,272,256]{2,1,0:T(8,128)(2,1)}, bf16[6,272,256]{2,1,0:T(8,128)(2,1)}, u32[]{:S(2)}, u32[]{:S(2)}) collective-permute-start(bf16[6,272,256]{2,1,0:T(8,128)(2,1)} %get-tuple-element.40.refs_3_.refs_1_), channel_id=1, source_target_pairs={{0,64},{64,128},{128,192},{192,0},{1,65},{65,129},{129,193},{193,1... | collective-permute-start | bytes 2506760 | tf_op jit(solution)/shard_map/ppermute | solution.py:39
  81.6 24.1 %collective-permute-start.11 = (bf16[5,272,256]{2,1,0:T(8,128)(2,1)}, bf16[5,272,256]{2,1,0:T(8,128)(2,1)S(1)}, u32[]{:S(2)}, u32[]{:S(2)}) collective-permute-start(bf16[5,272,256]{2,1,0:T(8,128)(2,1)} %get-tuple-element.41), channel_id=1, source_target_pairs={{0,192},{64,0},{128,64},{192,128},{1,193},{65,1},{129,65},{193,129... | collective-permute-start | bytes 2088968 | tf_op jit(solution)/shard_map/ppermute | solution.py:39
  88.9 41.6 %all-to-all-start.3 = ((bf16[8,128,384]{2,1,0:T(8,128)(2,1)}), bf16[8,128,384]{2,1,0:T(8,128)(2,1)S(1)}, u32[]{:S(2)}, u32[]{:S(2)}) async-start(bf16[8,128,384]{2,1,0:T(8,128)(2,1)} %shard_map.108), calls=%async_computation.3 | async-start | bytes 1572864 | tf_op jit(solution)/shard_map/all_to_all | solution.py:488
  106.9 10.4 %collective-permute-start.14 = (bf16[2,272,256]{2,1,0:T(8,128)(2,1)S(1)}, bf16[2,272,256]{2,1,0:T(8,128)(2,1)S(1)}, u32[]{:S(2)}, u32[]{:S(2)}) collective-permute-start(bf16[2,272,256]{2,1,0:T(8,128)(2,1)S(1)} %get-tuple-element.44), channel_id=1, source_target_pairs={{0,192},{64,0},{128,64},{192,128},{1,193},{65,1},{129,65},{193,129... | collective-permute-start | bytes 835592 | tf_op jit(solution)/shard_map/ppermute | solution.py:39
  107.0 10.3 %collective-permute-start.13 = (bf16[1,272,256]{2,1,0:T(8,128)(2,1)S(1)}, bf16[1,272,256]{2,1,0:T(8,128)(2,1)S(1)}, u32[]{:S(2)}, u32[]{:S(2)}) collective-permute-start(bf16[1,272,256]{2,1,0:T(8,128)(2,1)S(1)} %get-tuple-element.43), channel_id=1, source_target_pairs={{0,64},{64,128},{128,192},{192,0},{1,65},{65,129},{129,193},{193,1... | collective-permute-start | bytes 417800 | tf_op jit(solution)/shard_map/ppermute | solution.py:39
  120.5 4.9 %collective-permute-start.15 = (bf16[8,128,384]{2,1,0:T(8,128)(2,1)S(1)}, bf16[8,128,384]{2,1,0:T(8,128)(2,1)S(1)}, u32[]{:S(2)}, u32[]{:S(2)}) collective-permute-start(bf16[8,128,384]{2,1,0:T(8,128)(2,1)S(1)} %shard_map.105), channel_id=1, source_target_pairs={{0,4},{4,0},{1,5},{5,1},{2,6},{6,2},{3,7},{7,3},{8,12},{12,8},{9,1... | collective-permute-start | bytes 2359304 | tf_op jit(solution)/shard_map/ppermute | solution.py:43
  130.4 24.9 %all-to-all-start.1 = ((bf16[8,128,256]{2,1,0:T(8,128)(2,1)}), bf16[8,128,256]{2,1,0:T(8,128)(2,1)S(1)}, u32[]{:S(2)}, u32[]{:S(2)}) async-start(bf16[8,128,256]{2,1,0:T(8,128)(2,1)} %shard_map.106.refs_1_), calls=%async_computation.1 | async-start | bytes 1048576 | tf_op jit(solution)/shard_map/all_to_all | solution.py:505
  138.4 3.0 %collective-permute-start.16 = (bf16[32,256]{1,0:T(8,128)(2,1)S(1)}, bf16[32,256]{1,0:T(8,128)(2,1)S(1)}, u32[]{:S(2)}, u32[]{:S(2)}) collective-permute-start(bf16[32,256]{1,0:T(8,128)(2,1)S(1)} %get-tuple-element.49), channel_id=1, source_target_pairs={{0,192},{64,0},{128,64},{192,128},{1,193},{65,1},{129,65},{193,129... | collective-permute-start | bytes 49160 | tf_op jit(solution)/shard_map/ppermute | solution.py:39
  139.5 3.8 %collective-permute-start.17 = (bf16[32,256]{1,0:T(8,128)(2,1)S(1)}, bf16[32,256]{1,0:T(8,128)(2,1)S(1)}, u32[]{:S(2)}, u32[]{:S(2)}) collective-permute-start(bf16[32,256]{1,0:T(8,128)(2,1)S(1)} %get-tuple-element.50), channel_id=1, source_target_pairs={{0,64},{64,128},{128,192},{192,0},{1,65},{65,129},{129,193},{193,1... | collective-permute-start | bytes 49160 | tf_op jit(solution)/shard_map/ppermute | solution.py:39
  139.9 4.4 %collective-permute-start.18 = (bf16[32,256]{1,0:T(8,128)(2,1)S(1)}, bf16[32,256]{1,0:T(8,128)(2,1)S(1)}, u32[]{:S(2)}, u32[]{:S(2)}) collective-permute-start(bf16[32,256]{1,0:T(8,128)(2,1)S(1)} %get-tuple-element.51), channel_id=1, source_target_pairs={{0,128},{64,192},{128,0},{192,64},{1,129},{65,193},{129,1},{193,65... | collective-permute-start | bytes 49160 | tf_op jit(solution)/shard_map/ppermute | solution.py:39
  155.9 1.7 %collective-permute-start.19 = (bf16[4,128,256]{2,1,0:T(8,128)(2,1)S(1)}, bf16[4,128,256]{2,1,0:T(8,128)(2,1)S(1)}, u32[]{:S(2)}, u32[]{:S(2)}) collective-permute-start(bf16[4,128,256]{2,1,0:T(8,128)(2,1)S(1)} %shard_map.111), channel_id=1, source_target_pairs={{0,4},{4,0},{1,5},{5,1},{2,6},{6,2},{3,7},{7,3},{8,12},{12,8},{9,1... | collective-permute-start | bytes 786440 | tf_op jit(solution)/shard_map/ppermute | solution.py:43
  (19 other events, 193.0 us)

commit v5 on v3

--- a/solution.py
+++ b/solution.py
@@ -24,7 +24,7 @@
 X_ID = 4 * HALF
 X_T = X_ID + 16
 X_ROWS = X_T + 8 * TGT
-ORDER = (0, 3, 5, 1, 7, 2, 6, 4)
+ORDER = (0, 2, 6, 1, 7, 3, 5, 4)
 X_ORDER = (0, 1, 3, 2)
 WIDE = HEAD_DIM + 128
 MIB = 1024 * 1024

time: 158 us -> 157 us (level)
  waiting for transfers between devices: 51.9 us -> 47.7 us
  starting transfers between devices: 50.4 us -> 54.2 us
    ppermute x7, waiting for transfers between devices: 18.9 us -> 15.9 us  [z_send(): return lax.ppermute(array, 'z', [(i, (i + shift) % 8) for i in range(8)])]
    ppermute x4, starting transfers between devices: 6.56 us -> 9.1 us  [core_swap(): return lax.ppermute(array, 'core', [(0, 1), (1, 0)])]
    ppermute x9, waiting for transfers between devices: 10.1 us -> 8 us  [x_send(): return lax.ppermute(array, 'x', [(i, (i + shift) % 4) for i in range(4)])]
  transfers between devices with their start and end apart: 24 -> 24, of which waited for: 12 -> 11; matrix products, arithmetic and copies ran while one was open for 1% -> 1% of each run, Pallas kernels for 28% -> 28%
where the time goes in v5:
time: 157 us
  starting transfers between devices  54.2 us (35%)
  Pallas kernels  48.5 us (31%)
  waiting for transfers between devices  47.7 us (30%)
  local copies, waits for them, and re-layouts  4.56 us (3%)
    pallas_call x5, Pallas kernels, attend(): pl.pallas_call(functools.partial(attend_kernel, ids is not None, parts, l...  30 us
    ppermute x7, waiting for transfers between devices, z_send(): return lax.ppermute(array, 'z', [(i, (i + shift) % 8) for i in range(8)])  15.9 us
    ppermute x7, starting transfers between devices, z_send(): return lax.ppermute(array, 'z', [(i, (i + shift) % 8) for i in range(8)])  12.7 us
    all_to_all x1, waiting for transfers between devices, per_device(): back = lax.all_to_all(back, 'z', 0, 0, tiled=True)  11.3 us
    pallas_call x10, Pallas kernels, copies(): pl.pallas_call(kernel, out_shape=[shaped(*shape) for shape in outs], in_s...  11 us
    all_to_all x1, waiting for transfers between devices, per_device(): spread = lax.all_to_all(spread, 'z', 0, 0, tiled=True)  10.7 us
    ppermute x9, starting transfers between devices, x_send(): return lax.ppermute(array, 'x', [(i, (i + shift) % 4) for i in range(4)])  9.44 us
    ppermute x4, starting transfers between devices, core_swap(): return lax.ppermute(array, 'core', [(0, 1), (1, 0)])  9.1 us
  transfers between devices with their start and end apart: 24, of which 11 were waited for; matrix products, arithmetic and copies ran while one was open for 1% of the time, Pallas kernels for 28%

profile of v5, /device:TPU:1, one launch (start us, length us, event | category | flops | bytes accessed | tf_op | source)
XLA Modules:
  0.0 156.5 jit_solution(17592653621338555447)
XLA Ops:
  1.3 3.3 %shard_map.95 = (bf16[384,1024]{1,0:T(8,128)(2,1)}, bf16[384,1024]{1,0:T(8,128)(2,1)}) custom-call(s32[3]{0:T(128)} %pad_add_fusion.place_ref.refs_0_, bf16[256,1024]{1,0:T(8,128)(2,1)} %k_ref.1, bf16[256,1024]{1,0:T(8,128)(2,1)} %v_ref.1, bf16[256,1024]{1,0:T(8,128)(2,1)} %q_ref.1), custom_call_target="tpu_custom_call" | custom-call | bytes 6291456 | tf_op jit(solution)/shard_map/pallas_call | solution.py:123
  4.6 3.3 %collective-permute-start = (bf16[384,1024]{1,0:T(8,128)(2,1)}, bf16[384,1024]{1,0:T(8,128)(2,1)S(1)}, u32[]{:S(2)}, u32[]{:S(2)}) collective-permute-start(bf16[384,1024]{1,0:T(8,128)(2,1)} %get-tuple-element.28), channel_id=1, source_target_pairs={{0,4},{4,0},{1,5},{5,1},{2,6},{6,2},{3,7},{7,3},{8,12},{12,8},{9,1... | collective-permute-start | bytes 2359304 | tf_op jit(solution)/shard_map/ppermute | solution.py:43
  8.8 6.5 %all-to-all-start = ((bf16[8,32,1024]{2,1,0:T(8,128)(2,1)}), bf16[8,32,1024]{2,1,0:T(8,128)(2,1)S(1)}, u32[]{:S(2)}, u32[]{:S(2)}) async-start(bf16[8,32,1024]{2,1,0:T(8,128)(2,1)} %broadcast_in_dim.6), calls=%async_computation | async-start | bytes 1048576 | tf_op jit(solution)/shard_map/all_to_all | solution.py:434
  19.0 2.1 %collective-permute-start.5 = (bf16[400,256]{1,0:T(8,128)(2,1)}, bf16[400,256]{1,0:T(8,128)(2,1)}, u32[]{:S(2)}, u32[]{:S(2)}) collective-permute-start(bf16[400,256]{1,0:T(8,128)(2,1)} %get-tuple-element.34), channel_id=1, source_target_pairs={{0,16},{8,24},{16,32},{24,40},{32,48},{40,56},{48,0},{56,8},{1,17}... | collective-permute-start | bytes 614408 | tf_op jit(solution)/shard_map/ppermute | solution.py:35
  22.6 10.7 %all-to-all-done.t_ref = bf16[8,32,1024]{2,1,0:T(8,128)(2,1)S(1)} async-done(((bf16[8,32,1024]{2,1,0:T(8,128)(2,1)}), bf16[8,32,1024]{2,1,0:T(8,128)(2,1)S(1)}, u32[]{:S(2)}, u32[]{:S(2)}) %all-to-all-start) | async-done | bytes 524320 | tf_op jit(solution)/shard_map/all_to_all | solution.py:434
  35.0 3.7 %shard_map.98.refs_5_ = bf16[4,784,256]{2,1,0:T(8,128)(2,1)} custom-call(bf16[256,1024]{1,0:T(8,128)(2,1)} %xk_ref.1, bf16[256,1024]{1,0:T(8,128)(2,1)} %xv_ref.1, s32[2,128]{1,0:T(2,128)} %bitcast.5, bf16[8,32,1024]{2,1,0:T(8,128)(2,1)} %copy-done.16, bf16[400,256]{1,0:T(8,128)(2,1)} %copy-done.5), custom_call_target="tpu_custom_call" | custom-call | bytes 4194304 | tf_op jit(solution)/shard_map/pallas_call | solution.py:149
  38.7 4.2 %all-to-all-start.2 = ((bf16[4,784,256]{2,1,0:T(8,128)(2,1)}), bf16[4,784,256]{2,1,0:T(8,128)(2,1)S(1)}, u32[]{:S(2)}, u32[]{:S(2)}) async-start(bf16[4,784,256]{2,1,0:T(8,128)(2,1)} %shard_map.98.refs_5_), calls=%async_computation.2 | async-start | bytes 3211264 | tf_op jit(solution)/shard_map/all_to_all | solution.py:444
  45.2 2.8 %collective-permute-start.9 = (bf16[5,272,256]{2,1,0:T(8,128)(2,1)S(1)}, bf16[5,272,256]{2,1,0:T(8,128)(2,1)S(1)}, u32[]{:S(2)}, u32[]{:S(2)}) collective-permute-start(bf16[5,272,256]{2,1,0:T(8,128)(2,1)S(1)} %get-tuple-element.37.refs_2_), channel_id=1, source_target_pairs={{0,192},{64,0},{128,64},{192,128},{1,193},{65,1},{129,65},{193,129... | collective-permute-start | bytes 2088968 | tf_op jit(solution)/shard_map/ppermute | solution.py:39
  48.7 3.0 %collective-permute-start.2 = (bf16[400,256]{1,0:T(8,128)(2,1)S(1)}, bf16[400,256]{1,0:T(8,128)(2,1)S(1)}, u32[]{:S(2)}, u32[]{:S(2)}) collective-permute-start(bf16[400,256]{1,0:T(8,128)(2,1)S(1)} %get-tuple-element.30), channel_id=1, source_target_pairs={{0,24},{8,32},{16,40},{24,48},{32,56},{40,0},{48,8},{56,16},{1,25}... | collective-permute-start | bytes 614408 | tf_op jit(solution)/shard_map/ppermute | solution.py:35
  53.2 3.1 %collective-permute-start.4 = (bf16[400,256]{1,0:T(8,128)(2,1)S(1)}, bf16[400,256]{1,0:T(8,128)(2,1)S(1)}, u32[]{:S(2)}, u32[]{:S(2)}) collective-permute-start(bf16[400,256]{1,0:T(8,128)(2,1)S(1)} %get-tuple-element.32), channel_id=1, source_target_pairs={{0,32},{8,40},{16,48},{24,56},{32,0},{40,8},{48,16},{56,24},{1,33}... | collective-permute-start | bytes 614408 | tf_op jit(solution)/shard_map/ppermute | solution.py:35
  56.3 8.3 %collective-permute-done.2.refs_0_ = bf16[400,256]{1,0:T(8,128)(2,1)S(1)} collective-permute-done((bf16[400,256]{1,0:T(8,128)(2,1)S(1)}, bf16[400,256]{1,0:T(8,128)(2,1)S(1)}, u32[]{:S(2)}, u32[]{:S(2)}) %collective-permute-start.2) | collective-permute-done | bytes 204832 | tf_op jit(solution)/shard_map/ppermute | solution.py:35
  64.7 6.5 %collective-permute-done.4.refs_2_ = bf16[400,256]{1,0:T(8,128)(2,1)S(1)} collective-permute-done((bf16[400,256]{1,0:T(8,128)(2,1)S(1)}, bf16[400,256]{1,0:T(8,128)(2,1)S(1)}, u32[]{:S(2)}, u32[]{:S(2)}) %collective-permute-start.4) | collective-permute-done | bytes 204832 | tf_op jit(solution)/shard_map/ppermute | solution.py:35
  71.2 3.7 %collective-permute-done.9.refs_4_.refs_5_ = bf16[5,272,256]{2,1,0:T(8,128)(2,1)S(1)} collective-permute-done((bf16[5,272,256]{2,1,0:T(8,128)(2,1)S(1)}, bf16[5,272,256]{2,1,0:T(8,128)(2,1)S(1)}, u32[]{:S(2)}, u32[]{:S(2)}) %collective-permute-start.9) | collective-permute-done | bytes 696352 | tf_op jit(solution)/shard_map/ppermute | solution.py:39
  78.0 3.5 %collective-permute-start.12 = (bf16[8,144,256]{2,1,0:T(8,128)(2,1)}, bf16[8,144,256]{2,1,0:T(8,128)(2,1)}, u32[]{:S(2)}, u32[]{:S(2)}) collective-permute-start(bf16[8,144,256]{2,1,0:T(8,128)(2,1)} %get-tuple-element.39.refs_0_.refs_1_), channel_id=1, source_target_pairs={{0,4},{4,0},{1,5},{5,1},{2,6},{6,2},{3,7},{7,3},{8,12},{12,8},{9,1... | collective-permute-start | bytes 1769480 | tf_op jit(solution)/shard_map/ppermute | solution.py:43
  81.5 2.7 %collective-permute-start.11 = (bf16[5,272,256]{2,1,0:T(8,128)(2,1)}, bf16[5,272,256]{2,1,0:T(8,128)(2,1)S(1)}, u32[]{:S(2)}, u32[]{:S(2)}) collective-permute-start(bf16[5,272,256]{2,1,0:T(8,128)(2,1)} %get-tuple-element.41), channel_id=1, source_target_pairs={{0,192},{64,0},{128,64},{192,128},{1,193},{65,1},{129,65},{193,129... | collective-permute-start | bytes 2088968 | tf_op jit(solution)/shard_map/ppermute | solution.py:39
  85.0 3.8 %shard_map.107 = bf16[8,128,384]{2,1,0:T(8,128)(2,1)} custom-call(bf16[8,128,256]{2,1,0:T(8,128)(2,1)S(1)} %shard_map.106.refs_0_, f32[8,8,128]{2,1,0:T(8,128)S(1)} %broadcast_in_dim.15.refs_1_, bf16[4,784,256]{2,1,0:T(8,128)(2,1)S(1)} %all-to-all-done.2.refs_0_.refs_2_), custom_call_target="tpu_custom_call" | custom-call | flops 1073741824 | bytes 4194304 | tf_op jit(solution)/shard_map/pallas_call | solution.py:382
  88.8 5.4 %all-to-all-start.3 = ((bf16[8,128,384]{2,1,0:T(8,128)(2,1)}), bf16[8,128,384]{2,1,0:T(8,128)(2,1)S(1)}, u32[]{:S(2)}, u32[]{:S(2)}) async-start(bf16[8,128,384]{2,1,0:T(8,128)(2,1)} %shard_map.107), calls=%async_computation.3 | async-start | bytes 1572864 | tf_op jit(solution)/shard_map/all_to_all | solution.py:461
  95.3 10.2 %shard_map.101 = (f32[1024,384]{1,0:T(8,128)S(1)}, f32[1024,384]{1,0:T(8,128)S(1)}) custom-call(bf16[8,144,256]{2,1,0:T(8,128)(2,1)} %get-tuple-element.39.refs_0_.refs_1_, bf16[8,144,256]{2,1,0:T(8,128)(2,1)} %collective-permute-done.12.refs_1_.refs_0_, bf16[5,272,256]{2,1,0:T(8,128)(2,1)S(1)} %copy-done.15, ...), custom_call_target="tpu_custom_call" | custom-call | flops 4831838208 | bytes 4194304 | tf_op jit(solution)/shard_map/pallas_call | solution.py:382
  108.2 8.8 %shard_map.103 = (f32[1024,384]{1,0:T(8,128)S(1)}, f32[1024,384]{1,0:T(8,128)S(1)}) custom-call(bf16[8,144,256]{2,1,0:T(8,128)(2,1)} %get-tuple-element.39.refs_0_.refs_1_, bf16[8,144,256]{2,1,0:T(8,128)(2,1)} %collective-permute-done.12.refs_1_.refs_0_, ...), custom_call_target="tpu_custom_call", output_to_operand_aliasing={{0}: (4, {}), {1}: (5, {})} | custom-call | flops 2952790016 | bytes 4194304 | tf_op jit(solution)/shard_map/pallas_call | solution.py:382
  117.1 3.2 %shard_map.104 = bf16[8,128,384]{2,1,0:T(8,128)(2,1)S(1)} custom-call(bf16[8,144,256]{2,1,0:T(8,128)(2,1)} %collective-permute-done.12.refs_1_.refs_0_, bf16[1,272,256]{2,1,0:T(8,128)(2,1)S(1)} %collective-permute-done.13.refs_1_.refs_2_, bf16[2,272,256]{2,1,0:T(8,128)(2,1)S(1)} %collective-permute-done.14.refs_2_.refs_3_, ...), custom_call_target="tpu_custom_call" | custom-call | flops 402653184 | bytes 4194304 | tf_op jit(solution)/shard_map/pallas_call | solution.py:382
  123.9 4.0 %shard_map.105.refs_1_ = bf16[8,128,256]{2,1,0:T(8,128)(2,1)} custom-call(s32[3]{0:T(128)S(1)} %copy-done.11, bf16[8,144,256]{2,1,0:T(8,128)(2,1)} %get-tuple-element.39.refs_0_.refs_1_, bf16[1,272,256]{2,1,0:T(8,128)(2,1)S(1)} %collective-permute-done.13.refs_1_.refs_2_, bf16[2,272,256]{2,1,0:T(8,128)(2,1)S(1)} %collective-permute-done.14.refs_2_.refs_3_, ...), custom_call_target="tpu_custom_call" | custom-call | flops 402653184 | bytes 4194304 | tf_op jit(solution)/shard_map/pallas_call | solution.py:382
  127.9 6.9 %all-to-all-start.1 = ((bf16[8,128,256]{2,1,0:T(8,128)(2,1)}), bf16[8,128,256]{2,1,0:T(8,128)(2,1)S(1)}, u32[]{:S(2)}, u32[]{:S(2)}) async-start(bf16[8,128,256]{2,1,0:T(8,128)(2,1)} %shard_map.105.refs_1_), calls=%async_computation.1 | async-start | bytes 1048576 | tf_op jit(solution)/shard_map/all_to_all | solution.py:477
  138.6 2.3 %collective-permute-done.17.refs_3_.refs_2_ = bf16[32,256]{1,0:T(8,128)(2,1)S(1)} collective-permute-done((bf16[32,256]{1,0:T(8,128)(2,1)S(1)}, bf16[32,256]{1,0:T(8,128)(2,1)S(1)}, u32[]{:S(2)}, u32[]{:S(2)}) %collective-permute-start.17) | collective-permute-done | bytes 16416 | tf_op jit(solution)/shard_map/ppermute | solution.py:39
  141.5 11.3 %all-to-all-done.1.refs_0_ = bf16[8,128,256]{2,1,0:T(8,128)(2,1)S(1)} async-done(((bf16[8,128,256]{2,1,0:T(8,128)(2,1)}), bf16[8,128,256]{2,1,0:T(8,128)(2,1)S(1)}, u32[]{:S(2)}, u32[]{:S(2)}) %all-to-all-start.1) | async-done | bytes 524320 | tf_op jit(solution)/shard_map/all_to_all | solution.py:477
  (87 shorter events, 32.4 us)
Async XLA Ops:
  4.6 10.6 %collective-permute-start = (bf16[384,1024]{1,0:T(8,128)(2,1)}, bf16[384,1024]{1,0:T(8,128)(2,1)S(1)}, u32[]{:S(2)}, u32[]{:S(2)}) collective-permute-start(bf16[384,1024]{1,0:T(8,128)(2,1)} %get-tuple-element.28), channel_id=1, source_target_pairs={{0,4},{4,0},{1,5},{5,1},{2,6},{6,2},{3,7},{7,3},{8,12},{12,8},{9,1... | collective-permute-start | bytes 2359304 | tf_op jit(solution)/shard_map/ppermute | solution.py:43
  8.8 24.5 %all-to-all-start = ((bf16[8,32,1024]{2,1,0:T(8,128)(2,1)}), bf16[8,32,1024]{2,1,0:T(8,128)(2,1)S(1)}, u32[]{:S(2)}, u32[]{:S(2)}) async-start(bf16[8,32,1024]{2,1,0:T(8,128)(2,1)} %broadcast_in_dim.6), calls=%async_computation | async-start | bytes 1048576 | tf_op jit(solution)/shard_map/all_to_all | solution.py:434
  17.5 16.7 %collective-permute-start.1 = (bf16[400,256]{1,0:T(8,128)(2,1)S(1)}, bf16[400,256]{1,0:T(8,128)(2,1)S(1)}, u32[]{:S(2)}, u32[]{:S(2)}) collective-permute-start(bf16[400,256]{1,0:T(8,128)(2,1)S(1)} %get-tuple-element.29), channel_id=1, source_target_pairs={{0,8},{8,16},{16,24},{24,32},{32,40},{40,48},{48,56},{56,0},{1,9},... | collective-permute-start | bytes 614408 | tf_op jit(solution)/shard_map/ppermute | solution.py:35
  19.0 23.9 %collective-permute-start.5 = (bf16[400,256]{1,0:T(8,128)(2,1)}, bf16[400,256]{1,0:T(8,128)(2,1)}, u32[]{:S(2)}, u32[]{:S(2)}) collective-permute-start(bf16[400,256]{1,0:T(8,128)(2,1)} %get-tuple-element.34), channel_id=1, source_target_pairs={{0,16},{8,24},{16,32},{24,40},{32,48},{40,56},{48,0},{56,8},{1,17}... | collective-permute-start | bytes 614408 | tf_op jit(solution)/shard_map/ppermute | solution.py:35
  21.1 21.8 %collective-permute-start.6 = (bf16[400,256]{1,0:T(8,128)(2,1)}, bf16[400,256]{1,0:T(8,128)(2,1)}, u32[]{:S(2)}, u32[]{:S(2)}) collective-permute-start(bf16[400,256]{1,0:T(8,128)(2,1)} %get-tuple-element.35), channel_id=1, source_target_pairs={{0,48},{8,56},{16,0},{24,8},{32,16},{40,24},{48,32},{56,40},{1,49}... | collective-permute-start | bytes 614408 | tf_op jit(solution)/shard_map/ppermute | solution.py:35
  22.6 20.3 %collective-permute-start.7 = (bf16[400,256]{1,0:T(8,128)(2,1)}, bf16[400,256]{1,0:T(8,128)(2,1)}, u32[]{:S(2)}, u32[]{:S(2)}) collective-permute-start(bf16[400,256]{1,0:T(8,128)(2,1)} %get-tuple-element.36), channel_id=1, source_target_pairs={{0,56},{8,0},{16,8},{24,16},{32,24},{40,32},{48,40},{56,48},{1,57}... | collective-permute-start | bytes 614408 | tf_op jit(solution)/shard_map/ppermute | solution.py:35
  38.7 45.7 %all-to-all-start.2 = ((bf16[4,784,256]{2,1,0:T(8,128)(2,1)}), bf16[4,784,256]{2,1,0:T(8,128)(2,1)S(1)}, u32[]{:S(2)}, u32[]{:S(2)}) async-start(bf16[4,784,256]{2,1,0:T(8,128)(2,1)} %shard_map.98.refs_5_), calls=%async_computation.2 | async-start | bytes 3211264 | tf_op jit(solution)/shard_map/all_to_all | solution.py:444
  45.2 29.7 %collective-permute-start.9 = (bf16[5,272,256]{2,1,0:T(8,128)(2,1)S(1)}, bf16[5,272,256]{2,1,0:T(8,128)(2,1)S(1)}, u32[]{:S(2)}, u32[]{:S(2)}) collective-permute-start(bf16[5,272,256]{2,1,0:T(8,128)(2,1)S(1)} %get-tuple-element.37.refs_2_), channel_id=1, source_target_pairs={{0,192},{64,0},{128,64},{192,128},{1,193},{65,1},{129,65},{193,129... | collective-permute-start | bytes 2088968 | tf_op jit(solution)/shard_map/ppermute | solution.py:39
  47.9 28.1 %collective-permute-start.8 = (bf16[5,272,256]{2,1,0:T(8,128)(2,1)S(1)}, bf16[5,272,256]{2,1,0:T(8,128)(2,1)S(1)}, u32[]{:S(2)}, u32[]{:S(2)}) collective-permute-start(bf16[5,272,256]{2,1,0:T(8,128)(2,1)S(1)} %get-tuple-element.37.refs_2_), channel_id=1, source_target_pairs={{0,64},{64,128},{128,192},{192,0},{1,65},{65,129},{129,193},{193,1... | collective-permute-start | bytes 2088968 | tf_op jit(solution)/shard_map/ppermute | solution.py:39
  48.7 16.0 %collective-permute-start.2 = (bf16[400,256]{1,0:T(8,128)(2,1)S(1)}, bf16[400,256]{1,0:T(8,128)(2,1)S(1)}, u32[]{:S(2)}, u32[]{:S(2)}) collective-permute-start(bf16[400,256]{1,0:T(8,128)(2,1)S(1)} %get-tuple-element.30), channel_id=1, source_target_pairs={{0,24},{8,32},{16,40},{24,48},{32,56},{40,0},{48,8},{56,16},{1,25}... | collective-permute-start | bytes 614408 | tf_op jit(solution)/shard_map/ppermute | solution.py:35
  51.7 13.0 %collective-permute-start.3 = (bf16[400,256]{1,0:T(8,128)(2,1)S(1)}, bf16[400,256]{1,0:T(8,128)(2,1)S(1)}, u32[]{:S(2)}, u32[]{:S(2)}) collective-permute-start(bf16[400,256]{1,0:T(8,128)(2,1)S(1)} %get-tuple-element.31), channel_id=1, source_target_pairs={{0,40},{8,48},{16,56},{24,0},{32,8},{40,16},{48,24},{56,32},{1,41}... | collective-permute-start | bytes 614408 | tf_op jit(solution)/shard_map/ppermute | solution.py:35
  53.2 18.0 %collective-permute-start.4 = (bf16[400,256]{1,0:T(8,128)(2,1)S(1)}, bf16[400,256]{1,0:T(8,128)(2,1)S(1)}, u32[]{:S(2)}, u32[]{:S(2)}) collective-permute-start(bf16[400,256]{1,0:T(8,128)(2,1)S(1)} %get-tuple-element.32), channel_id=1, source_target_pairs={{0,32},{8,40},{16,48},{24,56},{32,0},{40,8},{48,16},{56,24},{1,33}... | collective-permute-start | bytes 614408 | tf_op jit(solution)/shard_map/ppermute | solution.py:35
  78.0 16.1 %collective-permute-start.12 = (bf16[8,144,256]{2,1,0:T(8,128)(2,1)}, bf16[8,144,256]{2,1,0:T(8,128)(2,1)}, u32[]{:S(2)}, u32[]{:S(2)}) collective-permute-start(bf16[8,144,256]{2,1,0:T(8,128)(2,1)} %get-tuple-element.39.refs_0_.refs_1_), channel_id=1, source_target_pairs={{0,4},{4,0},{1,5},{5,1},{2,6},{6,2},{3,7},{7,3},{8,12},{12,8},{9,1... | collective-permute-start | bytes 1769480 | tf_op jit(solution)/shard_map/ppermute | solution.py:43
  81.5 24.0 %collective-permute-start.10 = (bf16[6,272,256]{2,1,0:T(8,128)(2,1)}, bf16[6,272,256]{2,1,0:T(8,128)(2,1)}, u32[]{:S(2)}, u32[]{:S(2)}) collective-permute-start(bf16[6,272,256]{2,1,0:T(8,128)(2,1)} %get-tuple-element.40.refs_3_.refs_1_), channel_id=1, source_target_pairs={{0,64},{64,128},{128,192},{192,0},{1,65},{65,129},{129,193},{193,1... | collective-permute-start | bytes 2506760 | tf_op jit(solution)/shard_map/ppermute | solution.py:39
  81.5 23.9 %collective-permute-start.11 = (bf16[5,272,256]{2,1,0:T(8,128)(2,1)}, bf16[5,272,256]{2,1,0:T(8,128)(2,1)S(1)}, u32[]{:S(2)}, u32[]{:S(2)}) collective-permute-start(bf16[5,272,256]{2,1,0:T(8,128)(2,1)} %get-tuple-element.41), channel_id=1, source_target_pairs={{0,192},{64,0},{128,64},{192,128},{1,193},{65,1},{129,65},{193,129... | collective-permute-start | bytes 2088968 | tf_op jit(solution)/shard_map/ppermute | solution.py:39
  88.8 39.1 %all-to-all-start.3 = ((bf16[8,128,384]{2,1,0:T(8,128)(2,1)}), bf16[8,128,384]{2,1,0:T(8,128)(2,1)S(1)}, u32[]{:S(2)}, u32[]{:S(2)}) async-start(bf16[8,128,384]{2,1,0:T(8,128)(2,1)} %shard_map.107), calls=%async_computation.3 | async-start | bytes 1572864 | tf_op jit(solution)/shard_map/all_to_all | solution.py:461
  106.7 10.4 %collective-permute-start.14 = (bf16[2,272,256]{2,1,0:T(8,128)(2,1)S(1)}, bf16[2,272,256]{2,1,0:T(8,128)(2,1)S(1)}, u32[]{:S(2)}, u32[]{:S(2)}) collective-permute-start(bf16[2,272,256]{2,1,0:T(8,128)(2,1)S(1)} %get-tuple-element.44), channel_id=1, source_target_pairs={{0,192},{64,0},{128,64},{192,128},{1,193},{65,1},{129,65},{193,129... | collective-permute-start | bytes 835592 | tf_op jit(solution)/shard_map/ppermute | solution.py:39
  106.8 10.3 %collective-permute-start.13 = (bf16[1,272,256]{2,1,0:T(8,128)(2,1)S(1)}, bf16[1,272,256]{2,1,0:T(8,128)(2,1)S(1)}, u32[]{:S(2)}, u32[]{:S(2)}) collective-permute-start(bf16[1,272,256]{2,1,0:T(8,128)(2,1)S(1)} %get-tuple-element.43), channel_id=1, source_target_pairs={{0,64},{64,128},{128,192},{192,0},{1,65},{65,129},{129,193},{193,1... | collective-permute-start | bytes 417800 | tf_op jit(solution)/shard_map/ppermute | solution.py:39
  120.3 3.6 %collective-permute-start.15 = (bf16[8,128,384]{2,1,0:T(8,128)(2,1)S(1)}, bf16[8,128,384]{2,1,0:T(8,128)(2,1)S(1)}, u32[]{:S(2)}, u32[]{:S(2)}) collective-permute-start(bf16[8,128,384]{2,1,0:T(8,128)(2,1)S(1)} %shard_map.104), channel_id=1, source_target_pairs={{0,4},{4,0},{1,5},{5,1},{2,6},{6,2},{3,7},{7,3},{8,12},{12,8},{9,1... | collective-permute-start | bytes 2359304 | tf_op jit(solution)/shard_map/ppermute | solution.py:43
  127.9 24.9 %all-to-all-start.1 = ((bf16[8,128,256]{2,1,0:T(8,128)(2,1)}), bf16[8,128,256]{2,1,0:T(8,128)(2,1)S(1)}, u32[]{:S(2)}, u32[]{:S(2)}) async-start(bf16[8,128,256]{2,1,0:T(8,128)(2,1)} %shard_map.105.refs_1_), calls=%async_computation.1 | async-start | bytes 1048576 | tf_op jit(solution)/shard_map/all_to_all | solution.py:477
  135.9 2.7 %collective-permute-start.16 = (bf16[32,256]{1,0:T(8,128)(2,1)S(1)}, bf16[32,256]{1,0:T(8,128)(2,1)S(1)}, u32[]{:S(2)}, u32[]{:S(2)}) collective-permute-start(bf16[32,256]{1,0:T(8,128)(2,1)S(1)} %get-tuple-element.49), channel_id=1, source_target_pairs={{0,192},{64,0},{128,64},{192,128},{1,193},{65,1},{129,65},{193,129... | collective-permute-start | bytes 49160 | tf_op jit(solution)/shard_map/ppermute | solution.py:39
  137.1 3.8 %collective-permute-start.17 = (bf16[32,256]{1,0:T(8,128)(2,1)S(1)}, bf16[32,256]{1,0:T(8,128)(2,1)S(1)}, u32[]{:S(2)}, u32[]{:S(2)}) collective-permute-start(bf16[32,256]{1,0:T(8,128)(2,1)S(1)} %get-tuple-element.50), channel_id=1, source_target_pairs={{0,64},{64,128},{128,192},{192,0},{1,65},{65,129},{129,193},{193,1... | collective-permute-start | bytes 49160 | tf_op jit(solution)/shard_map/ppermute | solution.py:39
  137.4 4.1 %collective-permute-start.18 = (bf16[32,256]{1,0:T(8,128)(2,1)S(1)}, bf16[32,256]{1,0:T(8,128)(2,1)S(1)}, u32[]{:S(2)}, u32[]{:S(2)}) collective-permute-start(bf16[32,256]{1,0:T(8,128)(2,1)S(1)} %get-tuple-element.51), channel_id=1, source_target_pairs={{0,128},{64,192},{128,0},{192,64},{1,129},{65,193},{129,1},{193,65... | collective-permute-start | bytes 49160 | tf_op jit(solution)/shard_map/ppermute | solution.py:39
  153.4 1.8 %collective-permute-start.19 = (bf16[4,128,256]{2,1,0:T(8,128)(2,1)S(1)}, bf16[4,128,256]{2,1,0:T(8,128)(2,1)S(1)}, u32[]{:S(2)}, u32[]{:S(2)}) collective-permute-start(bf16[4,128,256]{2,1,0:T(8,128)(2,1)S(1)} %shard_map.110), channel_id=1, source_target_pairs={{0,4},{4,0},{1,5},{5,1},{2,6},{6,2},{3,7},{7,3},{8,12},{12,8},{9,1... | collective-permute-start | bytes 786440 | tf_op jit(solution)/shard_map/ppermute | solution.py:43
  (19 other events, 176.7 us)

commit v6 on v5

--- a/solution.py
+++ b/solution.py
@@ -130,18 +130,17 @@
     )(place, keys, values, query)
 
 
-def load_cross(cross_keys, cross_values, numbers, targets, after):
-    def kernel(xk_ref, xv_ref, id_ref, t_ref, _, heads, sems):
+def load_cross(cross_keys, cross_values, numbers, after):
+    def kernel(xk_ref, xv_ref, id_ref, _, heads, sems):
         made = []
         for j in range(4):
             for ref, row in ((xk_ref, 0), (xv_ref, X_V)):
                 made.append((ref.at[:, columns(j)], heads.at[j, pl.ds(row, 2 * HALF)]))
-            for z in range(8):
-                made.append((t_ref.at[z, :, columns(j)], heads.at[j, pl.ds(X_T + z * TGT, TGT)]))
         made = run(made, sems)
         for j in range(4):
             for half in (0, 1):
                 heads[j, X_ID:X_T, half * HALF : half * HALF + HALF] = named(id_ref, half)
+        heads[:, X_T:X_ROWS, :] = jnp.zeros((4, X_ROWS - X_T, HEAD_DIM), HALF_TYPE)
         for one in made:
             one.wait()
 
@@ -149,11 +148,27 @@
     return pl.pallas_call(
         kernel,
         out_shape=shaped(4, X_ROWS, HEAD_DIM),
-        in_specs=[anywhere, anywhere, whole(), anywhere, anywhere],
+        in_specs=[anywhere, anywhere, whole(), anywhere],
         out_specs=whole(),
-        scratch_shapes=[pltpu.SemaphoreType.DMA((40,))],
+        scratch_shapes=[pltpu.SemaphoreType.DMA((8,))],
         **params(0, 4 * MIB, 56),
-    )(cross_keys, cross_values, numbers, targets, after)
+    )(cross_keys, cross_values, numbers, after)
+
+
+def add_targets(heads, targets, after):
+    def kernel(_, t_ref, __, out):
+        for j in range(4):
+            for z in range(8):
+                out[j, X_T + z * TGT : X_T + (z + 1) * TGT, :] = t_ref[z, :, columns(j)]
+
+    return pl.pallas_call(
+        kernel,
+        out_shape=shaped(4, X_ROWS, HEAD_DIM),
+        in_specs=[whole(), whole(), pl.BlockSpec(memory_space=pl.ANY)],
+        out_specs=whole(),
+        input_output_aliases={0: 0},
+        **params(0, 1 * MIB),
+    )(heads, targets, after)
 
 
 class Either:
@@ -440,7 +455,8 @@
 
     sent = packed(ORDER[:5])
     got = [sent[0]] + [z_send(sent[k], ORDER[k]) for k in range(1, 5)]
-    heads = load_cross(cross_key, cross_value, numbers, spread, got[3])
+    heads = load_cross(cross_key, cross_value, numbers, sent[1])
+    heads = add_targets(heads, spread, got[3])
     cross = lax.all_to_all(heads, "x", 0, 0, tiled=True)
     group, ask = local(plan_first, got, [(5, KEYS, HEAD_DIM), (5, ASK, HEAD_DIM)], [heads])
 

time: 157 us -> 158 us (level)
  local copies, waits for them, and re-layouts: 4.56 us -> 9.1 us
  waiting for transfers between devices: 47.7 us -> 43.2 us
  starting transfers between devices: 54.2 us -> 56.6 us
  Pallas kernels: 48.5 us -> 46.5 us
    ppermute x9, waiting for transfers between devices: 8 us -> 3.13 us  [x_send(): return lax.ppermute(array, 'x', [(i, (i + shift) % 4) for i in range(4)])]
    unnamed x38 -> x36, local copies, waits for them, and re-layouts: 3.54 us -> 8.08 us
    ppermute x7, waiting for transfers between devices: 15.9 us -> 20.3 us  [z_send(): return lax.ppermute(array, 'z', [(i, (i + shift) % 8) for i in range(8)])]
    all_to_all x1, waiting for transfers between devices: 10.7 us -> 8.11 us  [per_device(): spread = lax.all_to_all(spread, 'z', 0, 0, tiled=True)]
    all_to_all x1, starting transfers between devices: 5.39 us -> 7.21 us  [per_device(): part = lax.all_to_all(part, 'z', 0, 0, tiled=True)]
    ppermute x4, starting transfers between devices: 9.1 us -> 7.33 us  [core_swap(): return lax.ppermute(array, 'core', [(0, 1), (1, 0)])]
  transfers between devices with their start and end apart: 24 -> 24, of which waited for: 11 -> 10; matrix products, arithmetic and copies ran while one was open for 1% -> 1% of each run, Pallas kernels for 28% -> 26%
where the time goes in v6:
time: 158 us; the launch traced here: 157 us
  starting transfers between devices  56.6 us (36%)
  Pallas kernels  46.5 us (29%)
  waiting for transfers between devices  43.2 us (27%)
  local copies, waits for them, and re-layouts  9.1 us (6%)
    pallas_call x5, Pallas kernels, attend(): pl.pallas_call(functools.partial(attend_kernel, ids is not None, parts, l...  28.8 us
    ppermute x7, waiting for transfers between devices, z_send(): return lax.ppermute(array, 'z', [(i, (i + shift) % 8) for i in range(8)])  20.3 us
    ppermute x7, starting transfers between devices, z_send(): return lax.ppermute(array, 'z', [(i, (i + shift) % 8) for i in range(8)])  13.8 us
    ppermute x9, starting transfers between devices, x_send(): return lax.ppermute(array, 'x', [(i, (i + shift) % 4) for i in range(4)])  10.9 us
    pallas_call x10, Pallas kernels, copies(): pl.pallas_call(kernel, out_shape=[shaped(*shape) for shape in outs], in_s...  10.7 us
    all_to_all x1, waiting for transfers between devices, per_device(): back = lax.all_to_all(back, 'z', 0, 0, tiled=True)  9.75 us
    all_to_all x1, waiting for transfers between devices, per_device(): spread = lax.all_to_all(spread, 'z', 0, 0, tiled=True)  8.11 us
    unnamed x36, local copies, waits for them, and re-layouts  8.08 us
  transfers between devices with their start and end apart: 24, of which 10 were waited for; matrix products, arithmetic and copies ran while one was open for 1% of the time, Pallas kernels for 26%

profile of v6, /device:TPU:1, one launch (start us, length us, event | category | flops | bytes accessed | tf_op | source)
XLA Modules:
  0.0 157.1 jit_solution(11966163001459516144)
XLA Ops:
  1.3 3.4 %shard_map.95 = (bf16[384,1024]{1,0:T(8,128)(2,1)}, bf16[384,1024]{1,0:T(8,128)(2,1)}) custom-call(s32[3]{0:T(128)} %pad_add_fusion.place_ref.refs_0_, bf16[256,1024]{1,0:T(8,128)(2,1)} %k_ref.1, bf16[256,1024]{1,0:T(8,128)(2,1)} %v_ref.1, bf16[256,1024]{1,0:T(8,128)(2,1)} %q_ref.1), custom_call_target="tpu_custom_call" | custom-call | bytes 6291456 | tf_op jit(solution)/shard_map/pallas_call | solution.py:123
  4.7 3.3 %collective-permute-start = (bf16[384,1024]{1,0:T(8,128)(2,1)}, bf16[384,1024]{1,0:T(8,128)(2,1)S(1)}, u32[]{:S(2)}, u32[]{:S(2)}) collective-permute-start(bf16[384,1024]{1,0:T(8,128)(2,1)} %get-tuple-element.28), channel_id=1, source_target_pairs={{0,4},{4,0},{1,5},{5,1},{2,6},{6,2},{3,7},{7,3},{8,12},{12,8},{9,1... | collective-permute-start | bytes 2359304 | tf_op jit(solution)/shard_map/ppermute | solution.py:43
  8.9 6.5 %all-to-all-start = ((bf16[8,32,1024]{2,1,0:T(8,128)(2,1)}), bf16[8,32,1024]{2,1,0:T(8,128)(2,1)S(1)}, u32[]{:S(2)}, u32[]{:S(2)}) async-start(bf16[8,32,1024]{2,1,0:T(8,128)(2,1)} %broadcast_in_dim.6), calls=%async_computation | async-start | bytes 1048576 | tf_op jit(solution)/shard_map/all_to_all | solution.py:449
  18.4 2.4 %collective-permute-start.6 = (bf16[400,256]{1,0:T(8,128)(2,1)}, bf16[400,256]{1,0:T(8,128)(2,1)}, u32[]{:S(2)}, u32[]{:S(2)}) collective-permute-start(bf16[400,256]{1,0:T(8,128)(2,1)} %get-tuple-element.35), channel_id=1, source_target_pairs={{0,48},{8,56},{16,0},{24,8},{32,16},{40,24},{48,32},{56,40},{1,49}... | collective-permute-start | bytes 614408 | tf_op jit(solution)/shard_map/ppermute | solution.py:35
  22.0 3.2 %shard_map.98._ = bf16[4,784,256]{2,1,0:T(8,128)(2,1)} custom-call(bf16[256,1024]{1,0:T(8,128)(2,1)} %xk_ref.1, bf16[256,1024]{1,0:T(8,128)(2,1)} %xv_ref.1, s32[2,128]{1,0:T(2,128)} %bitcast.5, bf16[400,256]{1,0:T(8,128)(2,1)} %get-tuple-element.34._), custom_call_target="tpu_custom_call" | custom-call | bytes 4194304 | tf_op jit(solution)/shard_map/pallas_call | solution.py:148
  25.2 8.1 %all-to-all-done.t_ref = bf16[8,32,1024]{2,1,0:T(8,128)(2,1)S(1)} async-done(((bf16[8,32,1024]{2,1,0:T(8,128)(2,1)}), bf16[8,32,1024]{2,1,0:T(8,128)(2,1)S(1)}, u32[]{:S(2)}, u32[]{:S(2)}) %all-to-all-start) | async-done | bytes 524320 | tf_op jit(solution)/shard_map/all_to_all | solution.py:449
  37.0 4.0 %all-to-all-start.2 = ((bf16[4,784,256]{2,1,0:T(8,128)(2,1)}), bf16[4,784,256]{2,1,0:T(8,128)(2,1)S(1)}, u32[]{:S(2)}, u32[]{:S(2)}) async-start(bf16[4,784,256]{2,1,0:T(8,128)(2,1)} %copy-done.1), calls=%async_computation.2 | async-start | bytes 3211264 | tf_op jit(solution)/shard_map/all_to_all | solution.py:460
  45.6 2.6 %collective-permute-start.9 = (bf16[5,272,256]{2,1,0:T(8,128)(2,1)S(1)}, bf16[5,272,256]{2,1,0:T(8,128)(2,1)S(1)}, u32[]{:S(2)}, u32[]{:S(2)}) collective-permute-start(bf16[5,272,256]{2,1,0:T(8,128)(2,1)S(1)} %get-tuple-element.37.refs_2_), channel_id=1, source_target_pairs={{0,192},{64,0},{128,64},{192,128},{1,193},{65,1},{129,65},{193,129... | collective-permute-start | bytes 2088968 | tf_op jit(solution)/shard_map/ppermute | solution.py:39
  48.9 4.3 %collective-permute-start.2 = (bf16[400,256]{1,0:T(8,128)(2,1)S(1)}, bf16[400,256]{1,0:T(8,128)(2,1)S(1)}, u32[]{:S(2)}, u32[]{:S(2)}) collective-permute-start(bf16[400,256]{1,0:T(8,128)(2,1)S(1)} %get-tuple-element.30), channel_id=1, source_target_pairs={{0,24},{8,32},{16,40},{24,48},{32,56},{40,0},{48,8},{56,16},{1,25}... | collective-permute-start | bytes 614408 | tf_op jit(solution)/shard_map/ppermute | solution.py:35
  53.4 4.2 %collective-permute-start.4 = (bf16[400,256]{1,0:T(8,128)(2,1)S(1)}, bf16[400,256]{1,0:T(8,128)(2,1)S(1)}, u32[]{:S(2)}, u32[]{:S(2)}) collective-permute-start(bf16[400,256]{1,0:T(8,128)(2,1)S(1)} %get-tuple-element.32), channel_id=1, source_target_pairs={{0,32},{8,40},{16,48},{24,56},{32,0},{40,8},{48,16},{56,24},{1,33}... | collective-permute-start | bytes 614408 | tf_op jit(solution)/shard_map/ppermute | solution.py:35
  57.6 4.6 %collective-permute-done.2.refs_0_ = bf16[400,256]{1,0:T(8,128)(2,1)S(1)} collective-permute-done((bf16[400,256]{1,0:T(8,128)(2,1)S(1)}, bf16[400,256]{1,0:T(8,128)(2,1)S(1)}, u32[]{:S(2)}, u32[]{:S(2)}) %collective-permute-start.2) | collective-permute-done | bytes 204832 | tf_op jit(solution)/shard_map/ppermute | solution.py:35
  62.3 5.1 %collective-permute-done.3.refs_1_ = bf16[400,256]{1,0:T(8,128)(2,1)S(1)} collective-permute-done((bf16[400,256]{1,0:T(8,128)(2,1)S(1)}, bf16[400,256]{1,0:T(8,128)(2,1)S(1)}, u32[]{:S(2)}, u32[]{:S(2)}) %collective-permute-start.3) | collective-permute-done | bytes 204832 | tf_op jit(solution)/shard_map/ppermute | solution.py:35
  67.4 8.6 %collective-permute-done.4.refs_2_ = bf16[400,256]{1,0:T(8,128)(2,1)S(1)} collective-permute-done((bf16[400,256]{1,0:T(8,128)(2,1)S(1)}, bf16[400,256]{1,0:T(8,128)(2,1)S(1)}, u32[]{:S(2)}, u32[]{:S(2)}) %collective-permute-start.4) | collective-permute-done | bytes 204832 | tf_op jit(solution)/shard_map/ppermute | solution.py:35
  79.7 2.5 %collective-permute-start.11 = (bf16[5,272,256]{2,1,0:T(8,128)(2,1)}, bf16[5,272,256]{2,1,0:T(8,128)(2,1)}, u32[]{:S(2)}, u32[]{:S(2)}) collective-permute-start(bf16[5,272,256]{2,1,0:T(8,128)(2,1)} %get-tuple-element.41), channel_id=1, source_target_pairs={{0,192},{64,0},{128,64},{192,128},{1,193},{65,1},{129,65},{193,129... | collective-permute-start | bytes 2088968 | tf_op jit(solution)/shard_map/ppermute | solution.py:39
  83.0 2.9 %shard_map.108 = bf16[8,128,384]{2,1,0:T(8,128)(2,1)S(1)} custom-call(bf16[8,128,256]{2,1,0:T(8,128)(2,1)S(1)} %shard_map.107.refs_0_, f32[8,8,128]{2,1,0:T(8,128)S(1)} %broadcast_in_dim.15.refs_1_, bf16[4,784,256]{2,1,0:T(8,128)(2,1)S(1)} %all-to-all-done.2.refs_0_.refs_2_), custom_call_target="tpu_custom_call" | custom-call | flops 1073741824 | bytes 4194304 | tf_op jit(solution)/shard_map/pallas_call | solution.py:397
  86.7 7.2 %all-to-all-start.3 = ((bf16[8,128,384]{2,1,0:T(8,128)(2,1)}), bf16[8,128,384]{2,1,0:T(8,128)(2,1)S(1)}, u32[]{:S(2)}, u32[]{:S(2)}) async-start(bf16[8,128,384]{2,1,0:T(8,128)(2,1)} %copy-done.4), calls=%async_computation.3 | async-start | bytes 1572864 | tf_op jit(solution)/shard_map/all_to_all | solution.py:477
  96.2 9.9 %shard_map.102 = (f32[1024,384]{1,0:T(8,128)S(1)}, f32[1024,384]{1,0:T(8,128)S(1)}) custom-call(bf16[8,144,256]{2,1,0:T(8,128)(2,1)} %get-tuple-element.39.refs_0_.refs_1_, bf16[8,144,256]{2,1,0:T(8,128)(2,1)} %collective-permute-done.12.refs_1_.refs_0_, bf16[5,272,256]{2,1,0:T(8,128)(2,1)S(1)} %copy-done.15, ...), custom_call_target="tpu_custom_call" | custom-call | flops 4831838208 | bytes 4194304 | tf_op jit(solution)/shard_map/pallas_call | solution.py:397
  108.8 8.8 %shard_map.104 = (f32[1024,384]{1,0:T(8,128)S(1)}, f32[1024,384]{1,0:T(8,128)S(1)}) custom-call(bf16[8,144,256]{2,1,0:T(8,128)(2,1)} %get-tuple-element.39.refs_0_.refs_1_, bf16[8,144,256]{2,1,0:T(8,128)(2,1)} %collective-permute-done.12.refs_1_.refs_0_, ...), custom_call_target="tpu_custom_call", output_to_operand_aliasing={{0}: (4, {}), {1}: (5, {})} | custom-call | flops 2952790016 | bytes 4194304 | tf_op jit(solution)/shard_map/pallas_call | solution.py:397
  117.6 3.2 %shard_map.105 = bf16[8,128,384]{2,1,0:T(8,128)(2,1)S(1)} custom-call(bf16[8,144,256]{2,1,0:T(8,128)(2,1)} %collective-permute-done.12.refs_1_.refs_0_, bf16[1,272,256]{2,1,0:T(8,128)(2,1)S(1)} %collective-permute-done.13.refs_1_.refs_2_, bf16[2,272,256]{2,1,0:T(8,128)(2,1)S(1)} %collective-permute-done.14.refs_2_.refs_3_, ...), custom_call_target="tpu_custom_call" | custom-call | flops 402653184 | bytes 4194304 | tf_op jit(solution)/shard_map/pallas_call | solution.py:397
  124.5 4.0 %shard_map.106.refs_1_ = bf16[8,128,256]{2,1,0:T(8,128)(2,1)} custom-call(s32[3]{0:T(128)S(1)} %copy-done.11, bf16[8,144,256]{2,1,0:T(8,128)(2,1)} %get-tuple-element.39.refs_0_.refs_1_, bf16[1,272,256]{2,1,0:T(8,128)(2,1)S(1)} %collective-permute-done.13.refs_1_.refs_2_, bf16[2,272,256]{2,1,0:T(8,128)(2,1)S(1)} %collective-permute-done.14.refs_2_.refs_3_, ...), custom_call_target="tpu_custom_call" | custom-call | flops 402653184 | bytes 4194304 | tf_op jit(solution)/shard_map/pallas_call | solution.py:397
  128.4 6.9 %all-to-all-start.1 = ((bf16[8,128,256]{2,1,0:T(8,128)(2,1)}), bf16[8,128,256]{2,1,0:T(8,128)(2,1)S(1)}, u32[]{:S(2)}, u32[]{:S(2)}) async-start(bf16[8,128,256]{2,1,0:T(8,128)(2,1)} %shard_map.106.refs_1_), calls=%async_computation.1 | async-start | bytes 1048576 | tf_op jit(solution)/shard_map/all_to_all | solution.py:493
  136.4 2.8 %collective-permute-start.16 = (bf16[32,256]{1,0:T(8,128)(2,1)S(1)}, bf16[32,256]{1,0:T(8,128)(2,1)S(1)}, u32[]{:S(2)}, u32[]{:S(2)}) collective-permute-start(bf16[32,256]{1,0:T(8,128)(2,1)S(1)} %get-tuple-element.49), channel_id=1, source_target_pairs={{0,192},{64,0},{128,64},{192,128},{1,193},{65,1},{129,65},{193,129... | collective-permute-start | bytes 49160 | tf_op jit(solution)/shard_map/ppermute | solution.py:39
  140.5 2.8 %collective-permute-done.17.refs_3_.refs_2_ = bf16[32,256]{1,0:T(8,128)(2,1)S(1)} collective-permute-done((bf16[32,256]{1,0:T(8,128)(2,1)S(1)}, bf16[32,256]{1,0:T(8,128)(2,1)S(1)}, u32[]{:S(2)}, u32[]{:S(2)}) %collective-permute-start.17) | collective-permute-done | bytes 16416 | tf_op jit(solution)/shard_map/ppermute | solution.py:39
  143.6 9.8 %all-to-all-done.1.refs_0_ = bf16[8,128,256]{2,1,0:T(8,128)(2,1)S(1)} async-done(((bf16[8,128,256]{2,1,0:T(8,128)(2,1)}), bf16[8,128,256]{2,1,0:T(8,128)(2,1)S(1)}, u32[]{:S(2)}, u32[]{:S(2)}) %all-to-all-start.1) | async-done | bytes 524320 | tf_op jit(solution)/shard_map/all_to_all | solution.py:493
  (86 shorter events, 35.1 us)
Async XLA Ops:
  4.7 10.6 %collective-permute-start = (bf16[384,1024]{1,0:T(8,128)(2,1)}, bf16[384,1024]{1,0:T(8,128)(2,1)S(1)}, u32[]{:S(2)}, u32[]{:S(2)}) collective-permute-start(bf16[384,1024]{1,0:T(8,128)(2,1)} %get-tuple-element.28), channel_id=1, source_target_pairs={{0,4},{4,0},{1,5},{5,1},{2,6},{6,2},{3,7},{7,3},{8,12},{12,8},{9,1... | collective-permute-start | bytes 2359304 | tf_op jit(solution)/shard_map/ppermute | solution.py:43
  8.9 24.5 %all-to-all-start = ((bf16[8,32,1024]{2,1,0:T(8,128)(2,1)}), bf16[8,32,1024]{2,1,0:T(8,128)(2,1)S(1)}, u32[]{:S(2)}, u32[]{:S(2)}) async-start(bf16[8,32,1024]{2,1,0:T(8,128)(2,1)} %broadcast_in_dim.6), calls=%async_computation | async-start | bytes 1048576 | tf_op jit(solution)/shard_map/all_to_all | solution.py:449
  16.9 17.4 %collective-permute-start.1 = (bf16[400,256]{1,0:T(8,128)(2,1)S(1)}, bf16[400,256]{1,0:T(8,128)(2,1)S(1)}, u32[]{:S(2)}, u32[]{:S(2)}) collective-permute-start(bf16[400,256]{1,0:T(8,128)(2,1)S(1)} %get-tuple-element.29), channel_id=1, source_target_pairs={{0,8},{8,16},{16,24},{24,32},{32,40},{40,48},{48,56},{56,0},{1,9},... | collective-permute-start | bytes 614408 | tf_op jit(solution)/shard_map/ppermute | solution.py:35
  18.4 22.6 %collective-permute-start.6 = (bf16[400,256]{1,0:T(8,128)(2,1)}, bf16[400,256]{1,0:T(8,128)(2,1)}, u32[]{:S(2)}, u32[]{:S(2)}) collective-permute-start(bf16[400,256]{1,0:T(8,128)(2,1)} %get-tuple-element.35), channel_id=1, source_target_pairs={{0,48},{8,56},{16,0},{24,8},{32,16},{40,24},{48,32},{56,40},{1,49}... | collective-permute-start | bytes 614408 | tf_op jit(solution)/shard_map/ppermute | solution.py:35
  20.8 21.2 %collective-permute-start.7 = (bf16[400,256]{1,0:T(8,128)(2,1)}, bf16[400,256]{1,0:T(8,128)(2,1)}, u32[]{:S(2)}, u32[]{:S(2)}) collective-permute-start(bf16[400,256]{1,0:T(8,128)(2,1)} %get-tuple-element.36), channel_id=1, source_target_pairs={{0,56},{8,0},{16,8},{24,16},{32,24},{40,32},{48,40},{56,48},{1,57}... | collective-permute-start | bytes 614408 | tf_op jit(solution)/shard_map/ppermute | solution.py:35
  22.0 20.0 %collective-permute-start.5 = (bf16[400,256]{1,0:T(8,128)(2,1)}, bf16[400,256]{1,0:T(8,128)(2,1)}, u32[]{:S(2)}, u32[]{:S(2)}) collective-permute-start(bf16[400,256]{1,0:T(8,128)(2,1)} %get-tuple-element.34._), channel_id=1, source_target_pairs={{0,16},{8,24},{16,32},{24,40},{32,48},{40,56},{48,0},{56,8},{1,17}... | collective-permute-start | bytes 614408 | tf_op jit(solution)/shard_map/ppermute | solution.py:35
  37.0 45.4 %all-to-all-start.2 = ((bf16[4,784,256]{2,1,0:T(8,128)(2,1)}), bf16[4,784,256]{2,1,0:T(8,128)(2,1)S(1)}, u32[]{:S(2)}, u32[]{:S(2)}) async-start(bf16[4,784,256]{2,1,0:T(8,128)(2,1)} %copy-done.1), calls=%async_computation.2 | async-start | bytes 3211264 | tf_op jit(solution)/shard_map/all_to_all | solution.py:460
  45.6 30.4 %collective-permute-start.9 = (bf16[5,272,256]{2,1,0:T(8,128)(2,1)S(1)}, bf16[5,272,256]{2,1,0:T(8,128)(2,1)S(1)}, u32[]{:S(2)}, u32[]{:S(2)}) collective-permute-start(bf16[5,272,256]{2,1,0:T(8,128)(2,1)S(1)} %get-tuple-element.37.refs_2_), channel_id=1, source_target_pairs={{0,192},{64,0},{128,64},{192,128},{1,193},{65,1},{129,65},{193,129... | collective-permute-start | bytes 2088968 | tf_op jit(solution)/shard_map/ppermute | solution.py:39
  48.1 27.8 %collective-permute-start.8 = (bf16[5,272,256]{2,1,0:T(8,128)(2,1)S(1)}, bf16[5,272,256]{2,1,0:T(8,128)(2,1)S(1)}, u32[]{:S(2)}, u32[]{:S(2)}) collective-permute-start(bf16[5,272,256]{2,1,0:T(8,128)(2,1)S(1)} %get-tuple-element.37.refs_2_), channel_id=1, source_target_pairs={{0,64},{64,128},{128,192},{192,0},{1,65},{65,129},{129,193},{193,1... | collective-permute-start | bytes 2088968 | tf_op jit(solution)/shard_map/ppermute | solution.py:39
  48.9 13.4 %collective-permute-start.2 = (bf16[400,256]{1,0:T(8,128)(2,1)S(1)}, bf16[400,256]{1,0:T(8,128)(2,1)S(1)}, u32[]{:S(2)}, u32[]{:S(2)}) collective-permute-start(bf16[400,256]{1,0:T(8,128)(2,1)S(1)} %get-tuple-element.30), channel_id=1, source_target_pairs={{0,24},{8,32},{16,40},{24,48},{32,56},{40,0},{48,8},{56,16},{1,25}... | collective-permute-start | bytes 614408 | tf_op jit(solution)/shard_map/ppermute | solution.py:35
  53.2 14.2 %collective-permute-start.3 = (bf16[400,256]{1,0:T(8,128)(2,1)S(1)}, bf16[400,256]{1,0:T(8,128)(2,1)S(1)}, u32[]{:S(2)}, u32[]{:S(2)}) collective-permute-start(bf16[400,256]{1,0:T(8,128)(2,1)S(1)} %get-tuple-element.31), channel_id=1, source_target_pairs={{0,40},{8,48},{16,56},{24,0},{32,8},{40,16},{48,24},{56,32},{1,41}... | collective-permute-start | bytes 614408 | tf_op jit(solution)/shard_map/ppermute | solution.py:35
  53.4 22.5 %collective-permute-start.4 = (bf16[400,256]{1,0:T(8,128)(2,1)S(1)}, bf16[400,256]{1,0:T(8,128)(2,1)S(1)}, u32[]{:S(2)}, u32[]{:S(2)}) collective-permute-start(bf16[400,256]{1,0:T(8,128)(2,1)S(1)} %get-tuple-element.32), channel_id=1, source_target_pairs={{0,32},{8,40},{16,48},{24,56},{32,0},{40,8},{48,16},{56,24},{1,33}... | collective-permute-start | bytes 614408 | tf_op jit(solution)/shard_map/ppermute | solution.py:35
  77.7 16.2 %collective-permute-start.12 = (bf16[8,144,256]{2,1,0:T(8,128)(2,1)}, bf16[8,144,256]{2,1,0:T(8,128)(2,1)}, u32[]{:S(2)}, u32[]{:S(2)}) collective-permute-start(bf16[8,144,256]{2,1,0:T(8,128)(2,1)} %get-tuple-element.39.refs_0_.refs_1_), channel_id=1, source_target_pairs={{0,4},{4,0},{1,5},{5,1},{2,6},{6,2},{3,7},{7,3},{8,12},{12,8},{9,1... | collective-permute-start | bytes 1769480 | tf_op jit(solution)/shard_map/ppermute | solution.py:43
  79.4 26.7 %collective-permute-start.10 = (bf16[6,272,256]{2,1,0:T(8,128)(2,1)S(1)}, bf16[6,272,256]{2,1,0:T(8,128)(2,1)S(1)}, u32[]{:S(2)}, u32[]{:S(2)}) collective-permute-start(bf16[6,272,256]{2,1,0:T(8,128)(2,1)S(1)} %get-tuple-element.40.refs_3_.refs_1_), channel_id=1, source_target_pairs={{0,64},{64,128},{128,192},{192,0},{1,65},{65,129},{129,193},{193,1... | collective-permute-start | bytes 2506760 | tf_op jit(solution)/shard_map/ppermute | solution.py:39
  79.7 26.5 %collective-permute-start.11 = (bf16[5,272,256]{2,1,0:T(8,128)(2,1)}, bf16[5,272,256]{2,1,0:T(8,128)(2,1)}, u32[]{:S(2)}, u32[]{:S(2)}) collective-permute-start(bf16[5,272,256]{2,1,0:T(8,128)(2,1)} %get-tuple-element.41), channel_id=1, source_target_pairs={{0,192},{64,0},{128,64},{192,128},{1,193},{65,1},{129,65},{193,129... | collective-permute-start | bytes 2088968 | tf_op jit(solution)/shard_map/ppermute | solution.py:39
  86.7 41.7 %all-to-all-start.3 = ((bf16[8,128,384]{2,1,0:T(8,128)(2,1)}), bf16[8,128,384]{2,1,0:T(8,128)(2,1)S(1)}, u32[]{:S(2)}, u32[]{:S(2)}) async-start(bf16[8,128,384]{2,1,0:T(8,128)(2,1)} %copy-done.4), calls=%async_computation.3 | async-start | bytes 1572864 | tf_op jit(solution)/shard_map/all_to_all | solution.py:477
  107.3 10.3 %collective-permute-start.14 = (bf16[2,272,256]{2,1,0:T(8,128)(2,1)S(1)}, bf16[2,272,256]{2,1,0:T(8,128)(2,1)S(1)}, u32[]{:S(2)}, u32[]{:S(2)}) collective-permute-start(bf16[2,272,256]{2,1,0:T(8,128)(2,1)S(1)} %get-tuple-element.44), channel_id=1, source_target_pairs={{0,192},{64,0},{128,64},{192,128},{1,193},{65,1},{129,65},{193,129... | collective-permute-start | bytes 835592 | tf_op jit(solution)/shard_map/ppermute | solution.py:39
  108.8 8.8 %collective-permute-start.13 = (bf16[1,272,256]{2,1,0:T(8,128)(2,1)S(1)}, bf16[1,272,256]{2,1,0:T(8,128)(2,1)S(1)}, u32[]{:S(2)}, u32[]{:S(2)}) collective-permute-start(bf16[1,272,256]{2,1,0:T(8,128)(2,1)S(1)} %get-tuple-element.43), channel_id=1, source_target_pairs={{0,64},{64,128},{128,192},{192,0},{1,65},{65,129},{129,193},{193,1... | collective-permute-start | bytes 417800 | tf_op jit(solution)/shard_map/ppermute | solution.py:39
  120.8 3.6 %collective-permute-start.15 = (bf16[8,128,384]{2,1,0:T(8,128)(2,1)S(1)}, bf16[8,128,384]{2,1,0:T(8,128)(2,1)S(1)}, u32[]{:S(2)}, u32[]{:S(2)}) collective-permute-start(bf16[8,128,384]{2,1,0:T(8,128)(2,1)S(1)} %shard_map.105), channel_id=1, source_target_pairs={{0,4},{4,0},{1,5},{5,1},{2,6},{6,2},{3,7},{7,3},{8,12},{12,8},{9,1... | collective-permute-start | bytes 2359304 | tf_op jit(solution)/shard_map/ppermute | solution.py:43
  128.4 24.9 %all-to-all-start.1 = ((bf16[8,128,256]{2,1,0:T(8,128)(2,1)}), bf16[8,128,256]{2,1,0:T(8,128)(2,1)S(1)}, u32[]{:S(2)}, u32[]{:S(2)}) async-start(bf16[8,128,256]{2,1,0:T(8,128)(2,1)} %shard_map.106.refs_1_), calls=%async_computation.1 | async-start | bytes 1048576 | tf_op jit(solution)/shard_map/all_to_all | solution.py:493
  136.4 4.0 %collective-permute-start.16 = (bf16[32,256]{1,0:T(8,128)(2,1)S(1)}, bf16[32,256]{1,0:T(8,128)(2,1)S(1)}, u32[]{:S(2)}, u32[]{:S(2)}) collective-permute-start(bf16[32,256]{1,0:T(8,128)(2,1)S(1)} %get-tuple-element.49), channel_id=1, source_target_pairs={{0,192},{64,0},{128,64},{192,128},{1,193},{65,1},{129,65},{193,129... | collective-permute-start | bytes 49160 | tf_op jit(solution)/shard_map/ppermute | solution.py:39
  139.2 4.1 %collective-permute-start.17 = (bf16[32,256]{1,0:T(8,128)(2,1)S(1)}, bf16[32,256]{1,0:T(8,128)(2,1)S(1)}, u32[]{:S(2)}, u32[]{:S(2)}) collective-permute-start(bf16[32,256]{1,0:T(8,128)(2,1)S(1)} %get-tuple-element.50), channel_id=1, source_target_pairs={{0,64},{64,128},{128,192},{192,0},{1,65},{65,129},{129,193},{193,1... | collective-permute-start | bytes 49160 | tf_op jit(solution)/shard_map/ppermute | solution.py:39
  139.2 4.4 %collective-permute-start.18 = (bf16[32,256]{1,0:T(8,128)(2,1)S(1)}, bf16[32,256]{1,0:T(8,128)(2,1)S(1)}, u32[]{:S(2)}, u32[]{:S(2)}) collective-permute-start(bf16[32,256]{1,0:T(8,128)(2,1)S(1)} %get-tuple-element.51), channel_id=1, source_target_pairs={{0,128},{64,192},{128,0},{192,64},{1,129},{65,193},{129,1},{193,65... | collective-permute-start | bytes 49160 | tf_op jit(solution)/shard_map/ppermute | solution.py:39
  153.9 1.8 %collective-permute-start.19 = (bf16[4,128,256]{2,1,0:T(8,128)(2,1)S(1)}, bf16[4,128,256]{2,1,0:T(8,128)(2,1)S(1)}, u32[]{:S(2)}, u32[]{:S(2)}) collective-permute-start(bf16[4,128,256]{2,1,0:T(8,128)(2,1)S(1)} %shard_map.111), channel_id=1, source_target_pairs={{0,4},{4,0},{1,5},{5,1},{2,6},{6,2},{3,7},{7,3},{8,12},{12,8},{9,1... | collective-permute-start | bytes 786440 | tf_op jit(solution)/shard_map/ppermute | solution.py:43
  (18 other events, 159.8 us)
